TPU v7x, 512 devices: a whole 4x4x16 slice. The times are simulated.
512 devices in a mesh: dp: 16 (over z), mp: 32 (over y, x, core).
Axes of the slice: x: 4, y: 4, z: 16, core: 2. Of those that a mesh axis runs over, the one named last changes fastest.
Arguments:
- normed_input: bfloat16 [16384, 5120], P(('dp', 'mp')), may hold values from -6 to 6
- key_gradient: bfloat16 [16384, 1024], P(('dp', 'mp')), may hold values from -6 to 6
- value_gradient: bfloat16 [16384, 1024], P(('dp', 'mp')), may hold values from -6 to 6
- frozen_key_weight: bfloat16 [5120, 1024], P('mp'), may hold values from -0.078125 to 0.078125
- frozen_value_weight: bfloat16 [5120, 1024], P('mp'), may hold values from -0.078125 to 0.078125
- key_down_weight: bfloat16 [64, 32, 5120], P(None, None, 'mp'), may hold values from -0.078125 to 0.078125
- value_down_weight: bfloat16 [64, 32, 5120], P(None, None, 'mp'), may hold values from -0.078125 to 0.078125
- key_up_weight: bfloat16 [64, 32, 1024], P(None, None, 'mp'), may hold values from -0.1875 to 0.1875
- value_up_weight: bfloat16 [64, 32, 1024], P(None, None, 'mp'), may hold values from -0.1875 to 0.1875
- tenant_of_block: int32 [16, 8], P('dp'), may hold values from 0 to 63, as said below
- live_token_count: int32 [16, 8], P('dp'), may hold values from 1 to 128, as said below
Outputs:
- grad_in: bfloat16 [16384, 5120], P(('dp', 'mp'))
- grad_a_key: float32 [64, 32, 5120], P('dp', None, 'mp')
- grad_a_value: float32 [64, 32, 5120], P('dp', None, 'mp')
- grad_b_key: float32 [64, 32, 1024], P('dp', None, 'mp')
- grad_b_value: float32 [64, 32, 1024], P('dp', None, 'mp')
Inputs may be any that keep to these rules, and one draw needn't show every extreme that they name: `tenant_of_block`: each group's blocks form tenant segments: runs of blocks of one tenant. `live_token_count`: the live tokens of a block are its first ones; the rest is padding.
All inputs are finite; a program needn't handle non-finite values.
Results may differ from a plain program's by a relative error of at most 0.001.
Values may be sent and summed in bfloat16 or wider, within the bound.
No kernel may reach another device: no remote copies, remote signals or barrier semaphores. Data moves between devices by JAX's collectives and lax.ppermute only.
A program may use at most 64 MiB of HBM per device.

v0:
```python
import jax
import jax.numpy as jnp
from jax import lax
from jax.sharding import PartitionSpec as P

TENANT_COUNT = 64
BLOCK = 128


SCALE = 0.5


def shards(
    normed_input,
    key_gradient,
    value_gradient,
    frozen_key_weight,
    frozen_value_weight,
    key_down_weight,
    value_down_weight,
    key_up_weight,
    value_up_weight,
    tenant_of_block,
    live_token_count,
):
    single_float = jnp.float32
    high = lax.Precision.HIGHEST
    tok_rows = normed_input.shape[0]
    group_rows = tok_rows * lax.axis_size("mp")
    blocks = group_rows // BLOCK
    feat_cols = frozen_key_weight.shape[0]
    key_value_columns = key_up_weight.shape[2]
    tenant_index = tenant_of_block[0]
    offsets = jnp.arange(BLOCK, dtype=jnp.int32)
    live_all = (
        (offsets[None, :] < live_token_count[0][:, None]).astype(jnp.bfloat16).reshape(group_rows)
    )
    live_mine = lax.dynamic_slice_in_dim(live_all, lax.axis_index("mp") * tok_rows, tok_rows, 0)
    masked_key = key_gradient * live_mine[:, None]
    masked_value = value_gradient * live_mine[:, None]
    contract = (((1,), (1,)), ((), ()))
    features, cols_key, cols_value = (
        lax.all_to_all(normed_input, "mp", split_axis=1, concat_axis=0, tiled=True),
        lax.all_to_all(masked_key, "mp", split_axis=1, concat_axis=0, tiled=True),
        lax.all_to_all(masked_value, "mp", split_axis=1, concat_axis=0, tiled=True),
    )
    pieces = lax.all_gather((masked_key, masked_value), "mp", axis=0, tiled=True)
    first = lax.dot_general(
        pieces[0], frozen_key_weight, contract, preferred_element_type=single_float
    )
    base = first + lax.dot_general(
        pieces[1], frozen_value_weight, contract, preferred_element_type=single_float
    )
    feat_blocks = features.reshape(blocks, BLOCK, feat_cols)
    key_blocks = cols_key.reshape(blocks, BLOCK, key_value_columns)
    value_blocks = cols_value.reshape(blocks, BLOCK, key_value_columns)
    chosen_key_down = key_down_weight[tenant_index]
    chosen_value_down = value_down_weight[tenant_index]
    chosen_key_up = key_up_weight[tenant_index]
    chosen_value_up = value_up_weight[tenant_index]
    down_key = jnp.einsum(
        "brd,bsd->brs", chosen_key_down, feat_blocks, preferred_element_type=single_float
    )
    down_value = jnp.einsum(
        "brd,bsd->brs", chosen_value_down, feat_blocks, preferred_element_type=single_float
    )
    back_key = jnp.einsum(
        "brc,bsc->brs", chosen_key_up, key_blocks, preferred_element_type=single_float
    )
    back_value = jnp.einsum(
        "brc,bsc->brs", chosen_value_up, value_blocks, preferred_element_type=single_float
    )
    down_key, down_value = lax.psum((down_key, down_value), "mp")
    back_key, back_value = lax.psum((back_key, back_value), "mp")
    wide_a_key = chosen_key_down.astype(single_float)
    wide_a_value = chosen_value_down.astype(single_float)
    lowrank = jnp.einsum("brs,brd->bsd", back_key, wide_a_key, precision=high) + jnp.einsum(
        "brs,brd->bsd", back_value, wide_a_value, precision=high
    )
    grad_feat = (base + SCALE * lowrank.reshape(group_rows, feat_cols)).astype(jnp.bfloat16)
    grad_in = lax.all_to_all(grad_feat, "mp", split_axis=0, concat_axis=1, tiled=True)
    feat_wide = feat_blocks.astype(single_float)
    key_wide = key_blocks.astype(single_float)
    value_wide = value_blocks.astype(single_float)
    onehot = (tenant_index[:, None] == jnp.arange(TENANT_COUNT, dtype=jnp.int32)[None, :]).astype(
        single_float
    )
    part_a_key = SCALE * jnp.einsum("brs,bsd->brd", back_key, feat_wide, precision=high)
    part_a_value = SCALE * jnp.einsum("brs,bsd->brd", back_value, feat_wide, precision=high)
    part_b_key = SCALE * jnp.einsum("brs,bsc->brc", down_key, key_wide, precision=high)
    part_b_value = SCALE * jnp.einsum("brs,bsc->brc", down_value, value_wide, precision=high)
    local_a_key = jnp.einsum("bt,brd->trd", onehot, part_a_key, precision=high)
    local_a_value = jnp.einsum("bt,brd->trd", onehot, part_a_value, precision=high)
    local_b_key = jnp.einsum("bt,brc->trc", onehot, part_b_key, precision=high)
    local_b_value = jnp.einsum("bt,brc->trc", onehot, part_b_value, precision=high)
    grad_a_key, grad_a_value, grad_b_key, grad_b_value = (
        lax.psum_scatter(local_a_key, "dp", scatter_dimension=0, tiled=True),
        lax.psum_scatter(local_a_value, "dp", scatter_dimension=0, tiled=True),
        lax.psum_scatter(local_b_key, "dp", scatter_dimension=0, tiled=True),
        lax.psum_scatter(local_b_value, "dp", scatter_dimension=0, tiled=True),
    )
    return (grad_in, grad_a_key, grad_a_value, grad_b_key, grad_b_value)


def solution(mesh):
    in_specs = (
        P(("dp", "mp"), None),
        P(("dp", "mp"), None),
        P(("dp", "mp"), None),
        P("mp", None),
        P("mp", None),
        P(None, None, "mp"),
        P(None, None, "mp"),
        P(None, None, "mp"),
        P(None, None, "mp"),
        P("dp", None),
        P("dp", None),
    )
    out_specs = (
        P(("dp", "mp"), None),
        P("dp", None, "mp"),
        P("dp", None, "mp"),
        P("dp", None, "mp"),
        P("dp", None, "mp"),
    )
    return jax.shard_map(shards, mesh=mesh, in_specs=in_specs, out_specs=out_specs, check_vma=False)
```

profile of v0, /device:TPU:8, one launch (start us, length us, event | category | flops | bytes accessed | tf_op | source)
XLA Modules:
  0.0 619.4 jit_solution(444414913949025404)
XLA Ops:
  7.2 0.8 fusion.24
  8.1 0.1 dynamic_slice.3
  8.1 1.0 broadcast_multiply_fusion
  9.1 0.2 copy.66
  9.3 0.9 reshape.113
  10.1 9.5 %all-to-all-start.1 = ((bf16[32,2,512]{2,1,0:T(2,128)(2,1)}), bf16[32,2,512]{2,1,0:T(2,128)(2,1)S(1)}, u32[]{:S(2)}, u32[]{:S(2)}) async-start(bf16[32,2,512]{2,1,0:T(2,128)(2,1)} %reshape.113), calls=%async_computation.1 | async-start | bytes 131072 | tf_op jit(solution)/shard_map/all_to_all | solution.py:45
  19.7 0.7 fusion.29
  20.3 0.6 gather_fusion.3
  20.9 1.8 gather_fusion.1
  22.7 0.2 copy.62
  22.9 0.9 reshape.111
  23.7 0.6 all_to_all.60
  24.4 1.1 copy.72
  25.5 0.8 copy.61
  26.3 0.6 gather_fusion
  26.9 0.8 copy.65
  27.7 0.6 gather_fusion.2
  28.2 7.5 %all-to-all-start = ((bf16[32,2,512]{2,1,0:T(2,128)(2,1)}), bf16[32,2,512]{2,1,0:T(2,128)(2,1)S(1)}, u32[]{:S(2)}, u32[]{:S(2)}) async-start(bf16[32,2,512]{2,1,0:T(2,128)(2,1)} %reshape.111), calls=%async_computation | async-start | bytes 131072 | tf_op jit(solution)/shard_map/all_to_all | solution.py:44
  35.7 0.2 reshape.114
  35.9 6.1 all-to-all-done
  42.0 5.0 all-to-all-start.3
  47.1 0.2 reshape.112
  47.3 0.1 copy.63
  47.4 0.2 reshape.74
  47.6 0.8 fusion.16
  48.4 0.1 copy.67
  48.5 0.2 reshape.75
  48.7 0.8 fusion.13
  49.5 7.3 %all-to-all-done.3 = bf16[32,32,160]{2,0,1:T(8,128)(2,1)S(1)} async-done(((bf16[32,32,160]{2,0,1:T(8,128)(2,1)}), bf16[32,32,160]{2,0,1:T(8,128)(2,1)S(1)}, u32[]{:S(2)}, u32[]{:S(2)}) %all-to-all-start.3) | async-done | bytes 327712 | tf_op jit(solution)/shard_map/all_to_all | solution.py:43
  56.8 0.9 fusion.33
  57.7 0.9 fusion.32
  58.7 0.7 all-gather.3.cloned.1.call-update
  59.4 0.7 all-gather.5.cloned.1.call-update
  60.2 133.0 %all-reduce.3.cloned.1.call-done = (f32[8,32,128]{2,1,0:T(8,128)}, f32[8,32,128]{2,1,0:T(8,128)}, f32[8,32,128]{2,1,0:T(8,128)}, f32[8,32,128]{2,1,0:T(8,128)}) async-done(((f32[8,32,128]{2,1,0:T(8,128)}, f32[8,32,128]{2,1,0:T(8,128)}, f32[8,32,128]{2,1,0:T(8,128)}, f32[8,32,128]{2,1,0:T(8,128)}), (f32[8,32,128]{2,1,0:T(8,128)}, f32[8,32,128]{2,1,0:T(8,128)}, f32[8,32,128]{2,1,0:T(8,128)}, ...) | async-done | bytes 524304 | tf_op jit(solution)/shard_map/psum | solution.py:74
  193.2 1.1 convolution_multiply_fusion.2
  194.4 0.7 fusion.8
  195.1 1.7 copy.86
  196.8 0.0 reduce-scatter.9.cloned.1.call-start
  196.8 0.2 convolution_multiply_fusion.3
  197.1 0.7 fusion.10
  197.8 1.6 copy.82
  199.4 0.0 reduce-scatter.7.cloned.1.call-start
  199.5 0.3 convolution_multiply_fusion
  199.8 1.1 fusion.4
  200.9 2.6 copy.78
  203.5 0.2 reduce-scatter.5.cloned.1.call-start
  203.8 0.6 copy-done.4
  204.4 0.3 convolution_multiply_fusion.1
  204.7 1.1 fusion.6
  205.8 2.6 copy.75
  208.5 0.5 fusion.31
  209.0 0.5 fusion.1
  209.5 46.5 %all-gather.3.cloned.1.call-done = bf16[1024,1024]{1,0:T(8,128)(2,1)} async-done(((bf16[32,1024]{1,0:T(8,128)(2,1)}), bf16[1024,1024]{1,0:T(8,128)(2,1)}) %all-gather.3.cloned.1.call-update) | async-done | bytes 2097168 | tf_op jit(solution)/shard_map/all_gather | solution.py:47
  256.0 2.4 fusion.30
  258.4 59.7 %all-gather.5.cloned.1.call-done = bf16[1024,1024]{1,0:T(8,128)(2,1)} async-done(((bf16[32,1024]{1,0:T(8,128)(2,1)}), bf16[1024,1024]{1,0:T(8,128)(2,1)}) %all-gather.5.cloned.1.call-update) | async-done | bytes 2097168 | tf_op jit(solution)/shard_map/all_gather | solution.py:47
  318.1 2.4 fusion.3
  320.6 0.2 copy.70
  320.8 15.4 %all_to_all.67 = bf16[32,32,160]{2,1,0:T(8,128)(2,1)S(1)} all-to-all(bf16[32,32,160]{2,1,0:T(8,128)(2,1)S(1)} %bitcast.63), channel_id=1, replica_groups=mesh['dp'=16,'mp'=32] {'mp'}, dimensions={0} | all-to-all | bytes 655360 | tf_op jit(solution)/shard_map/all_to_all | solution.py:81
  336.1 0.3 copy.71
  336.4 1.5 all_to_all.59
  337.9 53.9 %reduce-scatter.11.cloned.1.call-done = f32[4,32,32]{2,1,0:T(8,128)} async-done(((f32[64,32,32]{2,1,0:T(8,128)}), f32[4,32,32]{2,1,0:T(8,128)}) %reduce-scatter.11.cloned.1.call-update) | async-done | bytes 16400 | tf_op jit(solution)/shard_map/reduce_scatter | solution.py:100
  391.8 71.3 %reduce-scatter.9.cloned.1.call-done = f32[4,32,32]{2,1,0:T(8,128)} async-done(((f32[64,32,32]{2,1,0:T(8,128)}), f32[4,32,32]{2,1,0:T(8,128)}) %reduce-scatter.9.cloned.1.call-update) | async-done | bytes 16400 | tf_op jit(solution)/shard_map/reduce_scatter | solution.py:99
  463.2 74.6 %reduce-scatter.7.cloned.1.call-done = f32[4,32,160]{2,1,0:T(8,128)} async-done(((f32[64,32,160]{2,1,0:T(8,128)}), f32[4,32,160]{2,1,0:T(8,128)}) %reduce-scatter.7.cloned.1.call-update) | async-done | bytes 81936 | tf_op jit(solution)/shard_map/reduce_scatter | solution.py:98
  537.7 74.8 %reduce-scatter.5.cloned.1.call-done = f32[4,32,160]{2,1,0:T(8,128)} async-done(((f32[64,32,160]{2,1,0:T(8,128)}), f32[4,32,160]{2,1,0:T(8,128)}) %reduce-scatter.5.cloned.1.call-update) | async-done | bytes 81936 | tf_op jit(solution)/shard_map/reduce_scatter | solution.py:97
  (36 shorter events, 0.3 us)
Async XLA Ops:
  7.2 13.2 %copy-start = (bf16[64,32,160]{2,1,0:T(8,128)(2,1)S(1)}, bf16[64,32,160]{2,1,0:T(8,128)(2,1)}, u32[]{:S(2)}) copy-start(bf16[64,32,160]{2,1,0:T(8,128)(2,1)} %param.17) | copy-start | bytes 1966084
  7.2 16.5 %copy-start.6 = (bf16[32,5120]{1,0:T(8,128)(2,1)S(1)}, bf16[32,5120]{1,0:T(8,128)(2,1)}, u32[]{:S(2)}) copy-start(bf16[32,5120]{1,0:T(8,128)(2,1)} %param.11) | copy-start | bytes 983044
  7.2 18.3 %copy-start.8 = (bf16[64,32,32]{0,2,1:T(8,128)(2,1)S(1)}, bf16[64,32,32]{0,2,1:T(8,128)(2,1)}, u32[]{:S(2)}) copy-start(bf16[64,32,32]{0,2,1:T(8,128)(2,1)} %param.18) | copy-start | bytes 393220
  9.1 17.2 %copy-start.1 = (bf16[32,1024]{1,0:T(8,128)(2,1)}, bf16[32,1024]{1,0:T(8,128)(2,1)S(1)}, u32[]{:S(2)}) copy-start(bf16[32,1024]{1,0:T(8,128)(2,1)S(1)} %get-tuple-element.24) | copy-start | bytes 196612
  9.1 17.2 %copy-start.2 = (bf16[32,1024]{1,0:T(8,128)(2,1)}, bf16[32,1024]{1,0:T(8,128)(2,1)S(1)}, u32[]{:S(2)}) copy-start(bf16[32,1024]{1,0:T(8,128)(2,1)S(1)} %get-tuple-element.25) | copy-start | bytes 196612
  10.1 16.7 %copy-start.9 = (bf16[64,32,32]{0,2,1:T(8,128)(2,1)S(1)}, bf16[64,32,32]{0,2,1:T(8,128)(2,1)}, u32[]{:S(2)}) copy-start(bf16[64,32,32]{0,2,1:T(8,128)(2,1)} %param.19) | copy-start | bytes 393220
  10.1 18.1 %all-to-all-start.1 = ((bf16[32,2,512]{2,1,0:T(2,128)(2,1)}), bf16[32,2,512]{2,1,0:T(2,128)(2,1)S(1)}, u32[]{:S(2)}, u32[]{:S(2)}) async-start(bf16[32,2,512]{2,1,0:T(2,128)(2,1)} %reshape.113), calls=%async_computation.1 | async-start | bytes 131072 | tf_op jit(solution)/shard_map/all_to_all | solution.py:45
  28.2 13.8 %all-to-all-start = ((bf16[32,2,512]{2,1,0:T(2,128)(2,1)}), bf16[32,2,512]{2,1,0:T(2,128)(2,1)S(1)}, u32[]{:S(2)}, u32[]{:S(2)}) async-start(bf16[32,2,512]{2,1,0:T(2,128)(2,1)} %reshape.111), calls=%async_computation | async-start | bytes 131072 | tf_op jit(solution)/shard_map/all_to_all | solution.py:44
  42.0 14.8 %all-to-all-start.3 = ((bf16[32,32,160]{2,0,1:T(8,128)(2,1)}), bf16[32,32,160]{2,0,1:T(8,128)(2,1)S(1)}, u32[]{:S(2)}, u32[]{:S(2)}) async-start(bf16[32,32,160]{2,0,1:T(8,128)(2,1)} %copy.72), calls=%async_computation.3 | async-start | bytes 1048576 | tf_op jit(solution)/shard_map/all_to_all | solution.py:43
  47.0 146.2 %all-reduce.3.cloned.1.call-start = ((), (), s32[]{:S(2)}) async-start(), calls=%async_computation.14 | async-start | bytes 1048576 | tf_op jit(solution)/shard_map/psum | solution.py:74
  47.4 147.0 %copy-start.11 = (s32[1,8]{1,0:T(1,128)S(1)}, s32[1,8]{1,0:T(1,128)}, u32[]{:S(2)}) copy-start(s32[1,8]{1,0:T(1,128)} %param.20) | copy-start | bytes 100
  58.6 197.3 %all-gather.3.cloned.1.call-start = ((), (), s32[]{:S(2)}) async-start(), calls=%async_computation.8 | async-start | bytes 2162688 | tf_op jit(solution)/shard_map/all_gather | solution.py:47
  59.4 258.7 %all-gather.5.cloned.1.call-start = ((), (), s32[]{:S(2)}) async-start(), calls=%async_computation.9 | async-start | bytes 2162688 | tf_op jit(solution)/shard_map/all_gather | solution.py:47
  60.1 331.7 %reduce-scatter.11.cloned.1.call-start = ((), (), s32[]{:S(2)}) async-start(), calls=%async_computation.13 | async-start | bytes 1114112 | tf_op jit(solution)/shard_map/reduce_scatter | solution.py:100
  194.4 2.5 copy-start.10
  196.8 266.4 %reduce-scatter.9.cloned.1.call-start = ((), (), s32[]{:S(2)}) async-start(), calls=%async_computation.12 | async-start | bytes 1114112 | tf_op jit(solution)/shard_map/reduce_scatter | solution.py:99
  197.1 2.4 copy-start.3
  199.4 338.3 %reduce-scatter.7.cloned.1.call-start = ((), (), s32[]{:S(2)}) async-start(), calls=%async_computation.11 | async-start | bytes 2228224 | tf_op jit(solution)/shard_map/reduce_scatter | solution.py:98
  203.5 0.9 copy-start.4
  203.5 409.0 %reduce-scatter.5.cloned.1.call-start = ((), (), s32[]{:S(2)}) async-start(), calls=%async_computation.10 | async-start | bytes 2228224 | tf_op jit(solution)/shard_map/reduce_scatter | solution.py:97
  208.4 47.5 %copy-start.5 = (bf16[160,1024]{1,0:T(8,128)(2,1)S(1)}, bf16[160,1024]{1,0:T(8,128)(2,1)}, u32[]{:S(2)}) copy-start(bf16[160,1024]{1,0:T(8,128)(2,1)} %param.14) | copy-start | bytes 983044
  209.0 109.2 %copy-start.7 = (bf16[160,1024]{1,0:T(8,128)(2,1)S(1)}, bf16[160,1024]{1,0:T(8,128)(2,1)}, u32[]{:S(2)}) copy-start(bf16[160,1024]{1,0:T(8,128)(2,1)} %param.15) | copy-start | bytes 983044
Sparse Core Ops, SparseCore 0:
  58.8 134.4 all-reduce.2
  196.8 59.1 all-gather.2
  259.6 58.4 all-gather.4
  321.6 70.1 reduce-scatter.10
  395.1 68.0 reduce-scatter.8
  466.6 71.0 reduce-scatter.6
  541.3 71.1 reduce-scatter.4
where the time goes:
time: 620 us; the launch traced here: 619 us
  waiting for transfers between devices  529 us (85%)
  starting transfers between devices  22.4 us (4%)
  local copies, waits for them, and re-layouts  21 us (3%)
  blocking collectives  15.4 us (2%)
  matrix products  14.9 us (2%)
  between operations  14.5 us (2%)
    psum x1, waiting for transfers between devices, shards(): back_key, back_value = lax.psum((back_key, back_value), 'mp')  133 us
    all_gather x2, waiting for transfers between devices, shards(): lax.all_gather((masked_key, masked_value), 'mp', axis=0, tiled=True)  106 us
    reduce_scatter x1, waiting for transfers between devices, shards(): lax.psum_scatter(local_a_key, 'dp', scatter_dimension=0, tiled=True)  74.8 us
    reduce_scatter x1, waiting for transfers between devices, shards(): lax.psum_scatter(local_a_value, 'dp', scatter_dimension=0, tiled=True)  74.6 us
    reduce_scatter x1, waiting for transfers between devices, shards(): lax.psum_scatter(local_b_key, 'dp', scatter_dimension=0, tiled=True)  71.3 us
    reduce_scatter x1, waiting for transfers between devices, shards(): lax.psum_scatter(local_b_value, 'dp', scatter_dimension=0, tiled=True)  53.9 us
    all_to_all x1, blocking collectives, shards(): lax.all_to_all(grad_feat, 'mp', split_axis=0, concat_axis=1, tiled=True)  15.4 us
  transfers between devices with their start and end apart: 10, of which 9 were waited for; matrix products, arithmetic and copies ran while one was open for 5% of the time, Pallas kernels for 0%

commit v1 on v0

v1 whole, which is shorter than its diff:
```python
import functools

import jax
import jax.numpy as jnp
from jax import lax
from jax.experimental import pallas as pl
from jax.experimental.pallas import tpu as pltpu
from jax.sharding import Mesh, PartitionSpec as P

BLOCK = 128
SCALE = 0.5
F32 = jnp.float32
BF16 = jnp.bfloat16
VMEM = pl.BlockSpec(memory_space=pltpu.VMEM)
SMEM = pl.BlockSpec(memory_space=pltpu.SMEM)
ANY = pl.BlockSpec(memory_space=pl.ANY)
PARAMS = pltpu.CompilerParams(vmem_limit_bytes=24 * 1024 * 1024)
LANE = 128


def pack_kernel(
    tenants, counts, where, x_ref, k_ref, v_ref, up_ref, ak_hbm, av_hbm,
    send_ref, masked_ref, ak, av, sems,
):
    n_mp = send_ref.shape[0]
    blocks = ak.shape[0]
    rank = ak.shape[1]
    tok = x_ref.shape[0]
    feat = ak.shape[2]
    cols = k_ref.shape[1] // n_mp
    rest = feat - LANE
    quad = n_mp // blocks
    copies = []
    for b in range(blocks):
        t = tenants[0, b]
        copies.append(pltpu.make_async_copy(ak_hbm.at[t], ak.at[b], sems.at[0, b]))
        copies.append(pltpu.make_async_copy(av_hbm.at[t], av.at[b], sems.at[1, b]))
    for c in copies:
        c.start()
    me = where[0]
    count = counts[0, me // quad]
    row = lax.broadcasted_iota(jnp.int32, (tok, 1), 0) + (me % quad) * tok
    live = row < count
    mk = jnp.where(live, k_ref[...].astype(F32), 0.0).astype(BF16)
    mv = jnp.where(live, v_ref[...].astype(F32), 0.0).astype(BF16)
    masked_ref[:, : mk.shape[1]] = mk
    masked_ref[:, mk.shape[1] :] = mv
    x = x_ref[...]
    for j in range(n_mp):
        send_ref[j, 96:128, :] = x[:, feat * j : feat * j + LANE]
        last = x[:, feat * j + LANE : feat * (j + 1)]
        send_ref[j, 128:160, :] = jnp.concatenate(
            [last, mk[:, cols * j : cols * (j + 1)], last, mv[:, cols * j : cols * (j + 1)]], axis=1
        )
    for c in copies:
        c.wait()
    for b in range(blocks):
        a0 = ak[b]
        a1 = av[b]
        main = jnp.concatenate([a0[:, :LANE], a1[:, :LANE]], axis=0)
        up = up_ref[b]
        tail = jnp.concatenate(
            [a0[:, LANE:], up[:, :cols], a1[:, LANE:], up[:, cols : 2 * cols]], axis=1
        )
        for q in range(quad):
            send_ref[quad * b + q, 0:64, :] = main
            send_ref[quad * b + q, 64:96, :] = tail


def lane_mask(rows, slot):
    lane = lax.broadcasted_iota(jnp.int32, (rows, LANE), 1)
    return (lane >= 32 * slot) & (lane < 32 * slot + 32)


def vector_kernel(send_ref, recv_ref, out_ref):
    n_mp = send_ref.shape[0]
    masks = [lane_mask(32, s) for s in (0, 2, 1, 3)]
    total = jnp.zeros((32, LANE), F32)
    zero = jnp.zeros((64, LANE), BF16)
    for m in range(n_mp):
        lhs = jnp.concatenate([send_ref[m, 96:128, :], send_ref[m, 128:160, :]], axis=1)
        main = jnp.concatenate([recv_ref[m, 0:64, :], zero], axis=0)
        tail = recv_ref[m, 64:96, :]
        tails = jnp.concatenate([jnp.where(k, tail, jnp.zeros_like(tail)) for k in masks], axis=0)
        rhs = jnp.concatenate([main, tails], axis=1)
        total += lax.dot_general(lhs, rhs, (((1,), (1,)), ((), ())), preferred_element_type=F32)
    for m in range(n_mp):
        out_ref[m] = total


def split(x):
    hi = x.astype(BF16)
    return hi, (x - hi.astype(F32)).astype(BF16)


def parts_kernel(tenants, vec_ref, recv_ref, out_ref):
    blocks = vec_ref.shape[0] // 4
    out_ref[...] = jnp.zeros_like(out_ref)
    m0, m1, m2, m3 = [lane_mask(32, s) for s in range(4)]
    for b in range(blocks):
        vec = vec_ref[4 * b : 4 * b + 4].reshape(BLOCK, LANE) * SCALE
        lhs = jnp.concatenate(split(vec), axis=0)
        first = recv_ref[4 * b : 4 * b + 4, 96:128, :].reshape(BLOCK, LANE)
        second = recv_ref[4 * b : 4 * b + 4, 128:160, :].reshape(BLOCK, LANE)
        rhs = jnp.concatenate([first, second], axis=1)
        rhs = jnp.concatenate([rhs, rhs], axis=0)
        p = lax.dot_general(lhs, rhs, (((0,), (0,)), ((), ())), preferred_element_type=F32)
        t = tenants[0, b]
        out_ref[t, 0:64, :] += p[64:128, :LANE]
        q = p[:, LANE:]
        tail = jnp.where(m0, q[64:96], jnp.where(m1, q[0:32], jnp.where(m2, q[96:128], q[32:64])))
        out_ref[t, 64:96, :] += tail


def base_kernel(kv_ref, w_ref, vec_ref, a_ref, out_ref):
    blocks = a_ref.shape[0]
    per = kv_ref.shape[0] // blocks
    w = w_ref[...].reshape(-1, w_ref.shape[-1])
    for b in range(blocks):
        rows = kv_ref[per * b : per * (b + 1)].reshape(-1, kv_ref.shape[-1])
        vec = vec_ref[per * b : per * (b + 1)].reshape(-1, LANE)[:, 64:] * SCALE
        low = jnp.concatenate(split(vec), axis=1)
        a = a_ref[b].reshape(-1, LANE)
        dims = (((1,), (1,)), ((), ()))
        res = lax.dot_general(rows, w, dims, preferred_element_type=F32)
        res += lax.dot_general(low, a, dims, preferred_element_type=F32)
        out_ref[per * b : per * (b + 1)] = res.astype(BF16).reshape(per, -1, w.shape[0])


def finish_kernel(sum_ref, ak_ref, av_ref, bk_ref, bv_ref):
    for t in range(sum_ref.shape[0]):
        tail = sum_ref[t, 64:96, :]
        ak_ref[t, :, :LANE] = sum_ref[t, 0:32, :]
        ak_ref[t, :, LANE:] = tail[:, 0:32]
        av_ref[t, :, :LANE] = sum_ref[t, 32:64, :]
        av_ref[t, :, LANE:] = tail[:, 64:96]
        bk_ref[t] = tail[:, 32:64]
        bv_ref[t] = tail[:, 96:128]


def shards(x, kg, vg, wk, wv, ak, av, bk, bv, tenant_of_block, live_token_count):
    mp = ("y", "x", "core")
    n_mp = lax.axis_size(mp)
    tok, width = x.shape
    blocks = tenant_of_block.shape[1]
    feat = wk.shape[0]
    kv_width = kg.shape[1]
    tenants, rank = ak.shape[:2]
    me = lax.axis_index(mp).astype(jnp.int32).reshape(1)
    core = lax.axis_index("core")
    tenant_index = tenant_of_block[0]

    up = jnp.concatenate([bk[tenant_index], bv[tenant_index]], axis=-1)
    send, masked = pl.pallas_call(
        pack_kernel,
        out_shape=(
            jax.ShapeDtypeStruct((n_mp, 160, LANE), BF16),
            jax.ShapeDtypeStruct((tok, 2 * kv_width), BF16),
        ),
        in_specs=[SMEM, SMEM, SMEM, VMEM, VMEM, VMEM, VMEM, ANY, ANY],
        out_specs=(VMEM, VMEM),
        scratch_shapes=[
            pltpu.VMEM((blocks, rank, feat), BF16),
            pltpu.VMEM((blocks, rank, feat), BF16),
            pltpu.SemaphoreType.DMA((2, blocks)),
        ],
        compiler_params=PARAMS,
        name="pack",
    )(tenant_of_block, live_token_count, me, x, kg, vg, up, ak, av)
    recv = lax.all_to_all(send, mp, split_axis=0, concat_axis=0, tiled=True)
    vec_send = pl.pallas_call(
        vector_kernel,
        out_shape=jax.ShapeDtypeStruct((n_mp, tok, LANE), F32),
        in_specs=[VMEM, VMEM],
        out_specs=VMEM,
        compiler_params=PARAMS,
        name="vectors",
    )(send, recv)
    vec = lax.all_to_all(vec_send, mp, split_axis=0, concat_axis=0, tiled=True)
    parts = pl.pallas_call(
        parts_kernel,
        out_shape=jax.ShapeDtypeStruct((tenants, 96, LANE), F32),
        in_specs=[SMEM, VMEM, VMEM],
        out_specs=VMEM,
        compiler_params=PARAMS,
        name="parts",
    )(tenant_of_block, vec, recv)
    parts, masked, wk, wv = lax.optimization_barrier((parts, masked, wk, wv))
    sums = lax.psum_scatter(parts, "dp", scatter_dimension=0, tiled=True)

    def spread(a, axes):
        n = lax.axis_size(axes)
        return lax.all_to_all(
            jnp.broadcast_to(a[None], (n, *a.shape)), axes, split_axis=0, concat_axis=0, tiled=True
        )

    chosen = jnp.concatenate([ak[tenant_index], av[tenant_index]], axis=1)
    chosen = jnp.concatenate([chosen, chosen], axis=1).transpose(0, 2, 1)
    kv = spread(masked, ("y", "x"))
    w = spread(jnp.concatenate([wk, wv], axis=1), ("core",))
    a = spread(chosen, ("core",)).transpose(1, 0, 2, 3)
    mine = lax.dynamic_index_in_dim(vec.reshape(n_mp // 2, 2, tok, LANE), core, 1, keepdims=False)
    grad = pl.pallas_call(
        base_kernel,
        out_shape=jax.ShapeDtypeStruct((n_mp // 2, tok, 2 * feat), BF16),
        in_specs=[VMEM, VMEM, VMEM, VMEM],
        out_specs=VMEM,
        compiler_params=PARAMS,
        name="base",
    )(kv, w, mine, a)
    grad = lax.all_to_all(grad, ("y", "x"), split_axis=0, concat_axis=0, tiled=True)
    grad_in = grad.transpose(1, 0, 2).reshape(tok, width)

    owned = tenants // lax.axis_size("dp")
    grads = pl.pallas_call(
        finish_kernel,
        out_shape=(
            jax.ShapeDtypeStruct((owned, rank, feat), F32),
            jax.ShapeDtypeStruct((owned, rank, feat), F32),
            jax.ShapeDtypeStruct((owned, rank, bk.shape[2]), F32),
            jax.ShapeDtypeStruct((owned, rank, bk.shape[2]), F32),
        ),
        in_specs=[VMEM],
        out_specs=(VMEM, VMEM, VMEM, VMEM),
        compiler_params=PARAMS,
        name="finish",
    )(sums)
    return (grad_in, *grads)


def solution(mesh):
    n_dp, n_mp = mesh.devices.shape
    fine = Mesh(mesh.devices.reshape(n_dp, 4, n_mp // 8, 2), ("dp", "y", "x", "core"))
    mp = ("y", "x", "core")
    rows = P(("dp", *mp), None)
    in_specs = (
        rows, rows, rows,
        P(mp, None), P(mp, None),
        P(None, None, mp), P(None, None, mp), P(None, None, mp), P(None, None, mp),
        P("dp", None), P("dp", None),
    )
    grads = P("dp", None, mp)
    return jax.shard_map(
        shards, mesh=fine, in_specs=in_specs, out_specs=(rows, grads, grads, grads, grads),
        check_vma=False,
    )
```

time: 620 us -> 150 us (0.24)
  the two profiles are of different devices: /device:TPU:8 before, /device:TPU:10 now
where the time goes in v1:
time: 150 us; the launch traced here: 149 us
  blocking collectives  60.8 us (41%)
  waiting for transfers between devices  35.2 us (23%)
  local copies, waits for them, and re-layouts  18.8 us (13%)
  between operations  14.3 us (10%)
  starting transfers between devices  9.57 us (6%)
  Pallas kernels  9.3 us (6%)
    all_to_all x2, waiting for transfers between devices, spread(): lax.all_to_all(jnp.broadcast_to(a[None], (n, *a.shape)), axes, split_axis...  28.6 us
    all_to_all x1, blocking collectives, shards(): recv = lax.all_to_all(send, mp, split_axis=0, concat_axis=0, tiled=True)  26.2 us
    all_to_all x1, blocking collectives, shards(): lax.all_to_all(grad, ('y', 'x'), split_axis=0, concat_axis=0, tiled=True)  15 us
    all_to_all x1, blocking collectives, shards(): vec = lax.all_to_all(vec_send, mp, split_axis=0, concat_axis=0, tiled=True)  14.8 us
    all_to_all x2, starting transfers between devices, spread(): lax.all_to_all(jnp.broadcast_to(a[None], (n, *a.shape)), axes, split_axis...  9.53 us
    unnamed x32, local copies, waits for them, and re-layouts  8.47 us
    reduce_scatter x1, waiting for transfers between devices, shards(): sums = lax.psum_scatter(parts, 'dp', scatter_dimension=0, tiled=True)  6.52 us
    all_to_all x1, blocking collectives, spread(): lax.all_to_all(jnp.broadcast_to(a[None], (n, *a.shape)), axes, split_axis...  4.79 us
  transfers between devices with their start and end apart: 3, of which 3 were waited for; matrix products, arithmetic and copies ran while one was open for 6% of the time, Pallas kernels for 2%

profile of v1, /device:TPU:10, one launch (start us, length us, event | category | flops | bytes accessed | tf_op | source)
XLA Modules:
  0.0 148.9 jit_solution(12942234311631122945)
XLA Ops:
  7.2 0.0 copy-start.10
  7.2 0.0 copy-start.3
  7.2 0.0 copy-start.11
  7.2 0.0 copy-start.9
  7.2 0.0 copy-start.8
  7.2 0.0 copy-start.6
  7.2 0.0 reduce-scatter.2.cloned.1.call-start
  7.3 0.8 fusion
  8.0 1.7 %copy.23 = bf16[64,32,32]{2,1,0:T(8,128)(2,1)S(1)} copy(bf16[64,32,32]{0,2,1:T(8,128)(2,1)} %param.18) | data formatting | bytes 262144 | tf_op args[7]
  9.8 1.7 %copy.24 = bf16[64,32,32]{2,1,0:T(8,128)(2,1)S(1)} copy(bf16[64,32,32]{0,2,1:T(8,128)(2,1)} %param.19) | data formatting | bytes 262144 | tf_op args[8]
  11.5 0.6 gather_fusion
  12.1 0.6 gather_fusion.1
  12.6 0.1 pad_maximum_fusion.1.up_ref
  12.7 0.0 copy-done.10
  12.7 0.0 copy-done.3
  12.8 0.0 copy-done.11
  12.8 0.0 copy-done.9
  12.8 0.0 copy-done.8
  12.8 0.0 copy-done.6
  12.8 0.0 copy-start.4
  12.8 1.2 copy-done.4
  14.0 1.7 %pack.1 = (bf16[32,160,128]{2,1,0:T(8,128)(2,1)S(1)}, bf16[32,2048]{1,0:T(8,128)(2,1)S(1)}) custom-call(s32[1,8]{1,0:T(1,128)S(1)} %copy-done.10, s32[1,8]{1,0:T(1,128)S(1)} %copy-done.11, s32[1]{0:T(128)} %bitcast.where, bf16[32,5120]{1,0:T(8,128)(2,1)S(1)} %copy-done.6, bf16[32,1024]{1,0:T(8,128)(2,1)S(1)} %copy-done.8, bf16[32,1024]{1,0:T(8,128)(2,1)S(1)} %copy-done.9, ...), custom_call_target="tpu_custom_call" | custom-call | tf_op jit(solution)/shard_map/pack/pallas_call | solution.py:154
  15.7 26.2 %all_to_all.30.recv_ref = bf16[32,160,128]{2,1,0:T(8,128)(2,1)S(1)} all-to-all(bf16[32,160,128]{2,1,0:T(8,128)(2,1)S(1)} %get-tuple-element.15.send_ref), channel_id=1, replica_groups=mesh['dp'=16,'y'=4,'x'=4,'core'=2] {'y','x','core'}, dimensions={0} | all-to-all | bytes 2621440 | tf_op jit(solution)/shard_map/all_to_all | solution.py:170
  41.9 0.8 vectors.1
  42.7 14.8 %all_to_all.31.vec_ref = f32[32,32,128]{2,1,0:T(8,128)S(1)} all-to-all(f32[32,32,128]{2,1,0:T(8,128)S(1)} %vectors.1), channel_id=1, replica_groups=mesh['dp'=16,'y'=4,'x'=4,'core'=2] {'y','x','core'}, dimensions={0} | all-to-all | bytes 1048576 | tf_op jit(solution)/shard_map/all_to_all | solution.py:179
  57.5 2.7 %parts.1 = f32[64,96,128]{2,1,0:T(8,128)} custom-call(s32[1,8]{1,0:T(1,128)S(1)} %copy-done.10, f32[32,32,128]{2,1,0:T(8,128)S(1)} %all_to_all.31.vec_ref, bf16[32,160,128]{2,1,0:T(8,128)(2,1)S(1)} %all_to_all.30.recv_ref), custom_call_target="tpu_custom_call" | custom-call | tf_op jit(solution)/shard_map/parts/pallas_call | solution.py:180
  60.3 0.0 copy-start
  60.3 0.8 copy-done
  61.1 0.0 reduce-scatter.2.cloned.1.call-update
  61.1 0.6 gather_fusion.3
  61.6 1.8 %gather_fusion.2 = bf16[8,32,160]{2,1,0:T(8,128)(2,1)S(1)} fusion(bf16[64,32,160]{2,1,0:T(8,128)(2,1)} %ak_hbm.1, s32[1024]{0:T(1024)S(1)} %pad_clamp_fusion), kind=kCustom, calls=%fused_computation.2 | custom fusion | bytes 163872 | tf_op jit(solution)/shard_map/gather | solution.py:197
  63.5 0.3 copy.26
  63.7 0.0 copy-start.13
  63.8 0.0 copy-start.14
  63.8 0.9 broadcast_in_dim.8
  64.7 3.5 %all-to-all-start.4 = ((bf16[2,8,160,128]{3,2,1,0:T(8,128)(2,1)}), bf16[2,8,160,128]{3,2,1,0:T(8,128)(2,1)S(1)}, u32[]{:S(2)}, u32[]{:S(2)}) async-start(bf16[2,8,160,128]{3,2,1,0:T(8,128)(2,1)} %broadcast_in_dim.8), calls=%async_computation.4 | async-start | bytes 1310720 | tf_op jit(solution)/shard_map/all_to_all | solution.py:193
  68.2 0.0 copy-done.13
  68.2 0.0 copy-done.14
  68.3 2.5 %all-to-all-done.4 = bf16[2,8,160,128]{3,2,1,0:T(8,128)(2,1)S(1)} async-done(((bf16[2,8,160,128]{3,2,1,0:T(8,128)(2,1)}), bf16[2,8,160,128]{3,2,1,0:T(8,128)(2,1)S(1)}, u32[]{:S(2)}, u32[]{:S(2)}) %all-to-all-start.4) | async-done | bytes 655392 | tf_op jit(solution)/shard_map/all_to_all | solution.py:193
  70.8 0.0 copy-start.12
  70.8 0.2 broadcast_in_dim.7
  71.0 4.8 %all_to_all.32.w_ref = bf16[2,160,2048]{2,1,0:T(8,128)(2,1)S(1)} all-to-all(bf16[2,160,2048]{2,1,0:T(8,128)(2,1)S(1)} %broadcast_in_dim.7), channel_id=1, replica_groups=mesh['dp'=16,'y'=4,'x'=4,'core'=2] {'core'}, dimensions={0} | all-to-all | bytes 2621440 | tf_op jit(solution)/shard_map/all_to_all | solution.py:193
  75.8 1.6 %broadcast_in_dim.6 = bf16[16,32,2048]{2,1,0:T(8,128)(2,1)} broadcast(bf16[32,2048]{1,0:T(8,128)(2,1)S(1)} %get-tuple-element.17), dimensions={1,2} | broadcast | bytes 2228224 | tf_op jit(solution)/shard_map/broadcast_in_dim | solution.py:194
  77.4 0.0 copy-done.12
  77.4 6.0 %all-to-all-start.2 = ((bf16[16,32,2048]{2,1,0:T(8,128)(2,1)}), bf16[16,32,2048]{2,1,0:T(8,128)(2,1)S(1)}, u32[]{:S(2)}, u32[]{:S(2)}) async-start(bf16[16,32,2048]{2,1,0:T(8,128)(2,1)} %broadcast_in_dim.6), calls=%async_computation.2 | async-start | bytes 4194304 | tf_op jit(solution)/shard_map/all_to_all | solution.py:193
  83.4 0.0 copy-start.1
  83.4 2.0 %copy.31 = bf16[2,8,160,128]{3,2,0,1:T(8,128)(2,1)} copy(bf16[2,8,160,128]{3,2,1,0:T(8,128)(2,1)} %copy-done.12) | data formatting | bytes 1310720 | tf_op jit(solution)/shard_map/all_to_all | solution.py:193
  85.4 0.0 copy-done.1
  85.4 0.7 dynamic-slice_bitcast_fusion.vec_ref
  86.2 26.1 %all-to-all-done.2.kv_ref = bf16[16,32,2048]{2,1,0:T(8,128)(2,1)S(1)} async-done(((bf16[16,32,2048]{2,1,0:T(8,128)(2,1)}), bf16[16,32,2048]{2,1,0:T(8,128)(2,1)S(1)}, u32[]{:S(2)}, u32[]{:S(2)}) %all-to-all-start.2) | async-done | bytes 2097184 | tf_op jit(solution)/shard_map/all_to_all | solution.py:193
  112.3 0.0 copy-start.2
  112.3 1.1 copy-done.2
  113.4 0.0 copy-start.5
  113.4 1.0 copy-done.5
  114.4 3.3 %base.1 = bf16[16,32,320]{2,1,0:T(8,128)(2,1)S(1)} custom-call(bf16[16,32,2048]{2,1,0:T(8,128)(2,1)S(1)} %all-to-all-done.2.kv_ref, bf16[2,160,2048]{2,1,0:T(8,128)(2,1)S(1)} %all_to_all.32.w_ref, f32[16,32,128]{2,1,0:T(8,128)S(1)} %copy-done.5, bf16[8,2,160,128]{3,2,1,0:T(8,128)(2,1)S(1)} %bitcast.17), custom_call_target="tpu_custom_call" | custom-call | tf_op jit(solution)/shard_map/base/pallas_call | solution.py:203
  117.7 15.0 %all_to_all.33 = bf16[16,32,320]{2,1,0:T(8,128)(2,1)S(1)} all-to-all(bf16[16,32,320]{2,1,0:T(8,128)(2,1)S(1)} %base.1), channel_id=1, replica_groups=mesh['dp'=16,'y'=4,'x'=4,'core'=2] {'y','x'}, dimensions={0} | all-to-all | bytes 655360 | tf_op jit(solution)/shard_map/all_to_all | solution.py:211
  132.6 0.1 copy.28
  132.8 1.0 reshape.52
  133.8 6.5 %reduce-scatter.2.cloned.1.call-done.sum_ref = f32[4,96,128]{2,1,0:T(8,128)} async-done(((f32[64,96,128]{2,1,0:T(8,128)}), f32[4,96,128]{2,1,0:T(8,128)}) %reduce-scatter.2.cloned.1.call-update) | async-done | bytes 196624 | tf_op jit(solution)/shard_map/reduce_scatter | solution.py:189
  140.3 0.0 copy-start.7
  140.3 0.9 copy-done.7
  141.3 0.8 finish.1
  (3 shorter events, 0.1 us)
Async XLA Ops:
  7.2 5.6 %copy-start.10 = (s32[1,8]{1,0:T(1,128)S(1)}, s32[1,8]{1,0:T(1,128)}, u32[]{:S(2)}) copy-start(s32[1,8]{1,0:T(1,128)} %tenants.3) | copy-start | bytes 100
  7.2 5.6 %copy-start.3 = (bf16[64,32,160]{2,1,0:T(8,128)(2,1)S(1)}, bf16[64,32,160]{2,1,0:T(8,128)(2,1)}, u32[]{:S(2)}) copy-start(bf16[64,32,160]{2,1,0:T(8,128)(2,1)} %av_hbm.1) | copy-start | bytes 1966084
  7.2 5.6 %copy-start.11 = (s32[1,8]{1,0:T(1,128)S(1)}, s32[1,8]{1,0:T(1,128)}, u32[]{:S(2)}) copy-start(s32[1,8]{1,0:T(1,128)} %counts.1) | copy-start | bytes 100
  7.2 5.6 %copy-start.9 = (bf16[32,1024]{1,0:T(8,128)(2,1)S(1)}, bf16[32,1024]{1,0:T(8,128)(2,1)}, u32[]{:S(2)}) copy-start(bf16[32,1024]{1,0:T(8,128)(2,1)} %v_ref.1) | copy-start | bytes 196612
  7.2 5.6 %copy-start.8 = (bf16[32,1024]{1,0:T(8,128)(2,1)S(1)}, bf16[32,1024]{1,0:T(8,128)(2,1)}, u32[]{:S(2)}) copy-start(bf16[32,1024]{1,0:T(8,128)(2,1)} %k_ref.1) | copy-start | bytes 196612
  7.2 5.6 %copy-start.6 = (bf16[32,5120]{1,0:T(8,128)(2,1)S(1)}, bf16[32,5120]{1,0:T(8,128)(2,1)}, u32[]{:S(2)}) copy-start(bf16[32,5120]{1,0:T(8,128)(2,1)} %x_ref.1) | copy-start | bytes 983044
  7.2 133.1 %reduce-scatter.2.cloned.1.call-start = ((), (), s32[]{:S(2)}) async-start(), calls=%async_computation.7 | async-start | bytes 3342336 | tf_op jit(solution)/shard_map/reduce_scatter | solution.py:189
  12.8 1.2 copy-start.4
  60.3 0.8 copy-start
  63.7 4.5 %copy-start.13 = (bf16[160,1024]{1,0:T(8,128)(2,1)S(1)}, bf16[160,1024]{1,0:T(8,128)(2,1)}, u32[]{:S(2)}) copy-start(bf16[160,1024]{1,0:T(8,128)(2,1)} %param.15) | copy-start | bytes 983044
  63.8 4.5 %copy-start.14 = (bf16[160,1024]{1,0:T(8,128)(2,1)S(1)}, bf16[160,1024]{1,0:T(8,128)(2,1)}, u32[]{:S(2)}) copy-start(bf16[160,1024]{1,0:T(8,128)(2,1)} %param.14) | copy-start | bytes 983044
  64.7 6.1 %all-to-all-start.4 = ((bf16[2,8,160,128]{3,2,1,0:T(8,128)(2,1)}), bf16[2,8,160,128]{3,2,1,0:T(8,128)(2,1)S(1)}, u32[]{:S(2)}, u32[]{:S(2)}) async-start(bf16[2,8,160,128]{3,2,1,0:T(8,128)(2,1)} %broadcast_in_dim.8), calls=%async_computation.4 | async-start | bytes 1310720 | tf_op jit(solution)/shard_map/all_to_all | solution.py:193
  70.8 6.6 %copy-start.12 = (bf16[2,8,160,128]{3,2,1,0:T(8,128)(2,1)}, bf16[2,8,160,128]{3,2,1,0:T(8,128)(2,1)S(1)}, u32[]{:S(2)}) copy-start(bf16[2,8,160,128]{3,2,1,0:T(8,128)(2,1)S(1)} %all-to-all-done.4) | copy-start | bytes 1966084
  77.4 34.9 %all-to-all-start.2 = ((bf16[16,32,2048]{2,1,0:T(8,128)(2,1)}), bf16[16,32,2048]{2,1,0:T(8,128)(2,1)S(1)}, u32[]{:S(2)}, u32[]{:S(2)}) async-start(bf16[16,32,2048]{2,1,0:T(8,128)(2,1)} %broadcast_in_dim.6), calls=%async_computation.2 | async-start | bytes 4194304 | tf_op jit(solution)/shard_map/all_to_all | solution.py:193
  83.4 2.1 %copy-start.1 = (f32[32,32,128]{2,1,0:T(8,128)S(1)}, f32[32,32,128]{2,1,0:T(8,128)}, u32[]{:S(2)}) copy-start(f32[32,32,128]{2,1,0:T(8,128)} %copy-done) | copy-start | bytes 1572868
  112.3 1.1 copy-start.2
  113.4 1.0 copy-start.5
  140.3 0.9 copy-start.7
Sparse Core Ops, SparseCore 0:
  61.2 79.0 reduce-scatter.1

commit v2 on v1

--- a/solution.py
+++ b/solution.py
@@ -19,8 +19,8 @@
 
 
 def pack_kernel(
-    tenants, counts, where, x_ref, k_ref, v_ref, up_ref, ak_hbm, av_hbm,
-    send_ref, masked_ref, ak, av, sems,
+    tenants, counts, where, x_ref, k_ref, v_ref, bk_ref, bv_ref, ak_hbm, av_hbm,
+    send_ref, masked_ref, empty_hbm, ak, av, up, zeros, sems, zero_sems,
 ):
     n_mp = send_ref.shape[0]
     blocks = ak.shape[0]
@@ -36,6 +36,14 @@
         copies.append(pltpu.make_async_copy(ak_hbm.at[t], ak.at[b], sems.at[0, b]))
         copies.append(pltpu.make_async_copy(av_hbm.at[t], av.at[b], sems.at[1, b]))
     for c in copies:
+        c.start()
+    zeros[...] = jnp.zeros_like(zeros)
+    chunk = zeros.shape[0]
+    fills = [
+        pltpu.make_async_copy(zeros, empty_hbm.at[pl.ds(i * chunk, chunk)], zero_sems.at[i])
+        for i in range(empty_hbm.shape[0] // chunk)
+    ]
+    for c in fills:
         c.start()
     me = where[0]
     count = counts[0, me // quad]
@@ -52,19 +60,32 @@
         send_ref[j, 128:160, :] = jnp.concatenate(
             [last, mk[:, cols * j : cols * (j + 1)], last, mv[:, cols * j : cols * (j + 1)]], axis=1
         )
+    which = lax.broadcasted_iota(jnp.int32, (blocks, bk_ref.shape[2]), 0)
+    tenant = jnp.zeros_like(which)
+    for b in range(blocks):
+        tenant = jnp.where(which == b, tenants[0, b], tenant)
+    hot = lax.broadcasted_iota(jnp.int32, tenant.shape, 1) == tenant
+    hot = jnp.where(hot, 1.0, 0.0).astype(BF16)
+    for ref, at in ((bk_ref, 32), (bv_ref, 96)):
+        flat = ref[...].reshape(rank * cols, ref.shape[2])
+        got = lax.dot_general(hot, flat, (((1,), (1,)), ((), ())), preferred_element_type=F32)
+        for r in range(rank):
+            up[:, r, at : at + cols] = got[:, cols * r : cols * (r + 1)]
     for c in copies:
         c.wait()
     for b in range(blocks):
         a0 = ak[b]
         a1 = av[b]
         main = jnp.concatenate([a0[:, :LANE], a1[:, :LANE]], axis=0)
-        up = up_ref[b]
+        near = up[b].astype(BF16)
         tail = jnp.concatenate(
-            [a0[:, LANE:], up[:, :cols], a1[:, LANE:], up[:, cols : 2 * cols]], axis=1
+            [a0[:, LANE:], near[:, 32:64], a1[:, LANE:], near[:, 96:128]], axis=1
         )
         for q in range(quad):
             send_ref[quad * b + q, 0:64, :] = main
             send_ref[quad * b + q, 64:96, :] = tail
+    for c in fills:
+        c.wait()
 
 
 def lane_mask(rows, slot):
@@ -93,23 +114,36 @@
     return hi, (x - hi.astype(F32)).astype(BF16)
 
 
-def parts_kernel(tenants, vec_ref, recv_ref, out_ref):
+def parts_kernel(tenants, vec_ref, recv_ref, empty_hbm, out_hbm, acc, sems):
     blocks = vec_ref.shape[0] // 4
-    out_ref[...] = jnp.zeros_like(out_ref)
     m0, m1, m2, m3 = [lane_mask(32, s) for s in range(4)]
+    first = []
+    for b in range(blocks):
+        f = jnp.int32(b)
+        for c in range(b - 1, -1, -1):
+            f = jnp.where(tenants[0, c] == tenants[0, b], c, f)
+        first.append(f)
+    acc[...] = jnp.zeros_like(acc)
     for b in range(blocks):
         vec = vec_ref[4 * b : 4 * b + 4].reshape(BLOCK, LANE) * SCALE
         lhs = jnp.concatenate(split(vec), axis=0)
-        first = recv_ref[4 * b : 4 * b + 4, 96:128, :].reshape(BLOCK, LANE)
-        second = recv_ref[4 * b : 4 * b + 4, 128:160, :].reshape(BLOCK, LANE)
-        rhs = jnp.concatenate([first, second], axis=1)
+        near = recv_ref[4 * b : 4 * b + 4, 96:128, :].reshape(BLOCK, LANE)
+        far = recv_ref[4 * b : 4 * b + 4, 128:160, :].reshape(BLOCK, LANE)
+        rhs = jnp.concatenate([near, far], axis=1)
         rhs = jnp.concatenate([rhs, rhs], axis=0)
         p = lax.dot_general(lhs, rhs, (((0,), (0,)), ((), ())), preferred_element_type=F32)
-        t = tenants[0, b]
-        out_ref[t, 0:64, :] += p[64:128, :LANE]
         q = p[:, LANE:]
         tail = jnp.where(m0, q[64:96], jnp.where(m1, q[0:32], jnp.where(m2, q[96:128], q[32:64])))
-        out_ref[t, 64:96, :] += tail
+        acc[first[b], 0:64, :] += p[64:128, :LANE]
+        acc[first[b], 64:96, :] += tail
+    copies = [
+        pltpu.make_async_copy(acc.at[b], out_hbm.at[tenants[0, b]], sems.at[b])
+        for b in range(blocks)
+    ]
+    for b in range(blocks):
+        pl.when(first[b] == b)(copies[b].start)
+    for b in range(blocks):
+        pl.when(first[b] == b)(copies[b].wait)
 
 
 def base_kernel(kv_ref, w_ref, vec_ref, a_ref, out_ref):
@@ -150,23 +184,30 @@
     core = lax.axis_index("core")
     tenant_index = tenant_of_block[0]
 
-    up = jnp.concatenate([bk[tenant_index], bv[tenant_index]], axis=-1)
-    send, masked = pl.pallas_call(
+    packed = (tenants, 96, LANE)
+    send, masked, empty = pl.pallas_call(
         pack_kernel,
         out_shape=(
             jax.ShapeDtypeStruct((n_mp, 160, LANE), BF16),
             jax.ShapeDtypeStruct((tok, 2 * kv_width), BF16),
+            jax.ShapeDtypeStruct(packed, F32),
         ),
-        in_specs=[SMEM, SMEM, SMEM, VMEM, VMEM, VMEM, VMEM, ANY, ANY],
-        out_specs=(VMEM, VMEM),
+        in_specs=[SMEM, SMEM, SMEM, VMEM, VMEM, VMEM, VMEM, VMEM, ANY, ANY],
+        out_specs=(VMEM, VMEM, ANY),
         scratch_shapes=[
             pltpu.VMEM((blocks, rank, feat), BF16),
             pltpu.VMEM((blocks, rank, feat), BF16),
+            pltpu.VMEM((blocks, rank, LANE), F32),
+            pltpu.VMEM((tenants // 8, 96, LANE), F32),
             pltpu.SemaphoreType.DMA((2, blocks)),
+            pltpu.SemaphoreType.DMA((8,)),
         ],
         compiler_params=PARAMS,
         name="pack",
-    )(tenant_of_block, live_token_count, me, x, kg, vg, up, ak, av)
+    )(
+        tenant_of_block, live_token_count, me, x, kg, vg,
+        bk.transpose(1, 2, 0), bv.transpose(1, 2, 0), ak, av,
+    )
     recv = lax.all_to_all(send, mp, split_axis=0, concat_axis=0, tiled=True)
     vec_send = pl.pallas_call(
         vector_kernel,
@@ -179,12 +220,17 @@
     vec = lax.all_to_all(vec_send, mp, split_axis=0, concat_axis=0, tiled=True)
     parts = pl.pallas_call(
         parts_kernel,
-        out_shape=jax.ShapeDtypeStruct((tenants, 96, LANE), F32),
-        in_specs=[SMEM, VMEM, VMEM],
-        out_specs=VMEM,
+        out_shape=jax.ShapeDtypeStruct(packed, F32),
+        in_specs=[SMEM, VMEM, VMEM, ANY],
+        out_specs=ANY,
+        scratch_shapes=[
+            pltpu.VMEM((blocks, 96, LANE), F32),
+            pltpu.SemaphoreType.DMA((blocks,)),
+        ],
+        input_output_aliases={3: 0},
         compiler_params=PARAMS,
         name="parts",
-    )(tenant_of_block, vec, recv)
+    )(tenant_of_block, vec, recv, empty)
     parts, masked, wk, wv = lax.optimization_barrier((parts, masked, wk, wv))
     sums = lax.psum_scatter(parts, "dp", scatter_dimension=0, tiled=True)
 

time: 150 us -> 152 us (1.013)
  the two profiles are of different devices: /device:TPU:10 before, /device:TPU:2 now
where the time goes in v2:
time: 152 us; the launch traced here: 151 us
  blocking collectives  64.2 us (42%)
  waiting for transfers between devices  30.1 us (20%)
  local copies, waits for them, and re-layouts  24.1 us (16%)
  between operations  14.2 us (9%)
  Pallas kernels  10 us (7%)
  starting transfers between devices  8.55 us (6%)
    all_to_all x2, waiting for transfers between devices, spread(): lax.all_to_all(jnp.broadcast_to(a[None], (n, *a.shape)), axes, split_axis...  28.1 us
    all_to_all x1, blocking collectives, shards(): recv = lax.all_to_all(send, mp, split_axis=0, concat_axis=0, tiled=True)  27.6 us
    all_to_all x1, blocking collectives, shards(): lax.all_to_all(grad, ('y', 'x'), split_axis=0, concat_axis=0, tiled=True)  16.6 us
    all_to_all x1, blocking collectives, shards(): vec = lax.all_to_all(vec_send, mp, split_axis=0, concat_axis=0, tiled=True)  15.3 us
    unnamed x36, local copies, waits for them, and re-layouts  13.6 us
    all_to_all x2, starting transfers between devices, spread(): lax.all_to_all(jnp.broadcast_to(a[None], (n, *a.shape)), axes, split_axis...  8.52 us
    all_to_all x1, blocking collectives, spread(): lax.all_to_all(jnp.broadcast_to(a[None], (n, *a.shape)), axes, split_axis...  4.79 us
    gather x2, local copies, waits for them, and re-layouts, shards(): chosen = jnp.concatenate([ak[tenant_index], av[tenant_index]], axis=1)  3.56 us
  transfers between devices with their start and end apart: 3, of which 3 were waited for; matrix products, arithmetic and copies ran while one was open for 7% of the time, Pallas kernels for 2%

profile of v2, /device:TPU:2, one launch (start us, length us, event | category | flops | bytes accessed | tf_op | source)
XLA Modules:
  0.0 151.2 jit_solution(12116634952789029939)
XLA Ops:
  7.2 0.0 reduce-scatter.2.cloned.1.call-start
  7.2 0.0 copy-start.3
  7.2 1.2 copy-done.3
  8.4 0.0 copy-start.4
  8.5 1.2 copy-done.4
  9.7 0.0 copy-start.6
  9.7 1.0 copy-done.6
  10.6 0.0 copy-start.7
  10.7 0.9 copy-done.7
  11.6 0.0 copy-start.8
  11.6 0.9 copy-done.8
  12.5 0.0 copy-start.10
  12.6 0.8 copy-done.10
  13.4 0.0 copy-start.11
  13.4 0.8 copy-done.11
  14.2 0.0 copy-start.12
  14.2 0.7 copy-done.12
  14.9 0.0 copy-start.14
  14.9 0.7 copy-done.14
  15.5 3.5 %pack.1 = (bf16[32,160,128]{2,1,0:T(8,128)(2,1)S(1)}, bf16[32,2048]{1,0:T(8,128)(2,1)S(1)}, f32[64,96,128]{2,1,0:T(8,128)}) custom-call(s32[1,8]{1,0:T(1,128)S(1)} %copy-done.12, s32[1,8]{1,0:T(1,128)S(1)} %copy-done.14, s32[1]{0:T(128)} %bitcast.where, bf16[32,5120]{1,0:T(8,128)(2,1)S(1)} %copy-done.6, bf16[32,1024]{1,0:T(8,128)(2,1)S(1)} %copy-done.10, ...), custom_call_target="tpu_custom_call" | custom-call | tf_op jit(solution)/shard_map/pack/pallas_call | solution.py:188
  19.0 27.6 %all_to_all.30.recv_ref = bf16[32,160,128]{2,1,0:T(8,128)(2,1)S(1)} all-to-all(bf16[32,160,128]{2,1,0:T(8,128)(2,1)S(1)} %get-tuple-element.16.send_ref), channel_id=1, replica_groups=mesh['dp'=16,'y'=4,'x'=4,'core'=2] {'y','x','core'}, dimensions={0} | all-to-all | bytes 2621440 | tf_op jit(solution)/shard_map/all_to_all | solution.py:211
  46.6 0.8 vectors.1
  47.4 15.3 %all_to_all.31.vec_ref = f32[32,32,128]{2,1,0:T(8,128)S(1)} all-to-all(f32[32,32,128]{2,1,0:T(8,128)S(1)} %vectors.1), channel_id=1, replica_groups=mesh['dp'=16,'y'=4,'x'=4,'core'=2] {'y','x','core'}, dimensions={0} | all-to-all | bytes 1048576 | tf_op jit(solution)/shard_map/all_to_all | solution.py:220
  62.7 1.6 %parts.1 = f32[64,96,128]{2,1,0:T(8,128)} custom-call(s32[1,8]{1,0:T(1,128)S(1)} %copy-done.12, f32[32,32,128]{2,1,0:T(8,128)S(1)} %all_to_all.31.vec_ref, bf16[32,160,128]{2,1,0:T(8,128)(2,1)S(1)} %all_to_all.30.recv_ref, f32[64,96,128]{2,1,0:T(8,128)} %get-tuple-element.17.empty_hbm), custom_call_target="tpu_custom_call", output_to_operand_aliasing={{}: (3, {})} | custom-call | tf_op jit(solution)/shard_map/parts/pallas_call | solution.py:221
  64.3 0.0 copy-start
  64.3 0.8 copy-done
  65.1 0.0 copy-start.13
  65.1 0.0 reduce-scatter.2.cloned.1.call-update
  65.2 0.6 copy-done.13
  65.8 1.8 %gather_fusion.1 = bf16[8,32,160]{2,1,0:T(8,128)(2,1)S(1)} fusion(bf16[64,32,160]{2,1,0:T(8,128)(2,1)} %av_hbm.1, s32[1024]{0:T(1024)S(1)} %pad_clamp_fusion), kind=kCustom, calls=%fused_computation.1 | custom fusion | bytes 163872 | tf_op jit(solution)/shard_map/gather | solution.py:243
  67.6 1.8 %gather_fusion = bf16[8,32,160]{2,1,0:T(8,128)(2,1)S(1)} fusion(bf16[64,32,160]{2,1,0:T(8,128)(2,1)} %ak_hbm.1, s32[1024]{0:T(1024)S(1)} %pad_clamp_fusion), kind=kCustom, calls=%fused_computation | custom fusion | bytes 163872 | tf_op jit(solution)/shard_map/gather | solution.py:243
  69.4 0.3 copy.23
  69.7 0.0 copy-start.16
  69.7 0.0 copy-start.17
  69.7 0.9 broadcast_in_dim.8
  70.7 3.5 %all-to-all-start.4 = ((bf16[2,8,160,128]{3,2,1,0:T(8,128)(2,1)}), bf16[2,8,160,128]{3,2,1,0:T(8,128)(2,1)S(1)}, u32[]{:S(2)}, u32[]{:S(2)}) async-start(bf16[2,8,160,128]{3,2,1,0:T(8,128)(2,1)} %broadcast_in_dim.8), calls=%async_computation.4 | async-start | bytes 1310720 | tf_op jit(solution)/shard_map/all_to_all | solution.py:239
  74.2 0.0 copy-done.16
  74.2 0.0 copy-done.17
  74.3 1.7 %all-to-all-done.4 = bf16[2,8,160,128]{3,2,1,0:T(8,128)(2,1)S(1)} async-done(((bf16[2,8,160,128]{3,2,1,0:T(8,128)(2,1)}), bf16[2,8,160,128]{3,2,1,0:T(8,128)(2,1)S(1)}, u32[]{:S(2)}, u32[]{:S(2)}) %all-to-all-start.4) | async-done | bytes 655392 | tf_op jit(solution)/shard_map/all_to_all | solution.py:239
  76.0 0.0 copy-start.15
  76.0 0.8 copy-done.15
  76.8 0.2 broadcast_in_dim.7
  77.0 4.8 %all_to_all.32.w_ref = bf16[2,160,2048]{2,1,0:T(8,128)(2,1)S(1)} all-to-all(bf16[2,160,2048]{2,1,0:T(8,128)(2,1)S(1)} %broadcast_in_dim.7), channel_id=1, replica_groups=mesh['dp'=16,'y'=4,'x'=4,'core'=2] {'core'}, dimensions={0} | all-to-all | bytes 2621440 | tf_op jit(solution)/shard_map/all_to_all | solution.py:239
  81.8 1.6 %broadcast_in_dim.6 = bf16[16,32,2048]{2,1,0:T(8,128)(2,1)} broadcast(bf16[32,2048]{1,0:T(8,128)(2,1)S(1)} %get-tuple-element.19), dimensions={1,2} | broadcast | bytes 2228224 | tf_op jit(solution)/shard_map/broadcast_in_dim | solution.py:240
  83.5 5.0 %all-to-all-start.2 = ((bf16[16,32,2048]{2,1,0:T(8,128)(2,1)}), bf16[16,32,2048]{2,1,0:T(8,128)(2,1)S(1)}, u32[]{:S(2)}, u32[]{:S(2)}) async-start(bf16[16,32,2048]{2,1,0:T(8,128)(2,1)} %broadcast_in_dim.6), calls=%async_computation.2 | async-start | bytes 4194304 | tf_op jit(solution)/shard_map/all_to_all | solution.py:239
  88.5 0.0 copy-start.1
  88.5 2.1 %copy.28 = bf16[2,8,160,128]{3,2,0,1:T(8,128)(2,1)} copy(bf16[2,8,160,128]{3,2,1,0:T(8,128)(2,1)} %copy-done.15) | data formatting | bytes 1310720 | tf_op jit(solution)/shard_map/all_to_all | solution.py:239
  90.5 0.0 copy-done.1
  90.5 0.7 dynamic-slice_bitcast_fusion.vec_ref
  91.2 26.4 %all-to-all-done.2.kv_ref = bf16[16,32,2048]{2,1,0:T(8,128)(2,1)S(1)} async-done(((bf16[16,32,2048]{2,1,0:T(8,128)(2,1)}), bf16[16,32,2048]{2,1,0:T(8,128)(2,1)S(1)}, u32[]{:S(2)}, u32[]{:S(2)}) %all-to-all-start.2) | async-done | bytes 2097184 | tf_op jit(solution)/shard_map/all_to_all | solution.py:239
  117.6 0.0 copy-start.2
  117.6 1.1 copy-done.2
  118.7 0.0 copy-start.5
  118.7 0.9 copy-done.5
  119.7 3.3 %base.1 = bf16[16,32,320]{2,1,0:T(8,128)(2,1)S(1)} custom-call(bf16[16,32,2048]{2,1,0:T(8,128)(2,1)S(1)} %all-to-all-done.2.kv_ref, bf16[2,160,2048]{2,1,0:T(8,128)(2,1)S(1)} %all_to_all.32.w_ref, f32[16,32,128]{2,1,0:T(8,128)S(1)} %copy-done.5, bf16[8,2,160,128]{3,2,1,0:T(8,128)(2,1)S(1)} %bitcast.19), custom_call_target="tpu_custom_call" | custom-call | tf_op jit(solution)/shard_map/base/pallas_call | solution.py:249
  123.0 16.6 %all_to_all.33 = bf16[16,32,320]{2,1,0:T(8,128)(2,1)S(1)} all-to-all(bf16[16,32,320]{2,1,0:T(8,128)(2,1)S(1)} %base.1), channel_id=1, replica_groups=mesh['dp'=16,'y'=4,'x'=4,'core'=2] {'y','x'}, dimensions={0} | all-to-all | bytes 655360 | tf_op jit(solution)/shard_map/all_to_all | solution.py:257
  139.5 0.1 copy.25
  139.7 1.0 reshape.52
  140.7 2.0 %reduce-scatter.2.cloned.1.call-done.sum_ref = f32[4,96,128]{2,1,0:T(8,128)} async-done(((f32[64,96,128]{2,1,0:T(8,128)}), f32[4,96,128]{2,1,0:T(8,128)}) %reduce-scatter.2.cloned.1.call-update) | async-done | bytes 196624 | tf_op jit(solution)/shard_map/reduce_scatter | solution.py:235
  142.7 0.0 copy-start.9
  142.7 0.9 copy-done.9
  143.6 0.8 finish.1
  (4 shorter events, 0.1 us)
Async XLA Ops:
  7.2 135.5 %reduce-scatter.2.cloned.1.call-start = ((), (), s32[]{:S(2)}) async-start(), calls=%async_computation.7 | async-start | bytes 3342336 | tf_op jit(solution)/shard_map/reduce_scatter | solution.py:235
  7.2 1.2 copy-start.3
  8.4 1.2 copy-start.4
  9.7 1.0 copy-start.6
  10.6 0.9 copy-start.7
  11.6 0.9 copy-start.8
  12.5 0.8 copy-start.10
  13.4 0.8 copy-start.11
  14.2 0.7 copy-start.12
  14.9 0.7 copy-start.14
  64.3 0.8 copy-start
  65.1 0.7 copy-start.13
  69.7 4.5 %copy-start.16 = (bf16[160,1024]{1,0:T(8,128)(2,1)S(1)}, bf16[160,1024]{1,0:T(8,128)(2,1)}, u32[]{:S(2)}) copy-start(bf16[160,1024]{1,0:T(8,128)(2,1)} %param.15) | copy-start | bytes 983044
  69.7 4.5 %copy-start.17 = (bf16[160,1024]{1,0:T(8,128)(2,1)S(1)}, bf16[160,1024]{1,0:T(8,128)(2,1)}, u32[]{:S(2)}) copy-start(bf16[160,1024]{1,0:T(8,128)(2,1)} %param.14) | copy-start | bytes 983044
  70.7 5.3 %all-to-all-start.4 = ((bf16[2,8,160,128]{3,2,1,0:T(8,128)(2,1)}), bf16[2,8,160,128]{3,2,1,0:T(8,128)(2,1)S(1)}, u32[]{:S(2)}, u32[]{:S(2)}) async-start(bf16[2,8,160,128]{3,2,1,0:T(8,128)(2,1)} %broadcast_in_dim.8), calls=%async_computation.4 | async-start | bytes 1310720 | tf_op jit(solution)/shard_map/all_to_all | solution.py:239
  76.0 0.8 copy-start.15
  83.5 34.2 %all-to-all-start.2 = ((bf16[16,32,2048]{2,1,0:T(8,128)(2,1)}), bf16[16,32,2048]{2,1,0:T(8,128)(2,1)S(1)}, u32[]{:S(2)}, u32[]{:S(2)}) async-start(bf16[16,32,2048]{2,1,0:T(8,128)(2,1)} %broadcast_in_dim.6), calls=%async_computation.2 | async-start | bytes 4194304 | tf_op jit(solution)/shard_map/all_to_all | solution.py:239
  88.5 2.1 %copy-start.1 = (f32[32,32,128]{2,1,0:T(8,128)S(1)}, f32[32,32,128]{2,1,0:T(8,128)}, u32[]{:S(2)}) copy-start(f32[32,32,128]{2,1,0:T(8,128)} %copy-done) | copy-start | bytes 1572868
  117.6 1.1 copy-start.2
  118.7 1.0 copy-start.5
  142.7 0.9 copy-start.9
Sparse Core Ops, SparseCore 0:
  65.3 77.3 reduce-scatter.1

commit v3 on v2

--- a/solution.py
+++ b/solution.py
@@ -13,46 +13,62 @@
 BF16 = jnp.bfloat16
 VMEM = pl.BlockSpec(memory_space=pltpu.VMEM)
 SMEM = pl.BlockSpec(memory_space=pltpu.SMEM)
-ANY = pl.BlockSpec(memory_space=pl.ANY)
+HBM = pl.BlockSpec(memory_space=pltpu.HBM)
 PARAMS = pltpu.CompilerParams(vmem_limit_bytes=24 * 1024 * 1024)
 LANE = 128
 
 
-def pack_kernel(
-    tenants, counts, where, x_ref, k_ref, v_ref, bk_ref, bv_ref, ak_hbm, av_hbm,
-    send_ref, masked_ref, empty_hbm, ak, av, up, zeros, sems, zero_sems,
-):
-    n_mp = send_ref.shape[0]
-    blocks = ak.shape[0]
-    rank = ak.shape[1]
-    tok = x_ref.shape[0]
-    feat = ak.shape[2]
-    cols = k_ref.shape[1] // n_mp
-    rest = feat - LANE
-    quad = n_mp // blocks
-    copies = []
-    for b in range(blocks):
-        t = tenants[0, b]
-        copies.append(pltpu.make_async_copy(ak_hbm.at[t], ak.at[b], sems.at[0, b]))
-        copies.append(pltpu.make_async_copy(av_hbm.at[t], av.at[b], sems.at[1, b]))
-    for c in copies:
-        c.start()
+FILLS = (6, 10, 16)
+
+
+def start_fills(zeros, out_hbm, sems, first, last):
     zeros[...] = jnp.zeros_like(zeros)
-    chunk = zeros.shape[0]
+    chunk = out_hbm.shape[0] // FILLS[-1]
     fills = [
-        pltpu.make_async_copy(zeros, empty_hbm.at[pl.ds(i * chunk, chunk)], zero_sems.at[i])
-        for i in range(empty_hbm.shape[0] // chunk)
+        pltpu.make_async_copy(zeros, out_hbm.at[pl.ds(i * chunk, chunk)], sems.at[i - first])
+        for i in range(first, last)
     ]
     for c in fills:
         c.start()
+    return fills
+
+
+def pack_kernel(
+    where, tenants_hbm, counts_hbm, x_hbm, k_hbm, v_hbm, bk_hbm, bv_hbm, ak_hbm, av_hbm,
+    send_ref, masked_ref, chosen_ref, empty_hbm,
+    tenants, counts, x_ref, k_ref, v_ref, bk_ref, bv_ref, ak, av, up, zeros, sems, a_sems, fill_sems,
+):
+    n_mp = send_ref.shape[0]
+    blocks, rank, feat = ak.shape
+    tok, kv_width = k_ref.shape
+    cols = kv_width // n_mp
+    quad = n_mp // blocks
+    pairs = (
+        (tenants_hbm, tenants), (counts_hbm, counts), (x_hbm, x_ref), (k_hbm, k_ref),
+        (v_hbm, v_ref), (bk_hbm, bk_ref), (bv_hbm, bv_ref),
+    )
+    loads = [pltpu.make_async_copy(src, dst, sems.at[i]) for i, (src, dst) in enumerate(pairs)]
+    for c in loads:
+        c.start()
+    fills = start_fills(zeros, empty_hbm, fill_sems, 0, FILLS[0])
+    loads[0].wait()
+    copies = []
+    for b in range(blocks):
+        t = tenants[0, b]
+        copies.append(pltpu.make_async_copy(ak_hbm.at[t], ak.at[b], a_sems.at[0, b]))
+        copies.append(pltpu.make_async_copy(av_hbm.at[t], av.at[b], a_sems.at[1, b]))
+    for c in copies:
+        c.start()
+    for c in loads[1:]:
+        c.wait()
     me = where[0]
     count = counts[0, me // quad]
     row = lax.broadcasted_iota(jnp.int32, (tok, 1), 0) + (me % quad) * tok
     live = row < count
     mk = jnp.where(live, k_ref[...].astype(F32), 0.0).astype(BF16)
     mv = jnp.where(live, v_ref[...].astype(F32), 0.0).astype(BF16)
-    masked_ref[:, : mk.shape[1]] = mk
-    masked_ref[:, mk.shape[1] :] = mv
+    masked_ref[:, :kv_width] = mk
+    masked_ref[:, kv_width:] = mv
     x = x_ref[...]
     for j in range(n_mp):
         send_ref[j, 96:128, :] = x[:, feat * j : feat * j + LANE]
@@ -84,6 +100,9 @@
         for q in range(quad):
             send_ref[quad * b + q, 0:64, :] = main
             send_ref[quad * b + q, 64:96, :] = tail
+        for c in range(2):
+            chosen_ref[c, b, :rank, :] = a0
+            chosen_ref[c, b, rank:, :] = a1
     for c in fills:
         c.wait()
 
@@ -93,8 +112,9 @@
     return (lane >= 32 * slot) & (lane < 32 * slot + 32)
 
 
-def vector_kernel(send_ref, recv_ref, out_ref):
+def vector_kernel(send_ref, recv_ref, empty_hbm, out_ref, more_hbm, zeros, fill_sems):
     n_mp = send_ref.shape[0]
+    fills = start_fills(zeros, more_hbm, fill_sems, FILLS[0], FILLS[1])
     masks = [lane_mask(32, s) for s in (0, 2, 1, 3)]
     total = jnp.zeros((32, LANE), F32)
     zero = jnp.zeros((64, LANE), BF16)
@@ -107,6 +127,8 @@
         total += lax.dot_general(lhs, rhs, (((1,), (1,)), ((), ())), preferred_element_type=F32)
     for m in range(n_mp):
         out_ref[m] = total
+    for c in fills:
+        c.wait()
 
 
 def split(x):
@@ -114,8 +136,11 @@
     return hi, (x - hi.astype(F32)).astype(BF16)
 
 
-def parts_kernel(tenants, vec_ref, recv_ref, empty_hbm, out_hbm, acc, sems):
+def parts_kernel(
+    where, tenants, vec_ref, recv_ref, more_hbm, out_hbm, low_ref, acc, zeros, sems, fill_sems
+):
     blocks = vec_ref.shape[0] // 4
+    fills = start_fills(zeros, out_hbm, fill_sems, FILLS[1], FILLS[2])
     m0, m1, m2, m3 = [lane_mask(32, s) for s in range(4)]
     first = []
     for b in range(blocks):
@@ -136,32 +161,43 @@
         tail = jnp.where(m0, q[64:96], jnp.where(m1, q[0:32], jnp.where(m2, q[96:128], q[32:64])))
         acc[first[b], 0:64, :] += p[64:128, :LANE]
         acc[first[b], 64:96, :] += tail
+    for c in fills:
+        c.wait()
     copies = [
         pltpu.make_async_copy(acc.at[b], out_hbm.at[tenants[0, b]], sems.at[b])
         for b in range(blocks)
     ]
     for b in range(blocks):
         pl.when(first[b] == b)(copies[b].start)
+    core = where[0] % 2
+    for i in range(low_ref.shape[0]):
+        back = vec_ref[2 * i + core][:, 64:] * SCALE
+        low_ref[i] = jnp.concatenate(split(back), axis=1)
     for b in range(blocks):
         pl.when(first[b] == b)(copies[b].wait)
 
 
-def base_kernel(kv_ref, w_ref, vec_ref, a_ref, out_ref):
-    blocks = a_ref.shape[0]
+def base_kernel(kv_ref, w_ref, low_ref, a_ref, out_ref):
+    blocks = a_ref.shape[1]
     per = kv_ref.shape[0] // blocks
     w = w_ref[...].reshape(-1, w_ref.shape[-1])
     for b in range(blocks):
         rows = kv_ref[per * b : per * (b + 1)].reshape(-1, kv_ref.shape[-1])
-        vec = vec_ref[per * b : per * (b + 1)].reshape(-1, LANE)[:, 64:] * SCALE
-        low = jnp.concatenate(split(vec), axis=1)
-        a = a_ref[b].reshape(-1, LANE)
-        dims = (((1,), (1,)), ((), ()))
-        res = lax.dot_general(rows, w, dims, preferred_element_type=F32)
-        res += lax.dot_general(low, a, dims, preferred_element_type=F32)
+        low = low_ref[per * b : per * (b + 1)].reshape(-1, LANE)
+        res = lax.dot_general(rows, w, (((1,), (1,)), ((), ())), preferred_element_type=F32)
+        add = []
+        for c in range(2):
+            a = a_ref[c, b]
+            a = jnp.concatenate([a, a], axis=0)
+            add.append(jnp.dot(low, a, preferred_element_type=F32))
+        res += jnp.concatenate(add, axis=1)
         out_ref[per * b : per * (b + 1)] = res.astype(BF16).reshape(per, -1, w.shape[0])
 
 
-def finish_kernel(sum_ref, ak_ref, av_ref, bk_ref, bv_ref):
+def finish_kernel(sum_hbm, ak_ref, av_ref, bk_ref, bv_ref, sum_ref, sem):
+    load = pltpu.make_async_copy(sum_hbm, sum_ref, sem)
+    load.start()
+    load.wait()
     for t in range(sum_ref.shape[0]):
         tail = sum_ref[t, 64:96, :]
         ak_ref[t, :, :LANE] = sum_ref[t, 0:32, :]
@@ -181,71 +217,85 @@
     kv_width = kg.shape[1]
     tenants, rank = ak.shape[:2]
     me = lax.axis_index(mp).astype(jnp.int32).reshape(1)
-    core = lax.axis_index("core")
-    tenant_index = tenant_of_block[0]
-
+    cols = bk.shape[2]
+    hbm = lambda a: pltpu.with_memory_space_constraint(a, pltpu.HBM)
     packed = (tenants, 96, LANE)
-    send, masked, empty = pl.pallas_call(
+    zeros = pltpu.VMEM((tenants // FILLS[-1], 96, LANE), F32)
+    send, masked, chosen, empty = pl.pallas_call(
         pack_kernel,
         out_shape=(
             jax.ShapeDtypeStruct((n_mp, 160, LANE), BF16),
             jax.ShapeDtypeStruct((tok, 2 * kv_width), BF16),
+            jax.ShapeDtypeStruct((2, blocks, 2 * rank, feat), BF16),
             jax.ShapeDtypeStruct(packed, F32),
         ),
-        in_specs=[SMEM, SMEM, SMEM, VMEM, VMEM, VMEM, VMEM, VMEM, ANY, ANY],
-        out_specs=(VMEM, VMEM, ANY),
+        in_specs=[SMEM] + [HBM] * 9,
+        out_specs=(VMEM, VMEM, VMEM, HBM),
         scratch_shapes=[
+            pltpu.SMEM((1, blocks), jnp.int32),
+            pltpu.SMEM((1, blocks), jnp.int32),
+            pltpu.VMEM((tok, width), BF16),
+            pltpu.VMEM((tok, kv_width), BF16),
+            pltpu.VMEM((tok, kv_width), BF16),
+            pltpu.VMEM((rank, cols, tenants), BF16),
+            pltpu.VMEM((rank, cols, tenants), BF16),
             pltpu.VMEM((blocks, rank, feat), BF16),
             pltpu.VMEM((blocks, rank, feat), BF16),
             pltpu.VMEM((blocks, rank, LANE), F32),
-            pltpu.VMEM((tenants // 8, 96, LANE), F32),
+            zeros,
+            pltpu.SemaphoreType.DMA((7,)),
             pltpu.SemaphoreType.DMA((2, blocks)),
-            pltpu.SemaphoreType.DMA((8,)),
+            pltpu.SemaphoreType.DMA((FILLS[0],)),
         ],
         compiler_params=PARAMS,
         name="pack",
     )(
-        tenant_of_block, live_token_count, me, x, kg, vg,
-        bk.transpose(1, 2, 0), bv.transpose(1, 2, 0), ak, av,
+        me, hbm(tenant_of_block), hbm(live_token_count), hbm(x), hbm(kg), hbm(vg),
+        hbm(bk.transpose(1, 2, 0)), hbm(bv.transpose(1, 2, 0)), hbm(ak), hbm(av),
     )
     recv = lax.all_to_all(send, mp, split_axis=0, concat_axis=0, tiled=True)
-    vec_send = pl.pallas_call(
+    vec_send, empty = pl.pallas_call(
         vector_kernel,
-        out_shape=jax.ShapeDtypeStruct((n_mp, tok, LANE), F32),
-        in_specs=[VMEM, VMEM],
-        out_specs=VMEM,
+        out_shape=(
+            jax.ShapeDtypeStruct((n_mp, tok, LANE), F32),
+            jax.ShapeDtypeStruct(packed, F32),
+        ),
+        in_specs=[VMEM, VMEM, HBM],
+        out_specs=(VMEM, HBM),
+        scratch_shapes=[zeros, pltpu.SemaphoreType.DMA((FILLS[1] - FILLS[0],))],
+        input_output_aliases={2: 1},
         compiler_params=PARAMS,
         name="vectors",
-    )(send, recv)
+    )(send, recv, empty)
     vec = lax.all_to_all(vec_send, mp, split_axis=0, concat_axis=0, tiled=True)
-    parts = pl.pallas_call(
+    parts, low = pl.pallas_call(
         parts_kernel,
-        out_shape=jax.ShapeDtypeStruct(packed, F32),
-        in_specs=[SMEM, VMEM, VMEM, ANY],
-        out_specs=ANY,
+        out_shape=(
+            jax.ShapeDtypeStruct(packed, F32),
+            jax.ShapeDtypeStruct((n_mp // 2, tok, LANE), BF16),
+        ),
+        in_specs=[SMEM, SMEM, VMEM, VMEM, HBM],
+        out_specs=(HBM, VMEM),
         scratch_shapes=[
             pltpu.VMEM((blocks, 96, LANE), F32),
+            zeros,
             pltpu.SemaphoreType.DMA((blocks,)),
+            pltpu.SemaphoreType.DMA((FILLS[2] - FILLS[1],)),
         ],
-        input_output_aliases={3: 0},
+        input_output_aliases={4: 0},
         compiler_params=PARAMS,
         name="parts",
-    )(tenant_of_block, vec, recv, empty)
-    parts, masked, wk, wv = lax.optimization_barrier((parts, masked, wk, wv))
+    )(me, tenant_of_block, vec, recv, empty)
+    parts, masked = lax.optimization_barrier((parts, masked))
     sums = lax.psum_scatter(parts, "dp", scatter_dimension=0, tiled=True)
 
-    def spread(a, axes):
-        n = lax.axis_size(axes)
-        return lax.all_to_all(
-            jnp.broadcast_to(a[None], (n, *a.shape)), axes, split_axis=0, concat_axis=0, tiled=True
-        )
-
-    chosen = jnp.concatenate([ak[tenant_index], av[tenant_index]], axis=1)
-    chosen = jnp.concatenate([chosen, chosen], axis=1).transpose(0, 2, 1)
-    kv = spread(masked, ("y", "x"))
-    w = spread(jnp.concatenate([wk, wv], axis=1), ("core",))
-    a = spread(chosen, ("core",)).transpose(1, 0, 2, 3)
-    mine = lax.dynamic_index_in_dim(vec.reshape(n_mp // 2, 2, tok, LANE), core, 1, keepdims=False)
+    def swap(a, axes):
+        return lax.all_to_all(a, axes, split_axis=0, concat_axis=0, tiled=True)
+
+    a = swap(chosen, ("core",))
+    both = jnp.concatenate([wk, wv], axis=1)
+    w = swap(jnp.broadcast_to(both[None], (2, *both.shape)), ("core",))
+    kv = swap(jnp.broadcast_to(masked[None], (n_mp // 2, *masked.shape)), ("y", "x"))
     grad = pl.pallas_call(
         base_kernel,
         out_shape=jax.ShapeDtypeStruct((n_mp // 2, tok, 2 * feat), BF16),
@@ -253,8 +303,8 @@
         out_specs=VMEM,
         compiler_params=PARAMS,
         name="base",
-    )(kv, w, mine, a)
-    grad = lax.all_to_all(grad, ("y", "x"), split_axis=0, concat_axis=0, tiled=True)
+    )(kv, w, low, a)
+    grad = swap(grad, ("y", "x"))
     grad_in = grad.transpose(1, 0, 2).reshape(tok, width)
 
     owned = tenants // lax.axis_size("dp")
@@ -266,11 +316,12 @@
             jax.ShapeDtypeStruct((owned, rank, bk.shape[2]), F32),
             jax.ShapeDtypeStruct((owned, rank, bk.shape[2]), F32),
         ),
-        in_specs=[VMEM],
+        in_specs=[HBM],
         out_specs=(VMEM, VMEM, VMEM, VMEM),
+        scratch_shapes=[pltpu.VMEM((owned, 96, LANE), F32), pltpu.SemaphoreType.DMA],
         compiler_params=PARAMS,
         name="finish",
-    )(sums)
+    )(hbm(sums))
     return (grad_in, *grads)
 
 

time: 152 us -> 144 us (0.947)
  blocking collectives: 64.2 us -> 92.2 us
  local copies, waits for them, and re-layouts: 24.1 us -> 1.59 us
  waiting for transfers between devices: 30.1 us -> 19.5 us
  starting transfers between devices: 8.55 us -> 3.67 us
  Pallas kernels: 10 us -> 12.7 us
    all_to_all x2 -> x3, blocking collectives: 21.4 us -> 49.4 us  [swap(): return lax.all_to_all(a, axes, split_axis=0, concat_axis=0, tiled=True)]
    all_to_all x2 -> x1, waiting for transfers between devices: 28.1 us -> 1.65 us  [swap(): return lax.all_to_all(a, axes, split_axis=0, concat_axis=0, tiled=True)]
    reduce_scatter x1, waiting for transfers between devices: 1.98 us -> 17.8 us  [shards(): sums = lax.psum_scatter(parts, 'dp', scatter_dimension=0, tiled=True)]
    unnamed x36 -> x6, local copies, waits for them, and re-layouts: 13.6 us -> 0.02 us
    all_to_all x2 -> x1, starting transfers between devices: 8.52 us -> 3.63 us  [swap(): return lax.all_to_all(a, axes, split_axis=0, concat_axis=0, tiled=True)]
    gather x2 -> x0, local copies, waits for them, and re-layouts: 3.56 us -> none  [shards(): chosen = jnp.concatenate([ak[tenant_index], av[tenant_index]], axis=1)]
    broadcast_in_dim x3 -> x2, local copies, waits for them, and re-layouts: 2.74 us -> 0.41 us  [the longest x1 0.24 us: shards(): jnp.broadcast_to(masked[None], (n_mp // 2, *masked.shape))]
    all_to_all x1 -> x0, local copies, waits for them, and re-layouts: 2.05 us -> none  [spread(): lax.all_to_all(jnp.broadcast_to(a[None], (n, *a.shape)), axes, split_axis...]
  transfers between devices with their start and end apart: 3 -> 2, of which waited for: 3 -> 2; matrix products, arithmetic and copies ran while one was open for 7% -> 1% of each run, Pallas kernels for 2% -> 2%
where the time goes in v3:
time: 144 us
  blocking collectives  92.2 us (64%)
  waiting for transfers between devices  19.5 us (14%)
  between operations  14.2 us (10%)
  Pallas kernels  12.7 us (9%)
  starting transfers between devices  3.67 us (3%)
  local copies, waits for them, and re-layouts  1.59 us (1%)
    all_to_all x3, blocking collectives, swap(): return lax.all_to_all(a, axes, split_axis=0, concat_axis=0, tiled=True)  49.4 us
    all_to_all x1, blocking collectives, shards(): recv = lax.all_to_all(send, mp, split_axis=0, concat_axis=0, tiled=True)  27.6 us
    reduce_scatter x1, waiting for transfers between devices, shards(): sums = lax.psum_scatter(parts, 'dp', scatter_dimension=0, tiled=True)  17.8 us
    all_to_all x1, blocking collectives, shards(): vec = lax.all_to_all(vec_send, mp, split_axis=0, concat_axis=0, tiled=True)  15.3 us
    pallas_call x1, Pallas kernels, shards(): pl.pallas_call(pack_kernel, out_shape=(jax.ShapeDtypeStruct((n_mp, 160, L...  3.68 us
    all_to_all x1, starting transfers between devices, swap(): return lax.all_to_all(a, axes, split_axis=0, concat_axis=0, tiled=True)  3.63 us
    pallas_call x1, Pallas kernels, shards(): pl.pallas_call(base_kernel, out_shape=jax.ShapeDtypeStruct((n_mp // 2, to...  3.22 us
  transfers between devices with their start and end apart: 2, of which 2 were waited for; matrix products, arithmetic and copies ran while one was open for 1% of the time, Pallas kernels for 2%

profile of v3, /device:TPU:2, one launch (start us, length us, event | category | flops | bytes accessed | tf_op | source)
XLA Modules:
  0.0 143.9 jit_solution(15561881434618145307)
XLA Ops:
  7.2 0.0 reduce-scatter.2.cloned.1.call-start
  7.2 3.7 %pack.1 = (bf16[32,160,128]{2,1,0:T(8,128)(2,1)S(1)}, bf16[32,2048]{1,0:T(8,128)(2,1)S(1)}, bf16[2,8,64,160]{3,2,1,0:T(8,128)(2,1)}, f32[64,96,128]{2,1,0:T(8,128)}) custom-call(s32[1]{0:T(128)} %bitcast.where, s32[1,8]{1,0:T(1,128)} %tenants.1, s32[1,8]{1,0:T(1,128)} %counts_hbm.1, bf16[32,5120]{1,0:T(8,128)(2,1)} %x_hbm.1, bf16[32,1024]{1,0:T(8,128)(2,1)} %k_hbm.1, ...), custom_call_target="tpu_custom_call" | custom-call | tf_op jit(solution)/shard_map/pack/pallas_call | solution.py:224
  10.9 27.6 %all_to_all.30.recv_ref = bf16[32,160,128]{2,1,0:T(8,128)(2,1)S(1)} all-to-all(bf16[32,160,128]{2,1,0:T(8,128)(2,1)S(1)} %get-tuple-element.19.send_ref), channel_id=1, replica_groups=mesh['dp'=16,'y'=4,'x'=4,'core'=2] {'y','x','core'}, dimensions={0} | all-to-all | bytes 2621440 | tf_op jit(solution)/shard_map/all_to_all | solution.py:256
  38.5 0.0 copy-start
  38.5 1.6 %vectors.1 = (f32[32,32,128]{2,1,0:T(8,128)S(1)}, f32[64,96,128]{2,1,0:T(8,128)}) custom-call(bf16[32,160,128]{2,1,0:T(8,128)(2,1)S(1)} %get-tuple-element.19.send_ref, bf16[32,160,128]{2,1,0:T(8,128)(2,1)S(1)} %all_to_all.30.recv_ref, f32[64,96,128]{2,1,0:T(8,128)} %get-tuple-element.20.empty_hbm), custom_call_target="tpu_custom_call", output_to_operand_aliasing={{1}: (2, {})} | custom-call | tf_op jit(solution)/shard_map/vectors/pallas_call | solution.py:257
  40.1 15.3 %all_to_all.31.vec_ref = f32[32,32,128]{2,1,0:T(8,128)S(1)} all-to-all(f32[32,32,128]{2,1,0:T(8,128)S(1)} %get-tuple-element.21), channel_id=1, replica_groups=mesh['dp'=16,'y'=4,'x'=4,'core'=2] {'y','x','core'}, dimensions={0} | all-to-all | bytes 1048576 | tf_op jit(solution)/shard_map/all_to_all | solution.py:270
  55.3 0.0 copy-done
  55.3 2.6 %parts.1 = (f32[64,96,128]{2,1,0:T(8,128)}, bf16[16,32,128]{2,1,0:T(8,128)(2,1)S(1)}) custom-call(s32[1]{0:T(128)} %bitcast.where, s32[1,8]{1,0:T(1,128)S(1)} %copy-done, f32[32,32,128]{2,1,0:T(8,128)S(1)} %all_to_all.31.vec_ref, bf16[32,160,128]{2,1,0:T(8,128)(2,1)S(1)} %all_to_all.30.recv_ref, ...), custom_call_target="tpu_custom_call", output_to_operand_aliasing={{0}: (4, {})} | custom-call | tf_op jit(solution)/shard_map/parts/pallas_call | solution.py:271
  57.9 0.0 copy-start.1
  57.9 0.0 copy-start.2
  57.9 0.0 reduce-scatter.2.cloned.1.call-update
  58.0 3.6 %all-to-all-start.4 = ((bf16[2,8,64,160]{3,2,1,0:T(8,128)(2,1)}), bf16[2,8,64,160]{3,2,1,0:T(8,128)(2,1)S(1)}, u32[]{:S(2)}, u32[]{:S(2)}) async-start(bf16[2,8,64,160]{3,2,1,0:T(8,128)(2,1)} %get-tuple-element.27), calls=%async_computation.4 | async-start | bytes 1048576 | tf_op jit(solution)/shard_map/all_to_all | solution.py:293
  61.6 0.0 copy-done.1
  61.6 0.0 copy-done.2
  61.7 1.7 %all-to-all-done.4.a_ref = bf16[2,8,64,160]{3,2,1,0:T(8,128)(2,1)S(1)} async-done(((bf16[2,8,64,160]{3,2,1,0:T(8,128)(2,1)}), bf16[2,8,64,160]{3,2,1,0:T(8,128)(2,1)S(1)}, u32[]{:S(2)}, u32[]{:S(2)}) %all-to-all-start.4) | async-done | bytes 327712 | tf_op jit(solution)/shard_map/all_to_all | solution.py:293
  63.3 0.2 broadcast_in_dim.5
  63.5 4.8 %all_to_all.32.w_ref = bf16[2,160,2048]{2,1,0:T(8,128)(2,1)S(1)} all-to-all(bf16[2,160,2048]{2,1,0:T(8,128)(2,1)S(1)} %broadcast_in_dim.5), channel_id=1, replica_groups=mesh['dp'=16,'y'=4,'x'=4,'core'=2] {'core'}, dimensions={0} | all-to-all | bytes 2621440 | tf_op jit(solution)/shard_map/all_to_all | solution.py:293
  68.3 0.2 broadcast_in_dim.4
  68.5 31.9 %all_to_all.33.kv_ref = bf16[16,32,2048]{2,1,0:T(8,128)(2,1)S(1)} all-to-all(bf16[16,32,2048]{2,1,0:T(8,128)(2,1)S(1)} %broadcast_in_dim.4), channel_id=1, replica_groups=mesh['dp'=16,'y'=4,'x'=4,'core'=2] {'y','x'}, dimensions={0} | all-to-all | bytes 4194304 | tf_op jit(solution)/shard_map/all_to_all | solution.py:293
  100.4 3.2 %base.1 = bf16[16,32,320]{2,1,0:T(8,128)(2,1)S(1)} custom-call(bf16[16,32,2048]{2,1,0:T(8,128)(2,1)S(1)} %all_to_all.33.kv_ref, bf16[2,160,2048]{2,1,0:T(8,128)(2,1)S(1)} %all_to_all.32.w_ref, bf16[16,32,128]{2,1,0:T(8,128)(2,1)S(1)} %get-tuple-element.26.low_ref, bf16[2,8,64,160]{3,2,1,0:T(8,128)(2,1)S(1)} %all-to-all-done.4.a_ref), custom_call_target="tpu_custom_call" | custom-call | tf_op jit(solution)/shard_map/base/pallas_call | solution.py:299
  103.7 12.7 %all_to_all.34 = bf16[16,32,320]{2,1,0:T(8,128)(2,1)S(1)} all-to-all(bf16[16,32,320]{2,1,0:T(8,128)(2,1)S(1)} %base.1), channel_id=1, replica_groups=mesh['dp'=16,'y'=4,'x'=4,'core'=2] {'y','x'}, dimensions={0} | all-to-all | bytes 655360 | tf_op jit(solution)/shard_map/all_to_all | solution.py:293
  116.3 0.1 copy.18
  116.5 1.0 reshape.19
  117.5 17.8 %reduce-scatter.2.cloned.1.call-done.sum_hbm = f32[4,96,128]{2,1,0:T(8,128)} async-done(((f32[64,96,128]{2,1,0:T(8,128)}), f32[4,96,128]{2,1,0:T(8,128)}) %reduce-scatter.2.cloned.1.call-update) | async-done | bytes 196624 | tf_op jit(solution)/shard_map/reduce_scatter | solution.py:290
  135.3 1.7 %finish.1 = (f32[4,32,160]{2,1,0:T(8,128)}, f32[4,32,160]{2,1,0:T(8,128)}, f32[4,32,32]{2,1,0:T(8,128)}, f32[4,32,32]{2,1,0:T(8,128)}) custom-call(f32[4,96,128]{2,1,0:T(8,128)} %reduce-scatter.2.cloned.1.call-done.sum_hbm), custom_call_target="tpu_custom_call" | custom-call | tf_op jit(solution)/shard_map/finish/pallas_call | solution.py:311
  (1 shorter events, 0.0 us)
Async XLA Ops:
  7.2 128.2 %reduce-scatter.2.cloned.1.call-start = ((), (), s32[]{:S(2)}) async-start(), calls=%async_computation.7 | async-start | bytes 3342336 | tf_op jit(solution)/shard_map/reduce_scatter | solution.py:290
  38.5 16.8 %copy-start = (s32[1,8]{1,0:T(1,128)S(1)}, s32[1,8]{1,0:T(1,128)}, u32[]{:S(2)}) copy-start(s32[1,8]{1,0:T(1,128)} %tenants.1) | copy-start | bytes 100
  57.9 3.7 %copy-start.1 = (bf16[160,1024]{1,0:T(8,128)(2,1)S(1)}, bf16[160,1024]{1,0:T(8,128)(2,1)}, u32[]{:S(2)}) copy-start(bf16[160,1024]{1,0:T(8,128)(2,1)} %param.15) | copy-start | bytes 983044
  57.9 3.7 %copy-start.2 = (bf16[160,1024]{1,0:T(8,128)(2,1)S(1)}, bf16[160,1024]{1,0:T(8,128)(2,1)}, u32[]{:S(2)}) copy-start(bf16[160,1024]{1,0:T(8,128)(2,1)} %param.14) | copy-start | bytes 983044
  58.0 5.4 %all-to-all-start.4 = ((bf16[2,8,64,160]{3,2,1,0:T(8,128)(2,1)}), bf16[2,8,64,160]{3,2,1,0:T(8,128)(2,1)S(1)}, u32[]{:S(2)}, u32[]{:S(2)}) async-start(bf16[2,8,64,160]{3,2,1,0:T(8,128)(2,1)} %get-tuple-element.27), calls=%async_computation.4 | async-start | bytes 1048576 | tf_op jit(solution)/shard_map/all_to_all | solution.py:293
Sparse Core Ops, SparseCore 0:
  58.1 77.2 reduce-scatter.1

commit v4 on v3

v4 whole, which is shorter than its diff:
```python
import functools

import jax
import jax.numpy as jnp
from jax import lax
from jax.experimental import pallas as pl
from jax.experimental.pallas import tpu as pltpu
from jax.sharding import Mesh, PartitionSpec as P

BLOCK = 128
SCALE = 0.5
F32 = jnp.float32
BF16 = jnp.bfloat16
VMEM = pl.BlockSpec(memory_space=pltpu.VMEM)
SMEM = pl.BlockSpec(memory_space=pltpu.SMEM)
HBM = pl.BlockSpec(memory_space=pltpu.HBM)
PARAMS = pltpu.CompilerParams(vmem_limit_bytes=24 * 1024 * 1024)
LANE = 128


def pack_kernel(
    where, tenants_hbm, counts_hbm, x_hbm, k_hbm, v_hbm, bk_hbm, bv_hbm, ak_hbm, av_hbm, wk_hbm, wv_hbm,
    send_ref, masked_hbm, bundle_hbm,
    tenants, counts, x_ref, k_ref, v_ref, bk_ref, bv_ref, ak, av, up, masked, low, sems, a_sems, out_sems,
):
    n_mp = send_ref.shape[0]
    blocks, rank, feat = ak.shape
    tok, kv_width = k_ref.shape
    cols = kv_width // n_mp
    quad = n_mp // blocks
    pairs = (
        (tenants_hbm, tenants), (counts_hbm, counts), (x_hbm, x_ref), (k_hbm, k_ref),
        (v_hbm, v_ref), (bk_hbm, bk_ref), (bv_hbm, bv_ref),
    )
    loads = [pltpu.make_async_copy(src, dst, sems.at[i]) for i, (src, dst) in enumerate(pairs)]
    for c in loads:
        c.start()
    feat_rows = pl.ds(0, feat), pl.ds(feat, feat)
    stores = [
        pltpu.make_async_copy(wk_hbm, bundle_hbm.at[feat_rows[0]], out_sems.at[0]),
        pltpu.make_async_copy(wv_hbm, bundle_hbm.at[feat_rows[1]], out_sems.at[1]),
        pltpu.make_async_copy(masked, masked_hbm, out_sems.at[2]),
        pltpu.make_async_copy(low, bundle_hbm.at[pl.ds(2 * feat, low.shape[0])], out_sems.at[3]),
    ]
    stores[0].start()
    stores[1].start()
    loads[0].wait()
    copies = []
    for b in range(blocks):
        t = tenants[0, b]
        copies.append(pltpu.make_async_copy(ak_hbm.at[t], ak.at[b], a_sems.at[0, b]))
        copies.append(pltpu.make_async_copy(av_hbm.at[t], av.at[b], a_sems.at[1, b]))
    for c in copies:
        c.start()
    for c in loads[1:]:
        c.wait()
    me = where[0]
    count = counts[0, me // quad]
    row = lax.broadcasted_iota(jnp.int32, (tok, 1), 0) + (me % quad) * tok
    live = row < count
    mk = jnp.where(live, k_ref[...].astype(F32), 0.0).astype(BF16)
    mv = jnp.where(live, v_ref[...].astype(F32), 0.0).astype(BF16)
    masked[:, :kv_width] = mk
    masked[:, kv_width:] = mv
    stores[2].start()
    x = x_ref[...]
    for j in range(n_mp):
        send_ref[j, 96:128, :] = x[:, feat * j : feat * j + LANE]
        last = x[:, feat * j + LANE : feat * (j + 1)]
        send_ref[j, 128:160, :] = jnp.concatenate(
            [last, mk[:, cols * j : cols * (j + 1)], last, mv[:, cols * j : cols * (j + 1)]], axis=1
        )
    which = lax.broadcasted_iota(jnp.int32, (blocks, bk_ref.shape[2]), 0)
    tenant = jnp.zeros_like(which)
    for b in range(blocks):
        tenant = jnp.where(which == b, tenants[0, b], tenant)
    hot = lax.broadcasted_iota(jnp.int32, tenant.shape, 1) == tenant
    hot = jnp.where(hot, 1.0, 0.0).astype(BF16)
    for ref, at in ((bk_ref, 32), (bv_ref, 96)):
        flat = ref[...].reshape(rank * cols, ref.shape[2])
        got = lax.dot_general(hot, flat, (((1,), (1,)), ((), ())), preferred_element_type=F32)
        for r in range(rank):
            up[:, r, at : at + cols] = got[:, cols * r : cols * (r + 1)]
    for c in copies:
        c.wait()
    for b in range(blocks):
        at = slice(LANE * b, LANE * (b + 1))
        for i, ref in enumerate((ak, av)):
            low[rank * i : rank * (i + 1), at] = ref[b][:, :LANE]
            low[rank * (2 + i) : rank * (3 + i), LANE * b : LANE * b + feat - LANE] = ref[b][:, LANE:]
    stores[3].start()
    for b in range(blocks):
        a0 = ak[b]
        a1 = av[b]
        main = jnp.concatenate([a0[:, :LANE], a1[:, :LANE]], axis=0)
        near = up[b].astype(BF16)
        tail = jnp.concatenate(
            [a0[:, LANE:], near[:, 32:64], a1[:, LANE:], near[:, 96:128]], axis=1
        )
        for q in range(quad):
            send_ref[quad * b + q, 0:64, :] = main
            send_ref[quad * b + q, 64:96, :] = tail
    for c in stores:
        c.wait()


def lane_mask(rows, slot):
    lane = lax.broadcasted_iota(jnp.int32, (rows, LANE), 1)
    return (lane >= 32 * slot) & (lane < 32 * slot + 32)


def vector_kernel(send_ref, recv_ref, out_ref):
    n_mp = send_ref.shape[0]
    masks = [lane_mask(32, s) for s in (0, 2, 1, 3)]
    total = jnp.zeros((32, LANE), F32)
    zero = jnp.zeros((64, LANE), BF16)
    for m in range(n_mp):
        lhs = jnp.concatenate([send_ref[m, 96:128, :], send_ref[m, 128:160, :]], axis=1)
        main = jnp.concatenate([recv_ref[m, 0:64, :], zero], axis=0)
        tail = recv_ref[m, 64:96, :]
        tails = jnp.concatenate([jnp.where(k, tail, jnp.zeros_like(tail)) for k in masks], axis=0)
        rhs = jnp.concatenate([main, tails], axis=1)
        total += lax.dot_general(lhs, rhs, (((1,), (1,)), ((), ())), preferred_element_type=F32)
    for m in range(n_mp):
        out_ref[m] = total


def split(x):
    hi = x.astype(BF16)
    return hi, (x - hi.astype(F32)).astype(BF16)


def first_blocks(tenants, blocks):
    first = []
    for b in range(blocks):
        f = jnp.int32(b)
        for c in range(b - 1, -1, -1):
            f = jnp.where(tenants[0, c] == tenants[0, b], c, f)
        first.append(f)
    return first


PART = 96
HALF = 48


def parts_kernel(where, tenants, vec_ref, recv_ref, top_ref, bottom_ref, low_ref):
    blocks = vec_ref.shape[0] // 4
    m0, m1, m2, m3 = [lane_mask(32, s) for s in range(4)]
    first = first_blocks(tenants, blocks)
    top_ref[...] = jnp.zeros_like(top_ref)
    bottom_ref[...] = jnp.zeros_like(bottom_ref)
    for b in range(blocks):
        vec = vec_ref[4 * b : 4 * b + 4].reshape(BLOCK, LANE) * SCALE
        lhs = jnp.concatenate(split(vec), axis=0)
        near = recv_ref[4 * b : 4 * b + 4, 96:128, :].reshape(BLOCK, LANE)
        far = recv_ref[4 * b : 4 * b + 4, 128:160, :].reshape(BLOCK, LANE)
        rhs = jnp.concatenate([near, far], axis=1)
        rhs = jnp.concatenate([rhs, rhs], axis=0)
        p = lax.dot_general(lhs, rhs, (((0,), (0,)), ((), ())), preferred_element_type=F32)
        q = p[:, LANE:]
        tail = jnp.where(m0, q[64:96], jnp.where(m1, q[0:32], jnp.where(m2, q[96:128], q[32:64])))
        at = pl.multiple_of(first[b] * HALF, 8)
        top_ref[pl.ds(at, HALF), :] += p[64:112, :LANE]
        bottom_ref[pl.ds(at, HALF), :] += jnp.concatenate([p[112:128, :LANE], tail], axis=0)
    row = lax.broadcasted_iota(jnp.int32, (blocks, LANE), 0)
    ids = jnp.full((blocks, LANE), -1, jnp.int32)
    for b in range(blocks):
        ids = jnp.where((row == b) & (first[b] == b), tenants[0, b], ids)
    top_ref[blocks * HALF :, :] = ids.astype(F32)
    bottom_ref[blocks * HALF :, :] = ids.astype(F32)
    core = where[0] % 2
    for i in range(low_ref.shape[0]):
        back = vec_ref[2 * i + core][:, 64:] * SCALE
        low_ref[i] = jnp.concatenate(split(back), axis=1)


def kept(tenant, parity):
    return (tenant >= 0) & ((tenant // 4) % 2 == parity), (tenant // 8) * 4 + tenant % 4


def half_of(out_hbm, mine, place, h):
    return out_hbm.at[jnp.where(mine, place, 0), pl.ds(h * HALF, HALF)]


def own_kernel(plane, tenants, top_ref, bottom_ref, out_hbm, zeros, fill_sems, sems):
    blocks = sems.shape[1]
    zeros[...] = jnp.zeros_like(zeros)
    chunk = zeros.shape[0]
    fills = [
        pltpu.make_async_copy(zeros, out_hbm.at[pl.ds(i * chunk, chunk)], fill_sems.at[i])
        for i in range(out_hbm.shape[0] // chunk)
    ]
    for c in fills:
        c.start()
    first = first_blocks(tenants, blocks)
    for c in fills:
        c.wait()
    todo = []
    for b in range(blocks):
        mine, place = kept(tenants[0, b], plane[0] % 2)
        mine = mine & (first[b] == b)
        for h, ref in enumerate((top_ref, bottom_ref)):
            src = ref.at[pl.ds(b * HALF, HALF)]
            dst = half_of(out_hbm, mine, place, h)
            todo.append((mine, pltpu.make_async_copy(src, dst, sems.at[h, b])))
    for mine, copy in todo:
        pl.when(mine)(copy.start)
    for mine, copy in todo:
        pl.when(mine)(copy.wait)


def merge_kernel(plane, tenants, top_ref, bottom_ref, got_top, got_bottom, own_hbm, out_hbm, buf, sems):
    blocks = sems.shape[1]
    todo = []
    for h, (ref, got) in enumerate(((top_ref, got_top), (bottom_ref, got_bottom))):
        for b in range(blocks):
            tenant = jnp.max(got[blocks * HALF + b : blocks * HALF + b + 1, :]).astype(jnp.int32)
            mine, place = kept(tenant, plane[0] % 2)
            same = jnp.int32(-1)
            for c in range(blocks - 1, -1, -1):
                same = jnp.where(tenants[0, c] == tenant, c, same)
            at = pl.multiple_of(jnp.maximum(same, 0) * HALF, 8)
            here = jnp.where(same >= 0, 1.0, 0.0)
            buf[h, b] = got[b * HALF : (b + 1) * HALF, :] + ref[pl.ds(at, HALF), :] * here
            copy = pltpu.make_async_copy(buf.at[h, b], half_of(out_hbm, mine, place, h), sems.at[h, b])
            pl.when(mine)(copy.start)
            todo.append((mine, copy))
    for mine, copy in todo:
        pl.when(mine)(copy.wait)


def base_kernel(where, kv_ref, near_ref, far_ref, low_ref, out_ref, w):
    width = near_ref.shape[1]
    blocks = width // LANE
    feat = out_ref.shape[2] // 2
    per = kv_ref.shape[0] // blocks
    rank = (near_ref.shape[0] - 2 * feat) // 4
    core = where[0] % 2
    for c, ref in enumerate((near_ref, far_ref)):
        at = pl.multiple_of(jnp.where(core == 0, c, 1 - c) * feat, 16)
        w[pl.ds(at, feat), :width] = ref[0:feat, :]
        w[pl.ds(at, feat), width:] = ref[feat : 2 * feat, :]
    step = 4
    for s in range(0, blocks, step):
        rows = kv_ref[per * s : per * (s + step)].reshape(-1, kv_ref.shape[-1])
        res = lax.dot_general(rows, w[...], (((1,), (1,)), ((), ())), preferred_element_type=F32)
        size = res.shape[0] // step
        for i in range(step):
            b = s + i
            low = low_ref[per * b : per * (b + 1)].reshape(-1, LANE)
            add = []
            for ref in (near_ref, far_ref):
                main = ref[2 * feat : 2 * feat + 2 * rank, LANE * b : LANE * (b + 1)]
                rest = ref[2 * feat + 2 * rank :, LANE * b : LANE * b + feat - LANE]
                a = jnp.concatenate([main, rest], axis=1)
                add.append(jnp.dot(low, jnp.concatenate([a, a], axis=0), preferred_element_type=F32))
            swapped = jnp.concatenate(add[::-1], axis=1)
            add = jnp.where(core == 0, jnp.concatenate(add, axis=1), swapped)
            total = res[size * i : size * (i + 1)] + add
            out_ref[per * b : per * (b + 1)] = total.astype(BF16).reshape(per, -1, 2 * feat)


def finish_kernel(sum_hbm, ak_ref, av_ref, bk_ref, bv_ref, sum_ref, sem):
    load = pltpu.make_async_copy(sum_hbm, sum_ref, sem)
    load.start()
    load.wait()
    for t in range(sum_ref.shape[0]):
        tail = sum_ref[t, 64:96, :]
        ak_ref[t, :, :LANE] = sum_ref[t, 0:32, :]
        ak_ref[t, :, LANE:] = tail[:, 0:32]
        av_ref[t, :, :LANE] = sum_ref[t, 32:64, :]
        av_ref[t, :, LANE:] = tail[:, 64:96]
        bk_ref[t] = tail[:, 32:64]
        bv_ref[t] = tail[:, 96:128]


def shards(x, kg, vg, wk, wv, ak, av, bk, bv, tenant_of_block, live_token_count):
    mp = ("y", "x", "core")
    n_mp = lax.axis_size(mp)
    tok, width = x.shape
    blocks = tenant_of_block.shape[1]
    feat = wk.shape[0]
    kv_width = kg.shape[1]
    tenants, rank = ak.shape[:2]
    me = lax.axis_index(mp).astype(jnp.int32).reshape(1)
    cols = bk.shape[2]
    hbm = lambda a: pltpu.with_memory_space_constraint(a, pltpu.HBM)
    bundle_rows = 2 * feat + 4 * rank
    send, masked, bundle = pl.pallas_call(
        pack_kernel,
        out_shape=(
            jax.ShapeDtypeStruct((n_mp, 160, LANE), BF16),
            jax.ShapeDtypeStruct((tok, 2 * kv_width), BF16),
            jax.ShapeDtypeStruct((bundle_rows, kv_width), BF16),
        ),
        in_specs=[SMEM] + [HBM] * 11,
        out_specs=(VMEM, HBM, HBM),
        scratch_shapes=[
            pltpu.SMEM((1, blocks), jnp.int32),
            pltpu.SMEM((1, blocks), jnp.int32),
            pltpu.VMEM((tok, width), BF16),
            pltpu.VMEM((tok, kv_width), BF16),
            pltpu.VMEM((tok, kv_width), BF16),
            pltpu.VMEM((rank, cols, tenants), BF16),
            pltpu.VMEM((rank, cols, tenants), BF16),
            pltpu.VMEM((blocks, rank, feat), BF16),
            pltpu.VMEM((blocks, rank, feat), BF16),
            pltpu.VMEM((blocks, rank, LANE), F32),
            pltpu.VMEM((tok, 2 * kv_width), BF16),
            pltpu.VMEM((4 * rank, kv_width), BF16),
            pltpu.SemaphoreType.DMA((7,)),
            pltpu.SemaphoreType.DMA((2, blocks)),
            pltpu.SemaphoreType.DMA((4,)),
        ],
        compiler_params=PARAMS,
        name="pack",
    )(
        me, hbm(tenant_of_block), hbm(live_token_count), hbm(x), hbm(kg), hbm(vg),
        hbm(bk.transpose(1, 2, 0)), hbm(bv.transpose(1, 2, 0)), hbm(ak), hbm(av), hbm(wk), hbm(wv),
    )
    recv = lax.all_to_all(send, mp, split_axis=0, concat_axis=0, tiled=True)
    vec_send = pl.pallas_call(
        vector_kernel,
        out_shape=jax.ShapeDtypeStruct((n_mp, tok, LANE), F32),
        in_specs=[VMEM, VMEM],
        out_specs=VMEM,
        compiler_params=PARAMS,
        name="vectors",
    )(send, recv)
    vec = lax.all_to_all(vec_send, mp, split_axis=0, concat_axis=0, tiled=True)
    group = jax.ShapeDtypeStruct((blocks * HALF + blocks, LANE), F32)
    top, bottom, low = pl.pallas_call(
        parts_kernel,
        out_shape=(group, group, jax.ShapeDtypeStruct((n_mp // 2, tok, LANE), BF16)),
        in_specs=[SMEM, SMEM, VMEM, VMEM],
        out_specs=(VMEM, VMEM, VMEM),
        compiler_params=PARAMS,
        name="parts",
    )(me, tenant_of_block, vec, recv)

    dp = ("zh", "zl")
    n_dp = lax.axis_size(dp)
    pairs = [(z, z ^ 1) for z in range(n_dp)]
    others = [(z, (z + (1 if z % 2 else -1)) % n_dp) for z in range(n_dp)]
    got_top = lax.ppermute(top, dp, pairs)
    got_bottom = lax.ppermute(bottom, dp, others)
    plane = lax.axis_index("zl").astype(jnp.int32).reshape(1)
    half = jax.ShapeDtypeStruct((tenants // 2, PART, LANE), F32)
    own = pl.pallas_call(
        own_kernel,
        out_shape=half,
        in_specs=[SMEM, SMEM, VMEM, VMEM],
        out_specs=HBM,
        scratch_shapes=[
            pltpu.VMEM((tenants // 16, PART, LANE), F32),
            pltpu.SemaphoreType.DMA((8,)),
            pltpu.SemaphoreType.DMA((2, blocks)),
        ],
        compiler_params=PARAMS,
        name="own",
    )(plane, tenant_of_block, top, bottom)
    got_top, bundle = lax.optimization_barrier((got_top, bundle))
    far = lax.ppermute(bundle, "core", [(0, 1), (1, 0)])
    sums = pl.pallas_call(
        merge_kernel,
        out_shape=half,
        in_specs=[SMEM, SMEM, VMEM, VMEM, VMEM, VMEM, HBM],
        out_specs=HBM,
        scratch_shapes=[
            pltpu.VMEM((2, blocks, HALF, LANE), F32),
            pltpu.SemaphoreType.DMA((2, blocks)),
        ],
        input_output_aliases={6: 0},
        compiler_params=PARAMS,
        name="merge",
    )(plane, tenant_of_block, top, bottom, got_top, got_bottom, own)

    sums, masked = lax.optimization_barrier((sums, masked))
    sums = lax.psum_scatter(sums, "zh", scatter_dimension=0, tiled=True)

    def swap(a, axes):
        return lax.all_to_all(a, axes, split_axis=0, concat_axis=0, tiled=True)

    kv = swap(jnp.broadcast_to(masked[None], (n_mp // 2, *masked.shape)), ("y", "x"))
    grad = pl.pallas_call(
        base_kernel,
        out_shape=jax.ShapeDtypeStruct((n_mp // 2, tok, 2 * feat), BF16),
        in_specs=[SMEM] + [VMEM] * 4,
        out_specs=VMEM,
        scratch_shapes=[pltpu.VMEM((2 * feat, 2 * kv_width), BF16)],
        compiler_params=PARAMS,
        name="base",
    )(me, kv, bundle, far, low)
    grad = swap(grad, ("y", "x"))
    grad_in = grad.transpose(1, 0, 2).reshape(tok, width)
    sums, grad_in = lax.optimization_barrier((sums, grad_in))

    owned = tenants // lax.axis_size(("zh", "zl"))
    grads = pl.pallas_call(
        finish_kernel,
        out_shape=(
            jax.ShapeDtypeStruct((owned, rank, feat), F32),
            jax.ShapeDtypeStruct((owned, rank, feat), F32),
            jax.ShapeDtypeStruct((owned, rank, bk.shape[2]), F32),
            jax.ShapeDtypeStruct((owned, rank, bk.shape[2]), F32),
        ),
        in_specs=[HBM],
        out_specs=(VMEM, VMEM, VMEM, VMEM),
        scratch_shapes=[pltpu.VMEM((owned, PART, LANE), F32), pltpu.SemaphoreType.DMA],
        compiler_params=PARAMS,
        name="finish",
    )(hbm(sums))
    return (grad_in, *grads)


def solution(mesh):
    n_dp, n_mp = mesh.devices.shape
    fine = Mesh(
        mesh.devices.reshape(n_dp // 2, 2, 4, n_mp // 8, 2), ("zh", "zl", "y", "x", "core")
    )
    dp, mp = ("zh", "zl"), ("y", "x", "core")
    rows = P((*dp, *mp), None)
    in_specs = (
        rows, rows, rows,
        P(mp, None), P(mp, None),
        P(None, None, mp), P(None, None, mp), P(None, None, mp), P(None, None, mp),
        P(dp, None), P(dp, None),
    )
    grads = P(dp, None, mp)
    return jax.shard_map(
        shards, mesh=fine, in_specs=in_specs, out_specs=(rows, grads, grads, grads, grads),
        check_vma=False,
    )
```

time: 144 us -> 139 us (0.965)
  the two profiles are of different devices: /device:TPU:2 before, /device:TPU:42 now
where the time goes in v4:
time: 139 us; the launch traced here: 138 us
  blocking collectives  54.5 us (39%)
  waiting for transfers between devices  36.7 us (26%)
  starting transfers between devices  15.7 us (11%)
  between operations  14.2 us (10%)
  Pallas kernels  12.2 us (9%)
  local copies, waits for them, and re-layouts  4.88 us (4%)
    all_to_all x1, blocking collectives, shards(): recv = lax.all_to_all(send, mp, split_axis=0, concat_axis=0, tiled=True)  25 us
    all_to_all x1, waiting for transfers between devices, swap(): return lax.all_to_all(a, axes, split_axis=0, concat_axis=0, tiled=True)  21.4 us
    all_to_all x1, blocking collectives, shards(): vec = lax.all_to_all(vec_send, mp, split_axis=0, concat_axis=0, tiled=True)  14.8 us
    all_to_all x1, blocking collectives, swap(): return lax.all_to_all(a, axes, split_axis=0, concat_axis=0, tiled=True)  14.7 us
    reduce_scatter x1, waiting for transfers between devices, shards(): sums = lax.psum_scatter(sums, 'zh', scatter_dimension=0, tiled=True)  9.9 us
    all_to_all x1, starting transfers between devices, swap(): return lax.all_to_all(a, axes, split_axis=0, concat_axis=0, tiled=True)  6.15 us
    ppermute x1, starting transfers between devices, shards(): got_bottom = lax.ppermute(bottom, dp, others)  4.4 us
    ppermute x1, starting transfers between devices, shards(): got_top = lax.ppermute(top, dp, pairs)  3.26 us
  transfers between devices with their start and end apart: 5, of which 4 were waited for; matrix products, arithmetic and copies ran while one was open for 2% of the time, Pallas kernels for 3%

profile of v4, /device:TPU:42, one launch (start us, length us, event | category | flops | bytes accessed | tf_op | source)
XLA Modules:
  0.0 138.2 jit_solution(16381619862036489200)
XLA Ops:
  7.2 0.0 reduce-scatter.2.cloned.1.call-start
  7.2 2.8 %pack.1 = (bf16[32,160,128]{2,1,0:T(8,128)(2,1)S(1)}, bf16[32,2048]{1,0:T(8,128)(2,1)S(1)}, bf16[448,1024]{1,0:T(8,128)(2,1)S(1)}) custom-call(s32[1]{0:T(128)} %bitcast.1.where, s32[1,8]{1,0:T(1,128)} %tenants.5, s32[1,8]{1,0:T(1,128)} %counts_hbm.1, bf16[32,5120]{1,0:T(8,128)(2,1)} %x_hbm.1, bf16[32,1024]{1,0:T(8,128)(2,1)} %k_hbm.1, ...), custom_call_target="tpu_custom_call" | custom-call | tf_op jit(solution)/shard_map/pack/pallas_call | solution.py:290
  10.0 25.0 %all_to_all.20.recv_ref = bf16[32,160,128]{2,1,0:T(8,128)(2,1)S(1)} all-to-all(bf16[32,160,128]{2,1,0:T(8,128)(2,1)S(1)} %get-tuple-element.21.send_ref), channel_id=1, replica_groups=mesh['zh'=8,'zl'=2,'y'=4,'x'=4,'core'=2] {'y','x','core'}, dimensions={0} | all-to-all | bytes 2621440 | tf_op jit(solution)/shard_map/all_to_all | solution.py:322
  35.0 0.0 copy-start.2
  35.0 0.8 vectors.1
  35.8 14.8 %all_to_all.21.vec_ref = f32[32,32,128]{2,1,0:T(8,128)S(1)} all-to-all(f32[32,32,128]{2,1,0:T(8,128)S(1)} %vectors.1), channel_id=1, replica_groups=mesh['zh'=8,'zl'=2,'y'=4,'x'=4,'core'=2] {'y','x','core'}, dimensions={0} | all-to-all | bytes 1048576 | tf_op jit(solution)/shard_map/all_to_all | solution.py:331
  50.6 0.0 copy-done.2
  50.6 0.9 parts.1
  51.5 3.3 %collective-permute-start = (f32[392,128]{1,0:T(8,128)S(1)}, f32[392,128]{1,0:T(8,128)S(1)}, u32[]{:S(2)}, u32[]{:S(2)}) collective-permute-start(f32[392,128]{1,0:T(8,128)S(1)} %get-tuple-element.22.top_ref), channel_id=1, source_target_pairs={{0,32},{32,0},{64,96},{96,64},{128,160},{160,128},{192,224},{224,1... | collective-permute-start | bytes 602120 | tf_op jit(solution)/shard_map/ppermute | solution.py:346
  54.8 4.4 %collective-permute-start.1 = (f32[392,128]{1,0:T(8,128)S(1)}, f32[392,128]{1,0:T(8,128)S(1)}, u32[]{:S(2)}, u32[]{:S(2)}) collective-permute-start(f32[392,128]{1,0:T(8,128)S(1)} %get-tuple-element.23.bottom_ref), channel_id=1, source_target_pairs={{0,480},{32,64},{64,32},{96,128},{128,96},{160,192},{192,160},{224... | collective-permute-start | bytes 602120 | tf_op jit(solution)/shard_map/ppermute | solution.py:347
  59.2 2.6 %own.1.own_hbm = f32[32,96,128]{2,1,0:T(8,128)} custom-call(s32[1]{0:T(128)} %bitcast.plane, s32[1,8]{1,0:T(1,128)S(1)} %copy-done.2, f32[392,128]{1,0:T(8,128)S(1)} %get-tuple-element.22.top_ref, f32[392,128]{1,0:T(8,128)S(1)} %get-tuple-element.23.bottom_ref), custom_call_target="tpu_custom_call" | custom-call | tf_op jit(solution)/shard_map/own/pallas_call | solution.py:350
  61.8 0.0 collective-permute-done.got_top
  61.8 2.9 %collective-permute-done.1.got_bottom = f32[392,128]{1,0:T(8,128)S(1)} collective-permute-done((f32[392,128]{1,0:T(8,128)S(1)}, f32[392,128]{1,0:T(8,128)S(1)}, u32[]{:S(2)}, u32[]{:S(2)}) %collective-permute-start.1) | collective-permute-done | bytes 200736 | tf_op jit(solution)/shard_map/ppermute | solution.py:347
  64.7 1.8 %merge.1 = f32[32,96,128]{2,1,0:T(8,128)} custom-call(s32[1]{0:T(128)} %bitcast.plane, s32[1,8]{1,0:T(1,128)S(1)} %copy-done.2, f32[392,128]{1,0:T(8,128)S(1)} %get-tuple-element.22.top_ref, f32[392,128]{1,0:T(8,128)S(1)} %get-tuple-element.23.bottom_ref, f32[392,128]{1,0:T(8,128)S(1)} %collective-permute-done.got_top, ...), custom_call_target="tpu_custom_call", output_to_operand_aliasing={{}: (6, {})} | custom-call | tf_op jit(solution)/shard_map/merge/pallas_call | solution.py:365
  66.5 0.0 reduce-scatter.2.cloned.1.call-update
  66.6 1.6 %broadcast_in_dim.2 = bf16[16,32,2048]{2,1,0:T(8,128)(2,1)} broadcast(bf16[32,2048]{1,0:T(8,128)(2,1)S(1)} %get-tuple-element.28), dimensions={1,2} | broadcast | bytes 2228224 | tf_op jit(solution)/shard_map/broadcast_in_dim | solution.py:385
  68.2 6.1 %all-to-all-start.2 = ((bf16[16,32,2048]{2,1,0:T(8,128)(2,1)}), bf16[16,32,2048]{2,1,0:T(8,128)(2,1)S(1)}, u32[]{:S(2)}, u32[]{:S(2)}) async-start(bf16[16,32,2048]{2,1,0:T(8,128)(2,1)} %broadcast_in_dim.2), calls=%async_computation.3 | async-start | bytes 4194304 | tf_op jit(solution)/shard_map/all_to_all | solution.py:383
  74.3 1.9 %collective-permute-start.2 = (bf16[448,1024]{1,0:T(8,128)(2,1)S(1)}, bf16[448,1024]{1,0:T(8,128)(2,1)S(1)}, u32[]{:S(2)}, u32[]{:S(2)}) collective-permute-start(bf16[448,1024]{1,0:T(8,128)(2,1)S(1)} %get-tuple-element.29.near_ref), channel_id=1, source_target_pairs={{0,1},{1,0},{2,3},{3,2},{4,5},{5,4},{6,7},{7,6},{8,9},{9,8},{10,11... | collective-permute-start | bytes 2752520 | tf_op jit(solution)/shard_map/ppermute | solution.py:364
  76.2 2.4 %collective-permute-done.2.far_ref = bf16[448,1024]{1,0:T(8,128)(2,1)S(1)} collective-permute-done((bf16[448,1024]{1,0:T(8,128)(2,1)S(1)}, bf16[448,1024]{1,0:T(8,128)(2,1)S(1)}, u32[]{:S(2)}, u32[]{:S(2)}) %collective-permute-start.2) | collective-permute-done | bytes 917536 | tf_op jit(solution)/shard_map/ppermute | solution.py:364
  78.7 0.0 copy-start
  78.7 0.9 copy-done
  79.6 21.4 %all-to-all-done.2.kv_ref = bf16[16,32,2048]{2,1,0:T(8,128)(2,1)S(1)} async-done(((bf16[16,32,2048]{2,1,0:T(8,128)(2,1)}), bf16[16,32,2048]{2,1,0:T(8,128)(2,1)S(1)}, u32[]{:S(2)}, u32[]{:S(2)}) %all-to-all-start.2) | async-done | bytes 2097184 | tf_op jit(solution)/shard_map/all_to_all | solution.py:383
  101.0 0.0 copy-start.1
  101.0 1.2 copy-done.1
  102.2 1.6 %base.1 = bf16[16,32,320]{2,1,0:T(8,128)(2,1)S(1)} custom-call(s32[1]{0:T(128)} %bitcast.1.where, bf16[16,32,2048]{2,1,0:T(8,128)(2,1)S(1)} %all-to-all-done.2.kv_ref, bf16[448,1024]{1,0:T(8,128)(2,1)S(1)} %get-tuple-element.29.near_ref, bf16[448,1024]{1,0:T(8,128)(2,1)S(1)} %copy-done.1, bf16[16,32,128]{2,1,0:T(8,128)(2,1)S(1)} %get-tuple-element.30.low_ref), custom_call_target="tpu_custom_call" | custom-call | tf_op jit(solution)/shard_map/base/pallas_call | solution.py:386
  103.8 14.7 %all_to_all.22 = bf16[16,32,320]{2,1,0:T(8,128)(2,1)S(1)} all-to-all(bf16[16,32,320]{2,1,0:T(8,128)(2,1)S(1)} %base.1), channel_id=1, replica_groups=mesh['zh'=8,'zl'=2,'y'=4,'x'=4,'core'=2] {'y','x'}, dimensions={0} | all-to-all | bytes 655360 | tf_op jit(solution)/shard_map/all_to_all | solution.py:383
  118.6 0.1 copy.17
  118.7 1.0 reshape.22
  119.7 9.9 %reduce-scatter.2.cloned.1.call-done.sum_hbm = f32[4,96,128]{2,1,0:T(8,128)} async-done(((f32[32,96,128]{2,1,0:T(8,128)}), f32[4,96,128]{2,1,0:T(8,128)}) %reduce-scatter.2.cloned.1.call-update) | async-done | bytes 196624 | tf_op jit(solution)/shard_map/reduce_scatter | solution.py:380
  129.6 1.7 %finish.1 = (f32[4,32,160]{2,1,0:T(8,128)}, f32[4,32,160]{2,1,0:T(8,128)}, f32[4,32,32]{2,1,0:T(8,128)}, f32[4,32,32]{2,1,0:T(8,128)}) custom-call(f32[4,96,128]{2,1,0:T(8,128)} %reduce-scatter.2.cloned.1.call-done.sum_hbm), custom_call_target="tpu_custom_call" | custom-call | tf_op jit(solution)/shard_map/finish/pallas_call | solution.py:400
Async XLA Ops:
  7.2 122.5 %reduce-scatter.2.cloned.1.call-start = ((), (), s32[]{:S(2)}) async-start(), calls=%async_computation.5 | async-start | bytes 1769472 | tf_op jit(solution)/shard_map/reduce_scatter | solution.py:380
  35.0 15.6 %copy-start.2 = (s32[1,8]{1,0:T(1,128)S(1)}, s32[1,8]{1,0:T(1,128)}, u32[]{:S(2)}) copy-start(s32[1,8]{1,0:T(1,128)} %tenants.5) | copy-start | bytes 100
  51.5 10.3 %collective-permute-start = (f32[392,128]{1,0:T(8,128)S(1)}, f32[392,128]{1,0:T(8,128)S(1)}, u32[]{:S(2)}, u32[]{:S(2)}) collective-permute-start(f32[392,128]{1,0:T(8,128)S(1)} %get-tuple-element.22.top_ref), channel_id=1, source_target_pairs={{0,32},{32,0},{64,96},{96,64},{128,160},{160,128},{192,224},{224,1... | collective-permute-start | bytes 602120 | tf_op jit(solution)/shard_map/ppermute | solution.py:346
  54.8 9.9 %collective-permute-start.1 = (f32[392,128]{1,0:T(8,128)S(1)}, f32[392,128]{1,0:T(8,128)S(1)}, u32[]{:S(2)}, u32[]{:S(2)}) collective-permute-start(f32[392,128]{1,0:T(8,128)S(1)} %get-tuple-element.23.bottom_ref), channel_id=1, source_target_pairs={{0,480},{32,64},{64,32},{96,128},{128,96},{160,192},{192,160},{224... | collective-permute-start | bytes 602120 | tf_op jit(solution)/shard_map/ppermute | solution.py:347
  68.2 32.9 %all-to-all-start.2 = ((bf16[16,32,2048]{2,1,0:T(8,128)(2,1)}), bf16[16,32,2048]{2,1,0:T(8,128)(2,1)S(1)}, u32[]{:S(2)}, u32[]{:S(2)}) async-start(bf16[16,32,2048]{2,1,0:T(8,128)(2,1)} %broadcast_in_dim.2), calls=%async_computation.3 | async-start | bytes 4194304 | tf_op jit(solution)/shard_map/all_to_all | solution.py:383
  74.3 4.4 %collective-permute-start.2 = (bf16[448,1024]{1,0:T(8,128)(2,1)S(1)}, bf16[448,1024]{1,0:T(8,128)(2,1)S(1)}, u32[]{:S(2)}, u32[]{:S(2)}) collective-permute-start(bf16[448,1024]{1,0:T(8,128)(2,1)S(1)} %get-tuple-element.29.near_ref), channel_id=1, source_target_pairs={{0,1},{1,0},{2,3},{3,2},{4,5},{5,4},{6,7},{7,6},{8,9},{9,8},{10,11... | collective-permute-start | bytes 2752520 | tf_op jit(solution)/shard_map/ppermute | solution.py:364
  78.7 0.9 copy-start
  101.0 1.2 copy-start.1
Sparse Core Ops, SparseCore 0:
  66.7 62.9 reduce-scatter.1

commit v5 on v4

--- a/solution.py
+++ b/solution.py
@@ -140,8 +140,8 @@
     return first
 
 
-PART = 96
-HALF = 48
+PIECES = (64, 32)
+PART = sum(PIECES)
 
 
 def parts_kernel(where, tenants, vec_ref, recv_ref, top_ref, bottom_ref, low_ref):
@@ -160,15 +160,14 @@
         p = lax.dot_general(lhs, rhs, (((0,), (0,)), ((), ())), preferred_element_type=F32)
         q = p[:, LANE:]
         tail = jnp.where(m0, q[64:96], jnp.where(m1, q[0:32], jnp.where(m2, q[96:128], q[32:64])))
-        at = pl.multiple_of(first[b] * HALF, 8)
-        top_ref[pl.ds(at, HALF), :] += p[64:112, :LANE]
-        bottom_ref[pl.ds(at, HALF), :] += jnp.concatenate([p[112:128, :LANE], tail], axis=0)
+        top_ref[pl.ds(pl.multiple_of(first[b] * 64, 8), 64), :] += p[64:128, :LANE]
+        bottom_ref[pl.ds(pl.multiple_of(first[b] * 32, 8), 32), :] += tail
     row = lax.broadcasted_iota(jnp.int32, (blocks, LANE), 0)
     ids = jnp.full((blocks, LANE), -1, jnp.int32)
     for b in range(blocks):
         ids = jnp.where((row == b) & (first[b] == b), tenants[0, b], ids)
-    top_ref[blocks * HALF :, :] = ids.astype(F32)
-    bottom_ref[blocks * HALF :, :] = ids.astype(F32)
+    top_ref[blocks * 64 :, :] = ids.astype(F32)
+    bottom_ref[blocks * 32 :, :] = ids.astype(F32)
     core = where[0] % 2
     for i in range(low_ref.shape[0]):
         back = vec_ref[2 * i + core][:, 64:] * SCALE
@@ -179,8 +178,8 @@
     return (tenant >= 0) & ((tenant // 4) % 2 == parity), (tenant // 8) * 4 + tenant % 4
 
 
-def half_of(out_hbm, mine, place, h):
-    return out_hbm.at[jnp.where(mine, place, 0), pl.ds(h * HALF, HALF)]
+def piece_of(out_hbm, mine, place, h):
+    return out_hbm.at[jnp.where(mine, place, 0), pl.ds(sum(PIECES[:h]), PIECES[h])]
 
 
 def own_kernel(plane, tenants, top_ref, bottom_ref, out_hbm, zeros, fill_sems, sems):
@@ -201,8 +200,8 @@
         mine, place = kept(tenants[0, b], plane[0] % 2)
         mine = mine & (first[b] == b)
         for h, ref in enumerate((top_ref, bottom_ref)):
-            src = ref.at[pl.ds(b * HALF, HALF)]
-            dst = half_of(out_hbm, mine, place, h)
+            src = ref.at[pl.ds(b * PIECES[h], PIECES[h])]
+            dst = piece_of(out_hbm, mine, place, h)
             todo.append((mine, pltpu.make_async_copy(src, dst, sems.at[h, b])))
     for mine, copy in todo:
         pl.when(mine)(copy.start)
@@ -210,55 +209,76 @@
         pl.when(mine)(copy.wait)
 
 
-def merge_kernel(plane, tenants, top_ref, bottom_ref, got_top, got_bottom, own_hbm, out_hbm, buf, sems):
+def merge_kernel(
+    plane, tenants, top_ref, bottom_ref, got_top, got_bottom, own_hbm, out_hbm,
+    top_buf, bottom_buf, sems,
+):
     blocks = sems.shape[1]
+    gots = got_top, got_bottom
     todo = []
-    for h, (ref, got) in enumerate(((top_ref, got_top), (bottom_ref, got_bottom))):
+    for h, (ref, got, buf) in enumerate(zip((top_ref, bottom_ref), gots, (top_buf, bottom_buf))):
+        size = PIECES[h]
         for b in range(blocks):
-            tenant = jnp.max(got[blocks * HALF + b : blocks * HALF + b + 1, :]).astype(jnp.int32)
+            tenant = got[blocks * size + b, 0].astype(jnp.int32)
             mine, place = kept(tenant, plane[0] % 2)
             same = jnp.int32(-1)
             for c in range(blocks - 1, -1, -1):
                 same = jnp.where(tenants[0, c] == tenant, c, same)
-            at = pl.multiple_of(jnp.maximum(same, 0) * HALF, 8)
+            at = pl.multiple_of(jnp.maximum(same, 0) * size, 8)
             here = jnp.where(same >= 0, 1.0, 0.0)
-            buf[h, b] = got[b * HALF : (b + 1) * HALF, :] + ref[pl.ds(at, HALF), :] * here
-            copy = pltpu.make_async_copy(buf.at[h, b], half_of(out_hbm, mine, place, h), sems.at[h, b])
+            buf[b] = got[b * size : (b + 1) * size, :] + ref[pl.ds(at, size), :] * here
+            copy = pltpu.make_async_copy(buf.at[b], piece_of(out_hbm, mine, place, h), sems.at[h, b])
             pl.when(mine)(copy.start)
             todo.append((mine, copy))
     for mine, copy in todo:
         pl.when(mine)(copy.wait)
 
 
-def base_kernel(where, kv_ref, near_ref, far_ref, low_ref, out_ref, w):
+def weights_kernel(where, near_hbm, far_hbm, w_ref, a_ref, near_ref, far_ref, sems):
+    loads = [
+        pltpu.make_async_copy(near_hbm, near_ref, sems.at[0]),
+        pltpu.make_async_copy(far_hbm, far_ref, sems.at[1]),
+    ]
+    for c in loads:
+        c.start()
+    for c in loads:
+        c.wait()
     width = near_ref.shape[1]
-    blocks = width // LANE
-    feat = out_ref.shape[2] // 2
-    per = kv_ref.shape[0] // blocks
-    rank = (near_ref.shape[0] - 2 * feat) // 4
+    blocks = a_ref.shape[0]
+    feat = w_ref.shape[0] // 2
+    rank = a_ref.shape[1] // 4
     core = where[0] % 2
     for c, ref in enumerate((near_ref, far_ref)):
         at = pl.multiple_of(jnp.where(core == 0, c, 1 - c) * feat, 16)
-        w[pl.ds(at, feat), :width] = ref[0:feat, :]
-        w[pl.ds(at, feat), width:] = ref[feat : 2 * feat, :]
+        w_ref[pl.ds(at, feat), :width] = ref[0:feat, :]
+        w_ref[pl.ds(at, feat), width:] = ref[feat : 2 * feat, :]
+    first = 2 * feat
+    for b in range(blocks):
+        pair = []
+        for ref in (near_ref, far_ref):
+            main = ref[first : first + 2 * rank, LANE * b : LANE * (b + 1)]
+            rest = ref[first + 2 * rank :, LANE * b : LANE * b + feat - LANE]
+            pair.append(jnp.concatenate([main, rest], axis=1).astype(F32))
+        same, other = jnp.concatenate(pair, axis=1), jnp.concatenate(pair[::-1], axis=1)
+        a = jnp.where(core == 0, same, other).astype(BF16)
+        a_ref[b, : 2 * rank, :] = a
+        a_ref[b, 2 * rank :, :] = a
+
+
+def base_kernel(kv_ref, w_ref, a_ref, low_ref, out_ref):
+    blocks = a_ref.shape[0]
+    per = kv_ref.shape[0] // blocks
     step = 4
     for s in range(0, blocks, step):
-        rows = kv_ref[per * s : per * (s + step)].reshape(-1, kv_ref.shape[-1])
-        res = lax.dot_general(rows, w[...], (((1,), (1,)), ((), ())), preferred_element_type=F32)
+        rows = [kv_ref[i % 4 * (kv_ref.shape[0] // 4) + i // 4] for i in range(per * s, per * (s + step))]
+        rows = jnp.concatenate(rows, axis=0)
+        res = lax.dot_general(rows, w_ref[...], (((1,), (1,)), ((), ())), preferred_element_type=F32)
         size = res.shape[0] // step
         for i in range(step):
             b = s + i
             low = low_ref[per * b : per * (b + 1)].reshape(-1, LANE)
-            add = []
-            for ref in (near_ref, far_ref):
-                main = ref[2 * feat : 2 * feat + 2 * rank, LANE * b : LANE * (b + 1)]
-                rest = ref[2 * feat + 2 * rank :, LANE * b : LANE * b + feat - LANE]
-                a = jnp.concatenate([main, rest], axis=1)
-                add.append(jnp.dot(low, jnp.concatenate([a, a], axis=0), preferred_element_type=F32))
-            swapped = jnp.concatenate(add[::-1], axis=1)
-            add = jnp.where(core == 0, jnp.concatenate(add, axis=1), swapped)
-            total = res[size * i : size * (i + 1)] + add
-            out_ref[per * b : per * (b + 1)] = total.astype(BF16).reshape(per, -1, 2 * feat)
+            total = res[size * i : size * (i + 1)] + jnp.dot(low, a_ref[b], preferred_element_type=F32)
+            out_ref[per * b : per * (b + 1)] = total.astype(BF16).reshape(per, -1, w_ref.shape[0])
 
 
 def finish_kernel(sum_hbm, ak_ref, av_ref, bk_ref, bv_ref, sum_ref, sem):
@@ -329,10 +349,10 @@
         name="vectors",
     )(send, recv)
     vec = lax.all_to_all(vec_send, mp, split_axis=0, concat_axis=0, tiled=True)
-    group = jax.ShapeDtypeStruct((blocks * HALF + blocks, LANE), F32)
+    groups = [jax.ShapeDtypeStruct((blocks * n + blocks, LANE), F32) for n in PIECES]
     top, bottom, low = pl.pallas_call(
         parts_kernel,
-        out_shape=(group, group, jax.ShapeDtypeStruct((n_mp // 2, tok, LANE), BF16)),
+        out_shape=(*groups, jax.ShapeDtypeStruct((n_mp // 2, tok, LANE), BF16)),
         in_specs=[SMEM, SMEM, VMEM, VMEM],
         out_specs=(VMEM, VMEM, VMEM),
         compiler_params=PARAMS,
@@ -368,7 +388,7 @@
         in_specs=[SMEM, SMEM, VMEM, VMEM, VMEM, VMEM, HBM],
         out_specs=HBM,
         scratch_shapes=[
-            pltpu.VMEM((2, blocks, HALF, LANE), F32),
+            *[pltpu.VMEM((blocks, n, LANE), F32) for n in PIECES],
             pltpu.SemaphoreType.DMA((2, blocks)),
         ],
         input_output_aliases={6: 0},
@@ -382,16 +402,31 @@
     def swap(a, axes):
         return lax.all_to_all(a, axes, split_axis=0, concat_axis=0, tiled=True)
 
-    kv = swap(jnp.broadcast_to(masked[None], (n_mp // 2, *masked.shape)), ("y", "x"))
+    kv = swap(jnp.broadcast_to(masked[None], (n_mp // 2, *masked.shape)), ("x", "y"))
+    w, a = pl.pallas_call(
+        weights_kernel,
+        out_shape=(
+            pltpu.VMEM((2 * feat, 2 * kv_width), BF16),
+            pltpu.VMEM((blocks, 4 * rank, 2 * feat), BF16),
+        ),
+        in_specs=[SMEM, HBM, HBM],
+        out_specs=(VMEM, VMEM),
+        scratch_shapes=[
+            pltpu.VMEM(bundle.shape, BF16),
+            pltpu.VMEM(bundle.shape, BF16),
+            pltpu.SemaphoreType.DMA((2,)),
+        ],
+        compiler_params=PARAMS,
+        name="weights",
+    )(me, hbm(bundle), hbm(far))
     grad = pl.pallas_call(
         base_kernel,
         out_shape=jax.ShapeDtypeStruct((n_mp // 2, tok, 2 * feat), BF16),
-        in_specs=[SMEM] + [VMEM] * 4,
+        in_specs=[VMEM] * 4,
         out_specs=VMEM,
-        scratch_shapes=[pltpu.VMEM((2 * feat, 2 * kv_width), BF16)],
         compiler_params=PARAMS,
         name="base",
-    )(me, kv, bundle, far, low)
+    )(kv, w, a, low)
     grad = swap(grad, ("y", "x"))
     grad_in = grad.transpose(1, 0, 2).reshape(tok, width)
     sums, grad_in = lax.optimization_barrier((sums, grad_in))

time: 139 us -> 137 us (0.986)
  the two profiles are of different devices: /device:TPU:42 before, /device:TPU:56 now
where the time goes in v5:
time: 137 us
  blocking collectives  54 us (39%)
  waiting for transfers between devices  34 us (25%)
  starting transfers between devices  15.4 us (11%)
  between operations  14.2 us (10%)
  Pallas kernels  13.6 us (10%)
  local copies, waits for them, and re-layouts  5.75 us (4%)
    all_to_all x1, blocking collectives, shards(): recv = lax.all_to_all(send, mp, split_axis=0, concat_axis=0, tiled=True)  25.1 us
    all_to_all x1, waiting for transfers between devices, swap(): return lax.all_to_all(a, axes, split_axis=0, concat_axis=0, tiled=True)  19.2 us
    all_to_all x1, blocking collectives, shards(): vec = lax.all_to_all(vec_send, mp, split_axis=0, concat_axis=0, tiled=True)  15.2 us
    all_to_all x1, blocking collectives, swap(): return lax.all_to_all(a, axes, split_axis=0, concat_axis=0, tiled=True)  13.7 us
    reduce_scatter x1, waiting for transfers between devices, shards(): sums = lax.psum_scatter(sums, 'zh', scatter_dimension=0, tiled=True)  11.2 us
    all_to_all x1, starting transfers between devices, swap(): return lax.all_to_all(a, axes, split_axis=0, concat_axis=0, tiled=True)  5.76 us
    ppermute x1, starting transfers between devices, shards(): got_bottom = lax.ppermute(bottom, dp, others)  4.4 us
    ppermute x1, starting transfers between devices, shards(): got_top = lax.ppermute(top, dp, pairs)  3.26 us
  transfers between devices with their start and end apart: 5, of which 5 were waited for; matrix products, arithmetic and copies ran while one was open for 2% of the time, Pallas kernels for 4%

profile of v5, /device:TPU:56, one launch (start us, length us, event | category | flops | bytes accessed | tf_op | source)
XLA Modules:
  0.0 137.0 jit_solution(5786262139692141426)
XLA Ops:
  7.2 0.0 reduce-scatter.2.cloned.1.call-start
  7.2 2.8 %pack.1 = (bf16[32,160,128]{2,1,0:T(8,128)(2,1)S(1)}, bf16[32,2048]{1,0:T(8,128)(2,1)S(1)}, bf16[448,1024]{1,0:T(8,128)(2,1)S(1)}) custom-call(s32[1]{0:T(128)} %bitcast.1.where, s32[1,8]{1,0:T(1,128)} %tenants.5, s32[1,8]{1,0:T(1,128)} %counts_hbm.1, bf16[32,5120]{1,0:T(8,128)(2,1)} %x_hbm.1, bf16[32,1024]{1,0:T(8,128)(2,1)} %k_hbm.1, ...), custom_call_target="tpu_custom_call" | custom-call | tf_op jit(solution)/shard_map/pack/pallas_call | solution.py:310
  10.0 0.0 copy-start
  10.0 25.1 %all_to_all.20.recv_ref = bf16[32,160,128]{2,1,0:T(8,128)(2,1)S(1)} all-to-all(bf16[32,160,128]{2,1,0:T(8,128)(2,1)S(1)} %get-tuple-element.23.send_ref), channel_id=1, replica_groups=mesh['zh'=8,'zl'=2,'y'=4,'x'=4,'core'=2] {'y','x','core'}, dimensions={0} | all-to-all | bytes 2621440 | tf_op jit(solution)/shard_map/all_to_all | solution.py:342
  35.2 0.0 copy-start.3
  35.2 0.8 vectors.1
  36.0 15.2 %all_to_all.21.vec_ref = f32[32,32,128]{2,1,0:T(8,128)S(1)} all-to-all(f32[32,32,128]{2,1,0:T(8,128)S(1)} %vectors.1), channel_id=1, replica_groups=mesh['zh'=8,'zl'=2,'y'=4,'x'=4,'core'=2] {'y','x','core'}, dimensions={0} | all-to-all | bytes 1048576 | tf_op jit(solution)/shard_map/all_to_all | solution.py:351
  51.2 0.0 copy-done.3
  51.2 0.9 parts.1
  52.1 3.3 %collective-permute-start = (f32[520,128]{1,0:T(8,128)S(1)}, f32[520,128]{1,0:T(8,128)S(1)}, u32[]{:S(2)}, u32[]{:S(2)}) collective-permute-start(f32[520,128]{1,0:T(8,128)S(1)} %get-tuple-element.24.top_ref), channel_id=1, source_target_pairs={{0,32},{32,0},{64,96},{96,64},{128,160},{160,128},{192,224},{224,1... | collective-permute-start | bytes 798728 | tf_op jit(solution)/shard_map/ppermute | solution.py:366
  55.3 4.4 %collective-permute-start.1 = (f32[264,128]{1,0:T(8,128)S(1)}, f32[264,128]{1,0:T(8,128)S(1)}, u32[]{:S(2)}, u32[]{:S(2)}) collective-permute-start(f32[264,128]{1,0:T(8,128)S(1)} %get-tuple-element.25.bottom_ref), channel_id=1, source_target_pairs={{0,480},{32,64},{64,32},{96,128},{128,96},{160,192},{192,160},{224... | collective-permute-start | bytes 405512 | tf_op jit(solution)/shard_map/ppermute | solution.py:367
  59.7 2.6 %own.1.own_hbm = f32[32,96,128]{2,1,0:T(8,128)} custom-call(s32[1]{0:T(128)} %bitcast.plane, s32[1,8]{1,0:T(1,128)S(1)} %copy-done.3, f32[520,128]{1,0:T(8,128)S(1)} %get-tuple-element.24.top_ref, f32[264,128]{1,0:T(8,128)S(1)} %get-tuple-element.25.bottom_ref), custom_call_target="tpu_custom_call" | custom-call | tf_op jit(solution)/shard_map/own/pallas_call | solution.py:370
  62.3 0.2 collective-permute-done.got_top
  62.6 0.9 collective-permute-done.1.got_bottom
  63.5 1.7 %merge.1 = f32[32,96,128]{2,1,0:T(8,128)} custom-call(s32[1]{0:T(128)} %bitcast.plane, s32[1,8]{1,0:T(1,128)S(1)} %copy-done.3, f32[520,128]{1,0:T(8,128)S(1)} %get-tuple-element.24.top_ref, f32[264,128]{1,0:T(8,128)S(1)} %get-tuple-element.25.bottom_ref, f32[520,128]{1,0:T(8,128)S(1)} %collective-permute-done.got_top, ...), custom_call_target="tpu_custom_call", output_to_operand_aliasing={{}: (6, {})} | custom-call | tf_op jit(solution)/shard_map/merge/pallas_call | solution.py:385
  65.2 0.0 reduce-scatter.2.cloned.1.call-update
  65.2 1.6 %broadcast_in_dim.2 = bf16[16,32,2048]{2,1,0:T(8,128)(2,1)} broadcast(bf16[32,2048]{1,0:T(8,128)(2,1)S(1)} %get-tuple-element.30), dimensions={1,2} | broadcast | bytes 2228224 | tf_op jit(solution)/shard_map/broadcast_in_dim | solution.py:405
  66.8 5.8 %all-to-all-start.2 = ((bf16[16,32,2048]{2,1,0:T(8,128)(2,1)}), bf16[16,32,2048]{2,1,0:T(8,128)(2,1)S(1)}, u32[]{:S(2)}, u32[]{:S(2)}) async-start(bf16[16,32,2048]{2,1,0:T(8,128)(2,1)} %broadcast_in_dim.2), calls=%async_computation.3 | async-start | bytes 4194304 | tf_op jit(solution)/shard_map/all_to_all | solution.py:403
  72.5 0.0 copy-done
  72.5 1.9 %collective-permute-start.2 = (bf16[448,1024]{1,0:T(8,128)(2,1)S(1)}, bf16[448,1024]{1,0:T(8,128)(2,1)S(1)}, u32[]{:S(2)}, u32[]{:S(2)}) collective-permute-start(bf16[448,1024]{1,0:T(8,128)(2,1)S(1)} %get-tuple-element.31.near_hbm), channel_id=1, source_target_pairs={{0,1},{1,0},{2,3},{3,2},{4,5},{5,4},{6,7},{7,6},{8,9},{9,8},{10,11... | collective-permute-start | bytes 2752520 | tf_op jit(solution)/shard_map/ppermute | solution.py:384
  74.5 2.4 %collective-permute-done.2.far_hbm = bf16[448,1024]{1,0:T(8,128)(2,1)S(1)} collective-permute-done((bf16[448,1024]{1,0:T(8,128)(2,1)S(1)}, bf16[448,1024]{1,0:T(8,128)(2,1)S(1)}, u32[]{:S(2)}, u32[]{:S(2)}) %collective-permute-start.2) | collective-permute-done | bytes 917536 | tf_op jit(solution)/shard_map/ppermute | solution.py:384
  76.9 0.0 copy-start.4
  76.9 1.0 copy-done.4
  77.9 1.8 %weights.1 = (bf16[320,2048]{1,0:T(8,128)(2,1)S(1)}, bf16[8,128,320]{2,1,0:T(8,128)(2,1)S(1)}) custom-call(s32[1]{0:T(128)} %bitcast.1.where, bf16[448,1024]{1,0:T(8,128)(2,1)} %copy-done, bf16[448,1024]{1,0:T(8,128)(2,1)} %copy-done.4), custom_call_target="tpu_custom_call" | custom-call | tf_op jit(solution)/shard_map/weights/pallas_call | solution.py:406
  79.7 0.0 copy-start.1
  79.7 0.9 copy-done.1
  80.6 19.2 %all-to-all-done.2.kv_ref = bf16[16,32,2048]{2,1,0:T(8,128)(2,1)S(1)} async-done(((bf16[16,32,2048]{2,1,0:T(8,128)(2,1)}), bf16[16,32,2048]{2,1,0:T(8,128)(2,1)S(1)}, u32[]{:S(2)}, u32[]{:S(2)}) %all-to-all-start.2) | async-done | bytes 2097184 | tf_op jit(solution)/shard_map/all_to_all | solution.py:403
  99.7 0.0 copy-start.2
  99.8 1.1 copy-done.2
  100.9 1.4 %base.1 = bf16[16,32,320]{2,1,0:T(8,128)(2,1)S(1)} custom-call(bf16[16,32,2048]{2,1,0:T(8,128)(2,1)S(1)} %all-to-all-done.2.kv_ref, bf16[320,2048]{1,0:T(8,128)(2,1)S(1)} %get-tuple-element.32.w_ref, bf16[8,128,320]{2,1,0:T(8,128)(2,1)S(1)} %copy-done.2, bf16[16,32,128]{2,1,0:T(8,128)(2,1)S(1)} %get-tuple-element.34.low_ref), custom_call_target="tpu_custom_call" | custom-call | tf_op jit(solution)/shard_map/base/pallas_call | solution.py:422
  102.3 13.7 %all_to_all.22 = bf16[16,32,320]{2,1,0:T(8,128)(2,1)S(1)} all-to-all(bf16[16,32,320]{2,1,0:T(8,128)(2,1)S(1)} %base.1), channel_id=1, replica_groups=mesh['zh'=8,'zl'=2,'y'=4,'x'=4,'core'=2] {'y','x'}, dimensions={0} | all-to-all | bytes 655360 | tf_op jit(solution)/shard_map/all_to_all | solution.py:403
  116.0 0.1 copy.17
  116.1 1.0 reshape.22
  117.2 11.2 %reduce-scatter.2.cloned.1.call-done.sum_hbm = f32[4,96,128]{2,1,0:T(8,128)} async-done(((f32[32,96,128]{2,1,0:T(8,128)}), f32[4,96,128]{2,1,0:T(8,128)}) %reduce-scatter.2.cloned.1.call-update) | async-done | bytes 196624 | tf_op jit(solution)/shard_map/reduce_scatter | solution.py:400
  128.4 1.7 %finish.1 = (f32[4,32,160]{2,1,0:T(8,128)}, f32[4,32,160]{2,1,0:T(8,128)}, f32[4,32,32]{2,1,0:T(8,128)}, f32[4,32,32]{2,1,0:T(8,128)}) custom-call(f32[4,96,128]{2,1,0:T(8,128)} %reduce-scatter.2.cloned.1.call-done.sum_hbm), custom_call_target="tpu_custom_call" | custom-call | tf_op jit(solution)/shard_map/finish/pallas_call | solution.py:435
Async XLA Ops:
  7.2 121.2 %reduce-scatter.2.cloned.1.call-start = ((), (), s32[]{:S(2)}) async-start(), calls=%async_computation.5 | async-start | bytes 1769472 | tf_op jit(solution)/shard_map/reduce_scatter | solution.py:400
  10.0 62.5 %copy-start = (bf16[448,1024]{1,0:T(8,128)(2,1)}, bf16[448,1024]{1,0:T(8,128)(2,1)S(1)}, u32[]{:S(2)}) copy-start(bf16[448,1024]{1,0:T(8,128)(2,1)S(1)} %get-tuple-element.31.near_hbm) | copy-start | bytes 2752516
  35.2 16.0 %copy-start.3 = (s32[1,8]{1,0:T(1,128)S(1)}, s32[1,8]{1,0:T(1,128)}, u32[]{:S(2)}) copy-start(s32[1,8]{1,0:T(1,128)} %tenants.5) | copy-start | bytes 100
  52.1 10.5 %collective-permute-start = (f32[520,128]{1,0:T(8,128)S(1)}, f32[520,128]{1,0:T(8,128)S(1)}, u32[]{:S(2)}, u32[]{:S(2)}) collective-permute-start(f32[520,128]{1,0:T(8,128)S(1)} %get-tuple-element.24.top_ref), channel_id=1, source_target_pairs={{0,32},{32,0},{64,96},{96,64},{128,160},{160,128},{192,224},{224,1... | collective-permute-start | bytes 798728 | tf_op jit(solution)/shard_map/ppermute | solution.py:366
  55.3 8.2 %collective-permute-start.1 = (f32[264,128]{1,0:T(8,128)S(1)}, f32[264,128]{1,0:T(8,128)S(1)}, u32[]{:S(2)}, u32[]{:S(2)}) collective-permute-start(f32[264,128]{1,0:T(8,128)S(1)} %get-tuple-element.25.bottom_ref), channel_id=1, source_target_pairs={{0,480},{32,64},{64,32},{96,128},{128,96},{160,192},{192,160},{224... | collective-permute-start | bytes 405512 | tf_op jit(solution)/shard_map/ppermute | solution.py:367
  66.8 33.0 %all-to-all-start.2 = ((bf16[16,32,2048]{2,1,0:T(8,128)(2,1)}), bf16[16,32,2048]{2,1,0:T(8,128)(2,1)S(1)}, u32[]{:S(2)}, u32[]{:S(2)}) async-start(bf16[16,32,2048]{2,1,0:T(8,128)(2,1)} %broadcast_in_dim.2), calls=%async_computation.3 | async-start | bytes 4194304 | tf_op jit(solution)/shard_map/all_to_all | solution.py:403
  72.5 4.4 %collective-permute-start.2 = (bf16[448,1024]{1,0:T(8,128)(2,1)S(1)}, bf16[448,1024]{1,0:T(8,128)(2,1)S(1)}, u32[]{:S(2)}, u32[]{:S(2)}) collective-permute-start(bf16[448,1024]{1,0:T(8,128)(2,1)S(1)} %get-tuple-element.31.near_hbm), channel_id=1, source_target_pairs={{0,1},{1,0},{2,3},{3,2},{4,5},{5,4},{6,7},{7,6},{8,9},{9,8},{10,11... | collective-permute-start | bytes 2752520 | tf_op jit(solution)/shard_map/ppermute | solution.py:384
  76.9 1.0 copy-start.4
  79.7 0.9 copy-start.1
  99.7 1.1 copy-start.2
Sparse Core Ops, SparseCore 0:
  65.3 63.0 reduce-scatter.1

commit v6 on v5

--- a/solution.py
+++ b/solution.py
@@ -17,13 +17,24 @@
 PARAMS = pltpu.CompilerParams(vmem_limit_bytes=24 * 1024 * 1024)
 LANE = 128
 
+PACKED = 224
+
+
+def slot(chip):
+    return chip % 4 * 4 + chip // 4
+
+
+def tokens_of(ref, chip, core):
+    at = pl.multiple_of(96 + 64 * core, 32)
+    return ref[slot(chip), pl.ds(at, 32), :], ref[slot(chip), pl.ds(at + 32, 32), :]
+
 
 def pack_kernel(
     where, tenants_hbm, counts_hbm, x_hbm, k_hbm, v_hbm, bk_hbm, bv_hbm, ak_hbm, av_hbm, wk_hbm, wv_hbm,
     send_ref, masked_hbm, bundle_hbm,
     tenants, counts, x_ref, k_ref, v_ref, bk_ref, bv_ref, ak, av, up, masked, low, sems, a_sems, out_sems,
 ):
-    n_mp = send_ref.shape[0]
+    n_mp = 2 * send_ref.shape[0]
     blocks, rank, feat = ak.shape
     tok, kv_width = k_ref.shape
     cols = kv_width // n_mp
@@ -65,9 +76,10 @@
     stores[2].start()
     x = x_ref[...]
     for j in range(n_mp):
-        send_ref[j, 96:128, :] = x[:, feat * j : feat * j + LANE]
+        at = 96 + 64 * (j % 2)
+        send_ref[slot(j // 2), at : at + 32, :] = x[:, feat * j : feat * j + LANE]
         last = x[:, feat * j + LANE : feat * (j + 1)]
-        send_ref[j, 128:160, :] = jnp.concatenate(
+        send_ref[slot(j // 2), at + 32 : at + 64, :] = jnp.concatenate(
             [last, mk[:, cols * j : cols * (j + 1)], last, mv[:, cols * j : cols * (j + 1)]], axis=1
         )
     which = lax.broadcasted_iota(jnp.int32, (blocks, bk_ref.shape[2]), 0)
@@ -97,9 +109,9 @@
         tail = jnp.concatenate(
             [a0[:, LANE:], near[:, 32:64], a1[:, LANE:], near[:, 96:128]], axis=1
         )
-        for q in range(quad):
-            send_ref[quad * b + q, 0:64, :] = main
-            send_ref[quad * b + q, 64:96, :] = tail
+        for q in range(quad // 2):
+            send_ref[slot(quad // 2 * b + q), 0:64, :] = main
+            send_ref[slot(quad // 2 * b + q), 64:96, :] = tail
     for c in stores:
         c.wait()
 
@@ -109,19 +121,20 @@
     return (lane >= 32 * slot) & (lane < 32 * slot + 32)
 
 
-def vector_kernel(send_ref, recv_ref, out_ref):
-    n_mp = send_ref.shape[0]
+def vector_kernel(where, send_ref, recv_ref, other_ref, out_ref):
+    core = where[0] % 2
     masks = [lane_mask(32, s) for s in (0, 2, 1, 3)]
     total = jnp.zeros((32, LANE), F32)
     zero = jnp.zeros((64, LANE), BF16)
-    for m in range(n_mp):
-        lhs = jnp.concatenate([send_ref[m, 96:128, :], send_ref[m, 128:160, :]], axis=1)
-        main = jnp.concatenate([recv_ref[m, 0:64, :], zero], axis=0)
-        tail = recv_ref[m, 64:96, :]
-        tails = jnp.concatenate([jnp.where(k, tail, jnp.zeros_like(tail)) for k in masks], axis=0)
-        rhs = jnp.concatenate([main, tails], axis=1)
-        total += lax.dot_general(lhs, rhs, (((1,), (1,)), ((), ())), preferred_element_type=F32)
-    for m in range(n_mp):
+    for chip in range(send_ref.shape[0]):
+        for ref, c in ((recv_ref, core), (other_ref, 1 - core)):
+            lhs = jnp.concatenate(tokens_of(send_ref, chip, c), axis=1)
+            main = jnp.concatenate([ref[slot(chip), 0:64, :], zero], axis=0)
+            tail = ref[slot(chip), 64:96, :]
+            tails = jnp.concatenate([jnp.where(k, tail, jnp.zeros_like(tail)) for k in masks], axis=0)
+            rhs = jnp.concatenate([main, tails], axis=1)
+            total += lax.dot_general(lhs, rhs, (((1,), (1,)), ((), ())), preferred_element_type=F32)
+    for m in range(out_ref.shape[0]):
         out_ref[m] = total
 
 
@@ -144,17 +157,24 @@
 PART = sum(PIECES)
 
 
-def parts_kernel(where, tenants, vec_ref, recv_ref, top_ref, bottom_ref, low_ref):
+def parts_kernel(where, tenants, vec_ref, recv_ref, other_ref, top_ref, bottom_ref, low_ref):
+    core = where[0] % 2
     blocks = vec_ref.shape[0] // 4
     m0, m1, m2, m3 = [lane_mask(32, s) for s in range(4)]
     first = first_blocks(tenants, blocks)
     top_ref[...] = jnp.zeros_like(top_ref)
     bottom_ref[...] = jnp.zeros_like(bottom_ref)
     for b in range(blocks):
-        vec = vec_ref[4 * b : 4 * b + 4].reshape(BLOCK, LANE) * SCALE
-        lhs = jnp.concatenate(split(vec), axis=0)
-        near = recv_ref[4 * b : 4 * b + 4, 96:128, :].reshape(BLOCK, LANE)
-        far = recv_ref[4 * b : 4 * b + 4, 128:160, :].reshape(BLOCK, LANE)
+        vec, near, far = [], [], []
+        for chip in (2 * b, 2 * b + 1):
+            for ref, c in ((recv_ref, core), (other_ref, 1 - core)):
+                vec.append(vec_ref[2 * chip + c] * SCALE)
+                first_part, last_part = tokens_of(ref, chip, core)
+                near.append(first_part)
+                far.append(last_part)
+        lhs = jnp.concatenate(split(jnp.concatenate(vec, axis=0)), axis=0)
+        near = jnp.concatenate(near, axis=0)
+        far = jnp.concatenate(far, axis=0)
         rhs = jnp.concatenate([near, far], axis=1)
         rhs = jnp.concatenate([rhs, rhs], axis=0)
         p = lax.dot_general(lhs, rhs, (((0,), (0,)), ((), ())), preferred_element_type=F32)
@@ -168,7 +188,6 @@
         ids = jnp.where((row == b) & (first[b] == b), tenants[0, b], ids)
     top_ref[blocks * 64 :, :] = ids.astype(F32)
     bottom_ref[blocks * 32 :, :] = ids.astype(F32)
-    core = where[0] % 2
     for i in range(low_ref.shape[0]):
         back = vec_ref[2 * i + core][:, 64:] * SCALE
         low_ref[i] = jnp.concatenate(split(back), axis=1)
@@ -234,15 +253,7 @@
         pl.when(mine)(copy.wait)
 
 
-def weights_kernel(where, near_hbm, far_hbm, w_ref, a_ref, near_ref, far_ref, sems):
-    loads = [
-        pltpu.make_async_copy(near_hbm, near_ref, sems.at[0]),
-        pltpu.make_async_copy(far_hbm, far_ref, sems.at[1]),
-    ]
-    for c in loads:
-        c.start()
-    for c in loads:
-        c.wait()
+def weights_kernel(where, near_ref, far_ref, w_ref, a_ref):
     width = near_ref.shape[1]
     blocks = a_ref.shape[0]
     feat = w_ref.shape[0] // 2
@@ -265,7 +276,9 @@
         a_ref[b, 2 * rank :, :] = a
 
 
-def base_kernel(kv_ref, w_ref, a_ref, low_ref, out_ref):
+def base_kernel(kv_ref, w_ref, a_hbm, low_ref, out_ref, a_ref, sem):
+    load = pltpu.make_async_copy(a_hbm, a_ref, sem)
+    load.start()
     blocks = a_ref.shape[0]
     per = kv_ref.shape[0] // blocks
     step = 4
@@ -274,6 +287,8 @@
         rows = jnp.concatenate(rows, axis=0)
         res = lax.dot_general(rows, w_ref[...], (((1,), (1,)), ((), ())), preferred_element_type=F32)
         size = res.shape[0] // step
+        if s == 0:
+            load.wait()
         for i in range(step):
             b = s + i
             low = low_ref[per * b : per * (b + 1)].reshape(-1, LANE)
@@ -310,7 +325,7 @@
     send, masked, bundle = pl.pallas_call(
         pack_kernel,
         out_shape=(
-            jax.ShapeDtypeStruct((n_mp, 160, LANE), BF16),
+            jax.ShapeDtypeStruct((n_mp // 2, PACKED, LANE), BF16),
             jax.ShapeDtypeStruct((tok, 2 * kv_width), BF16),
             jax.ShapeDtypeStruct((bundle_rows, kv_width), BF16),
         ),
@@ -339,25 +354,27 @@
         me, hbm(tenant_of_block), hbm(live_token_count), hbm(x), hbm(kg), hbm(vg),
         hbm(bk.transpose(1, 2, 0)), hbm(bv.transpose(1, 2, 0)), hbm(ak), hbm(av), hbm(wk), hbm(wv),
     )
-    recv = lax.all_to_all(send, mp, split_axis=0, concat_axis=0, tiled=True)
+    recv = lax.all_to_all(send, ("x", "y"), split_axis=0, concat_axis=0, tiled=True)
+    siblings = [(0, 1), (1, 0)]
+    other = lax.ppermute(recv, "core", siblings)
     vec_send = pl.pallas_call(
         vector_kernel,
         out_shape=jax.ShapeDtypeStruct((n_mp, tok, LANE), F32),
-        in_specs=[VMEM, VMEM],
+        in_specs=[SMEM, VMEM, VMEM, VMEM],
         out_specs=VMEM,
         compiler_params=PARAMS,
         name="vectors",
-    )(send, recv)
+    )(me, send, recv, other)
     vec = lax.all_to_all(vec_send, mp, split_axis=0, concat_axis=0, tiled=True)
     groups = [jax.ShapeDtypeStruct((blocks * n + blocks, LANE), F32) for n in PIECES]
     top, bottom, low = pl.pallas_call(
         parts_kernel,
         out_shape=(*groups, jax.ShapeDtypeStruct((n_mp // 2, tok, LANE), BF16)),
-        in_specs=[SMEM, SMEM, VMEM, VMEM],
+        in_specs=[SMEM, SMEM, VMEM, VMEM, VMEM],
         out_specs=(VMEM, VMEM, VMEM),
         compiler_params=PARAMS,
         name="parts",
-    )(me, tenant_of_block, vec, recv)
+    )(me, tenant_of_block, vec, recv, other)
 
     dp = ("zh", "zl")
     n_dp = lax.axis_size(dp)
@@ -381,7 +398,7 @@
         name="own",
     )(plane, tenant_of_block, top, bottom)
     got_top, bundle = lax.optimization_barrier((got_top, bundle))
-    far = lax.ppermute(bundle, "core", [(0, 1), (1, 0)])
+    far = lax.ppermute(bundle, "core", siblings)
     sums = pl.pallas_call(
         merge_kernel,
         out_shape=half,
@@ -407,26 +424,22 @@
         weights_kernel,
         out_shape=(
             pltpu.VMEM((2 * feat, 2 * kv_width), BF16),
-            pltpu.VMEM((blocks, 4 * rank, 2 * feat), BF16),
+            jax.ShapeDtypeStruct((blocks, 4 * rank, 2 * feat), BF16),
         ),
-        in_specs=[SMEM, HBM, HBM],
+        in_specs=[SMEM, VMEM, VMEM],
         out_specs=(VMEM, VMEM),
-        scratch_shapes=[
-            pltpu.VMEM(bundle.shape, BF16),
-            pltpu.VMEM(bundle.shape, BF16),
-            pltpu.SemaphoreType.DMA((2,)),
-        ],
         compiler_params=PARAMS,
         name="weights",
-    )(me, hbm(bundle), hbm(far))
+    )(me, bundle, far)
     grad = pl.pallas_call(
         base_kernel,
         out_shape=jax.ShapeDtypeStruct((n_mp // 2, tok, 2 * feat), BF16),
-        in_specs=[VMEM] * 4,
+        in_specs=[VMEM, VMEM, HBM, VMEM],
         out_specs=VMEM,
+        scratch_shapes=[pltpu.VMEM(a.shape, BF16), pltpu.SemaphoreType.DMA],
         compiler_params=PARAMS,
         name="base",
-    )(kv, w, a, low)
+    )(kv, w, hbm(a), low)
     grad = swap(grad, ("y", "x"))
     grad_in = grad.transpose(1, 0, 2).reshape(tok, width)
     sums, grad_in = lax.optimization_barrier((sums, grad_in))

time: 137 us -> 137 us (level)
  the two profiles are of different devices: /device:TPU:56 before, /device:TPU:60 now
where the time goes in v6:
time: 137 us; the launch traced here: 136 us
  blocking collectives  46.5 us (34%)
  waiting for transfers between devices  39 us (28%)
  starting transfers between devices  19.2 us (14%)
  between operations  14.2 us (10%)
  Pallas kernels  12.9 us (9%)
  local copies, waits for them, and re-layouts  4.82 us (4%)
    all_to_all x1, waiting for transfers between devices, swap(): return lax.all_to_all(a, axes, split_axis=0, concat_axis=0, tiled=True)  19.6 us
    all_to_all x1, blocking collectives, shards(): lax.all_to_all(send, ('x', 'y'), split_axis=0, concat_axis=0, tiled=True)  18.6 us
    all_to_all x1, blocking collectives, shards(): vec = lax.all_to_all(vec_send, mp, split_axis=0, concat_axis=0, tiled=True)  15.3 us
    reduce_scatter x1, waiting for transfers between devices, shards(): sums = lax.psum_scatter(sums, 'zh', scatter_dimension=0, tiled=True)  13.3 us
    all_to_all x1, blocking collectives, swap(): return lax.all_to_all(a, axes, split_axis=0, concat_axis=0, tiled=True)  12.6 us
    all_to_all x1, starting transfers between devices, swap(): return lax.all_to_all(a, axes, split_axis=0, concat_axis=0, tiled=True)  7.51 us
    ppermute x1, starting transfers between devices, shards(): got_bottom = lax.ppermute(bottom, dp, others)  5.69 us
    pallas_call x1, Pallas kernels, shards(): pl.pallas_call(pack_kernel, out_shape=(jax.ShapeDtypeStruct((n_mp // 2, P...  2.76 us
  transfers between devices with their start and end apart: 6, of which 6 were waited for; matrix products, arithmetic and copies ran while one was open for 2% of the time, Pallas kernels for 4%

profile of v6, /device:TPU:60, one launch (start us, length us, event | category | flops | bytes accessed | tf_op | source)
XLA Modules:
  0.0 136.5 jit_solution(7651540222290906607)
XLA Ops:
  7.2 0.0 reduce-scatter.2.cloned.1.call-start
  7.2 2.8 %pack.1 = (bf16[16,224,128]{2,1,0:T(8,128)(2,1)S(1)}, bf16[32,2048]{1,0:T(8,128)(2,1)S(1)}, bf16[448,1024]{1,0:T(8,128)(2,1)S(1)}) custom-call(s32[1]{0:T(128)} %bitcast.1.where, s32[1,8]{1,0:T(1,128)} %tenants.5, s32[1,8]{1,0:T(1,128)} %counts_hbm.1, bf16[32,5120]{1,0:T(8,128)(2,1)} %x_hbm.1, bf16[32,1024]{1,0:T(8,128)(2,1)} %k_hbm.1, ...), custom_call_target="tpu_custom_call" | custom-call | tf_op jit(solution)/shard_map/pack/pallas_call | solution.py:325
  10.0 0.0 copy-start
  10.0 18.6 %all_to_all.20.recv_ref = bf16[16,224,128]{2,1,0:T(8,128)(2,1)S(1)} all-to-all(bf16[16,224,128]{2,1,0:T(8,128)(2,1)S(1)} %get-tuple-element.23.send_ref), channel_id=1, replica_groups=mesh['zh'=8,'zl'=2,'y'=4,'x'=4,'core'=2] {'x','y'}, dimensions={0} | all-to-all | bytes 1835008 | tf_op jit(solution)/shard_map/all_to_all | solution.py:357
  28.6 0.0 copy-start.3
  28.6 2.0 %collective-permute-start = (bf16[16,224,128]{2,1,0:T(8,128)(2,1)S(1)}, bf16[16,224,128]{2,1,0:T(8,128)(2,1)S(1)}, u32[]{:S(2)}, u32[]{:S(2)}) collective-permute-start(bf16[16,224,128]{2,1,0:T(8,128)(2,1)S(1)} %all_to_all.20.recv_ref), channel_id=1, source_target_pairs={{0,1},{1,0},{2,3},{3,2},{4,5},{5,4},{6,7},{7,6},{8,9},{9,8},{10,11... | collective-permute-start | bytes 2752520 | tf_op jit(solution)/shard_map/ppermute | solution.py:359
  30.6 2.4 %collective-permute-done.other_ref = bf16[16,224,128]{2,1,0:T(8,128)(2,1)S(1)} collective-permute-done((bf16[16,224,128]{2,1,0:T(8,128)(2,1)S(1)}, bf16[16,224,128]{2,1,0:T(8,128)(2,1)S(1)}, u32[]{:S(2)}, u32[]{:S(2)}) %collective-permute-start) | collective-permute-done | bytes 917536 | tf_op jit(solution)/shard_map/ppermute | solution.py:359
  33.1 0.8 vectors.1
  33.9 15.3 %all_to_all.21.vec_ref = f32[32,32,128]{2,1,0:T(8,128)S(1)} all-to-all(f32[32,32,128]{2,1,0:T(8,128)S(1)} %vectors.1), channel_id=1, replica_groups=mesh['zh'=8,'zl'=2,'y'=4,'x'=4,'core'=2] {'y','x','core'}, dimensions={0} | all-to-all | bytes 1048576 | tf_op jit(solution)/shard_map/all_to_all | solution.py:368
  49.2 0.0 copy-done.3
  49.2 0.9 parts.1
  50.1 2.0 %collective-permute-start.1 = (f32[520,128]{1,0:T(8,128)S(1)}, f32[520,128]{1,0:T(8,128)S(1)}, u32[]{:S(2)}, u32[]{:S(2)}) collective-permute-start(f32[520,128]{1,0:T(8,128)S(1)} %get-tuple-element.24.top_ref), channel_id=1, source_target_pairs={{0,32},{32,0},{64,96},{96,64},{128,160},{160,128},{192,224},{224,1... | collective-permute-start | bytes 798728 | tf_op jit(solution)/shard_map/ppermute | solution.py:383
  52.0 5.7 %collective-permute-start.2 = (f32[264,128]{1,0:T(8,128)S(1)}, f32[264,128]{1,0:T(8,128)S(1)}, u32[]{:S(2)}, u32[]{:S(2)}) collective-permute-start(f32[264,128]{1,0:T(8,128)S(1)} %get-tuple-element.25.bottom_ref), channel_id=1, source_target_pairs={{0,480},{32,64},{64,32},{96,128},{128,96},{160,192},{192,160},{224... | collective-permute-start | bytes 405512 | tf_op jit(solution)/shard_map/ppermute | solution.py:384
  57.7 2.6 %own.1.own_hbm = f32[32,96,128]{2,1,0:T(8,128)} custom-call(s32[1]{0:T(128)} %bitcast.plane, s32[1,8]{1,0:T(1,128)S(1)} %copy-done.3, f32[520,128]{1,0:T(8,128)S(1)} %get-tuple-element.24.top_ref, f32[264,128]{1,0:T(8,128)S(1)} %get-tuple-element.25.bottom_ref), custom_call_target="tpu_custom_call" | custom-call | tf_op jit(solution)/shard_map/own/pallas_call | solution.py:387
  60.4 0.2 collective-permute-done.1.got_top
  60.6 0.9 collective-permute-done.2.got_bottom
  61.5 1.7 %merge.1 = f32[32,96,128]{2,1,0:T(8,128)} custom-call(s32[1]{0:T(128)} %bitcast.plane, s32[1,8]{1,0:T(1,128)S(1)} %copy-done.3, f32[520,128]{1,0:T(8,128)S(1)} %get-tuple-element.24.top_ref, f32[264,128]{1,0:T(8,128)S(1)} %get-tuple-element.25.bottom_ref, f32[520,128]{1,0:T(8,128)S(1)} %collective-permute-done.1.got_top, ...), custom_call_target="tpu_custom_call", output_to_operand_aliasing={{}: (6, {})} | custom-call | tf_op jit(solution)/shard_map/merge/pallas_call | solution.py:402
  63.2 0.0 reduce-scatter.2.cloned.1.call-update
  63.2 1.6 %broadcast_in_dim.2 = bf16[16,32,2048]{2,1,0:T(8,128)(2,1)} broadcast(bf16[32,2048]{1,0:T(8,128)(2,1)S(1)} %get-tuple-element.30), dimensions={1,2} | broadcast | bytes 2228224 | tf_op jit(solution)/shard_map/broadcast_in_dim | solution.py:422
  64.8 7.5 %all-to-all-start.2 = ((bf16[16,32,2048]{2,1,0:T(8,128)(2,1)}), bf16[16,32,2048]{2,1,0:T(8,128)(2,1)S(1)}, u32[]{:S(2)}, u32[]{:S(2)}) async-start(bf16[16,32,2048]{2,1,0:T(8,128)(2,1)} %broadcast_in_dim.2), calls=%async_computation.3 | async-start | bytes 4194304 | tf_op jit(solution)/shard_map/all_to_all | solution.py:420
  72.3 0.0 copy-done
  72.4 1.9 %collective-permute-start.3 = (bf16[448,1024]{1,0:T(8,128)(2,1)S(1)}, bf16[448,1024]{1,0:T(8,128)(2,1)S(1)}, u32[]{:S(2)}, u32[]{:S(2)}) collective-permute-start(bf16[448,1024]{1,0:T(8,128)(2,1)S(1)} %get-tuple-element.31.near_ref), channel_id=1, source_target_pairs={{0,1},{1,0},{2,3},{3,2},{4,5},{5,4},{6,7},{7,6},{8,9},{9,8},{10,11... | collective-permute-start | bytes 2752520 | tf_op jit(solution)/shard_map/ppermute | solution.py:401
  74.3 2.4 %collective-permute-done.3.far_ref = bf16[448,1024]{1,0:T(8,128)(2,1)S(1)} collective-permute-done((bf16[448,1024]{1,0:T(8,128)(2,1)S(1)}, bf16[448,1024]{1,0:T(8,128)(2,1)S(1)}, u32[]{:S(2)}, u32[]{:S(2)}) %collective-permute-start.3) | collective-permute-done | bytes 917536 | tf_op jit(solution)/shard_map/ppermute | solution.py:401
  76.7 0.0 copy-start.1
  76.7 1.2 copy-done.1
  77.9 0.3 weights.1
  78.3 0.0 copy-start.2
  78.3 0.9 copy-done.2
  79.1 19.6 %all-to-all-done.2.kv_ref = bf16[16,32,2048]{2,1,0:T(8,128)(2,1)S(1)} async-done(((bf16[16,32,2048]{2,1,0:T(8,128)(2,1)}), bf16[16,32,2048]{2,1,0:T(8,128)(2,1)S(1)}, u32[]{:S(2)}, u32[]{:S(2)}) %all-to-all-start.2) | async-done | bytes 2097184 | tf_op jit(solution)/shard_map/all_to_all | solution.py:420
  98.8 2.0 %base.1 = bf16[16,32,320]{2,1,0:T(8,128)(2,1)S(1)} custom-call(bf16[16,32,2048]{2,1,0:T(8,128)(2,1)S(1)} %all-to-all-done.2.kv_ref, bf16[320,2048]{1,0:T(8,128)(2,1)S(1)} %get-tuple-element.32.w_ref, bf16[8,128,320]{2,1,0:T(8,128)(2,1)} %copy-done.2, bf16[16,32,128]{2,1,0:T(8,128)(2,1)S(1)} %get-tuple-element.34.low_ref), custom_call_target="tpu_custom_call" | custom-call | tf_op jit(solution)/shard_map/base/pallas_call | solution.py:434
  100.8 12.6 %all_to_all.22 = bf16[16,32,320]{2,1,0:T(8,128)(2,1)S(1)} all-to-all(bf16[16,32,320]{2,1,0:T(8,128)(2,1)S(1)} %base.1), channel_id=1, replica_groups=mesh['zh'=8,'zl'=2,'y'=4,'x'=4,'core'=2] {'y','x'}, dimensions={0} | all-to-all | bytes 655360 | tf_op jit(solution)/shard_map/all_to_all | solution.py:420
  113.4 0.1 copy.17
  113.6 1.0 reshape.22
  114.6 13.3 %reduce-scatter.2.cloned.1.call-done.sum_hbm = f32[4,96,128]{2,1,0:T(8,128)} async-done(((f32[32,96,128]{2,1,0:T(8,128)}), f32[4,96,128]{2,1,0:T(8,128)}) %reduce-scatter.2.cloned.1.call-update) | async-done | bytes 196624 | tf_op jit(solution)/shard_map/reduce_scatter | solution.py:417
  127.9 1.7 %finish.1 = (f32[4,32,160]{2,1,0:T(8,128)}, f32[4,32,160]{2,1,0:T(8,128)}, f32[4,32,32]{2,1,0:T(8,128)}, f32[4,32,32]{2,1,0:T(8,128)}) custom-call(f32[4,96,128]{2,1,0:T(8,128)} %reduce-scatter.2.cloned.1.call-done.sum_hbm), custom_call_target="tpu_custom_call" | custom-call | tf_op jit(solution)/shard_map/finish/pallas_call | solution.py:448
Async XLA Ops:
  7.2 120.7 %reduce-scatter.2.cloned.1.call-start = ((), (), s32[]{:S(2)}) async-start(), calls=%async_computation.5 | async-start | bytes 1769472 | tf_op jit(solution)/shard_map/reduce_scatter | solution.py:417
  10.0 62.4 %copy-start = (bf16[448,1024]{1,0:T(8,128)(2,1)}, bf16[448,1024]{1,0:T(8,128)(2,1)S(1)}, u32[]{:S(2)}) copy-start(bf16[448,1024]{1,0:T(8,128)(2,1)S(1)} %get-tuple-element.31.near_ref) | copy-start | bytes 2752516
  28.6 20.6 %copy-start.3 = (s32[1,8]{1,0:T(1,128)S(1)}, s32[1,8]{1,0:T(1,128)}, u32[]{:S(2)}) copy-start(s32[1,8]{1,0:T(1,128)} %tenants.5) | copy-start | bytes 100
  28.6 4.5 %collective-permute-start = (bf16[16,224,128]{2,1,0:T(8,128)(2,1)S(1)}, bf16[16,224,128]{2,1,0:T(8,128)(2,1)S(1)}, u32[]{:S(2)}, u32[]{:S(2)}) collective-permute-start(bf16[16,224,128]{2,1,0:T(8,128)(2,1)S(1)} %all_to_all.20.recv_ref), channel_id=1, source_target_pairs={{0,1},{1,0},{2,3},{3,2},{4,5},{5,4},{6,7},{7,6},{8,9},{9,8},{10,11... | collective-permute-start | bytes 2752520 | tf_op jit(solution)/shard_map/ppermute | solution.py:359
  50.1 10.5 %collective-permute-start.1 = (f32[520,128]{1,0:T(8,128)S(1)}, f32[520,128]{1,0:T(8,128)S(1)}, u32[]{:S(2)}, u32[]{:S(2)}) collective-permute-start(f32[520,128]{1,0:T(8,128)S(1)} %get-tuple-element.24.top_ref), channel_id=1, source_target_pairs={{0,32},{32,0},{64,96},{96,64},{128,160},{160,128},{192,224},{224,1... | collective-permute-start | bytes 798728 | tf_op jit(solution)/shard_map/ppermute | solution.py:383
  52.0 9.5 %collective-permute-start.2 = (f32[264,128]{1,0:T(8,128)S(1)}, f32[264,128]{1,0:T(8,128)S(1)}, u32[]{:S(2)}, u32[]{:S(2)}) collective-permute-start(f32[264,128]{1,0:T(8,128)S(1)} %get-tuple-element.25.bottom_ref), channel_id=1, source_target_pairs={{0,480},{32,64},{64,32},{96,128},{128,96},{160,192},{192,160},{224... | collective-permute-start | bytes 405512 | tf_op jit(solution)/shard_map/ppermute | solution.py:384
  64.8 33.9 %all-to-all-start.2 = ((bf16[16,32,2048]{2,1,0:T(8,128)(2,1)}), bf16[16,32,2048]{2,1,0:T(8,128)(2,1)S(1)}, u32[]{:S(2)}, u32[]{:S(2)}) async-start(bf16[16,32,2048]{2,1,0:T(8,128)(2,1)} %broadcast_in_dim.2), calls=%async_computation.3 | async-start | bytes 4194304 | tf_op jit(solution)/shard_map/all_to_all | solution.py:420
  72.4 4.4 %collective-permute-start.3 = (bf16[448,1024]{1,0:T(8,128)(2,1)S(1)}, bf16[448,1024]{1,0:T(8,128)(2,1)S(1)}, u32[]{:S(2)}, u32[]{:S(2)}) collective-permute-start(bf16[448,1024]{1,0:T(8,128)(2,1)S(1)} %get-tuple-element.31.near_ref), channel_id=1, source_target_pairs={{0,1},{1,0},{2,3},{3,2},{4,5},{5,4},{6,7},{7,6},{8,9},{9,8},{10,11... | collective-permute-start | bytes 2752520 | tf_op jit(solution)/shard_map/ppermute | solution.py:401
  76.7 1.2 copy-start.1
  78.3 0.9 copy-start.2
Sparse Core Ops, SparseCore 0:
  63.4 64.4 reduce-scatter.1

commit v7 on v6

--- a/solution.py
+++ b/solution.py
@@ -53,8 +53,6 @@
         pltpu.make_async_copy(masked, masked_hbm, out_sems.at[2]),
         pltpu.make_async_copy(low, bundle_hbm.at[pl.ds(2 * feat, low.shape[0])], out_sems.at[3]),
     ]
-    stores[0].start()
-    stores[1].start()
     loads[0].wait()
     copies = []
     for b in range(blocks):
@@ -63,8 +61,15 @@
         copies.append(pltpu.make_async_copy(av_hbm.at[t], av.at[b], a_sems.at[1, b]))
     for c in copies:
         c.start()
-    for c in loads[1:]:
-        c.wait()
+    stores[0].start()
+    stores[1].start()
+    loads[2].wait()
+    x = x_ref[...]
+    for j in range(n_mp):
+        at = 96 + 64 * (j % 2)
+        send_ref[slot(j // 2), at : at + 32, :] = x[:, feat * j : feat * j + LANE]
+    for i in (1, 3, 4):
+        loads[i].wait()
     me = where[0]
     count = counts[0, me // quad]
     row = lax.broadcasted_iota(jnp.int32, (tok, 1), 0) + (me % quad) * tok
@@ -74,14 +79,14 @@
     masked[:, :kv_width] = mk
     masked[:, kv_width:] = mv
     stores[2].start()
-    x = x_ref[...]
     for j in range(n_mp):
-        at = 96 + 64 * (j % 2)
-        send_ref[slot(j // 2), at : at + 32, :] = x[:, feat * j : feat * j + LANE]
+        at = 128 + 64 * (j % 2)
         last = x[:, feat * j + LANE : feat * (j + 1)]
-        send_ref[slot(j // 2), at + 32 : at + 64, :] = jnp.concatenate(
+        send_ref[slot(j // 2), at : at + 32, :] = jnp.concatenate(
             [last, mk[:, cols * j : cols * (j + 1)], last, mv[:, cols * j : cols * (j + 1)]], axis=1
         )
+    for i in (5, 6):
+        loads[i].wait()
     which = lax.broadcasted_iota(jnp.int32, (blocks, bk_ref.shape[2]), 0)
     tenant = jnp.zeros_like(which)
     for b in range(blocks):
@@ -121,19 +126,26 @@
     return (lane >= 32 * slot) & (lane < 32 * slot + 32)
 
 
-def vector_kernel(where, send_ref, recv_ref, other_ref, out_ref):
-    core = where[0] % 2
+def vectors_of(send_ref, ref, core):
     masks = [lane_mask(32, s) for s in (0, 2, 1, 3)]
     total = jnp.zeros((32, LANE), F32)
     zero = jnp.zeros((64, LANE), BF16)
     for chip in range(send_ref.shape[0]):
-        for ref, c in ((recv_ref, core), (other_ref, 1 - core)):
-            lhs = jnp.concatenate(tokens_of(send_ref, chip, c), axis=1)
-            main = jnp.concatenate([ref[slot(chip), 0:64, :], zero], axis=0)
-            tail = ref[slot(chip), 64:96, :]
-            tails = jnp.concatenate([jnp.where(k, tail, jnp.zeros_like(tail)) for k in masks], axis=0)
-            rhs = jnp.concatenate([main, tails], axis=1)
-            total += lax.dot_general(lhs, rhs, (((1,), (1,)), ((), ())), preferred_element_type=F32)
+        lhs = jnp.concatenate(tokens_of(send_ref, chip, core), axis=1)
+        main = jnp.concatenate([ref[slot(chip), 0:64, :], zero], axis=0)
+        tail = ref[slot(chip), 64:96, :]
+        tails = jnp.concatenate([jnp.where(k, tail, jnp.zeros_like(tail)) for k in masks], axis=0)
+        rhs = jnp.concatenate([main, tails], axis=1)
+        total += lax.dot_general(lhs, rhs, (((1,), (1,)), ((), ())), preferred_element_type=F32)
+    return total
+
+
+def half_kernel(where, send_ref, recv_ref, out_ref):
+    out_ref[...] = vectors_of(send_ref, recv_ref, where[0] % 2)
+
+
+def vector_kernel(where, send_ref, other_ref, half_ref, out_ref):
+    total = half_ref[...] + vectors_of(send_ref, other_ref, 1 - where[0] % 2)
     for m in range(out_ref.shape[0]):
         out_ref[m] = total
 
@@ -357,6 +369,14 @@
     recv = lax.all_to_all(send, ("x", "y"), split_axis=0, concat_axis=0, tiled=True)
     siblings = [(0, 1), (1, 0)]
     other = lax.ppermute(recv, "core", siblings)
+    half_vec = pl.pallas_call(
+        half_kernel,
+        out_shape=jax.ShapeDtypeStruct((tok, LANE), F32),
+        in_specs=[SMEM, VMEM, VMEM],
+        out_specs=VMEM,
+        compiler_params=PARAMS,
+        name="half",
+    )(me, send, recv)
     vec_send = pl.pallas_call(
         vector_kernel,
         out_shape=jax.ShapeDtypeStruct((n_mp, tok, LANE), F32),
@@ -364,7 +384,7 @@
         out_specs=VMEM,
         compiler_params=PARAMS,
         name="vectors",
-    )(me, send, recv, other)
+    )(me, send, other, half_vec)
     vec = lax.all_to_all(vec_send, mp, split_axis=0, concat_axis=0, tiled=True)
     groups = [jax.ShapeDtypeStruct((blocks * n + blocks, LANE), F32) for n in PIECES]
     top, bottom, low = pl.pallas_call(

time: 137 us -> 137 us (level)
  the two profiles are of different devices: /device:TPU:60 before, /device:TPU:8 now
where the time goes in v7:
time: 137 us; the launch traced here: 136 us
  blocking collectives  48 us (35%)
  waiting for transfers between devices  32.2 us (24%)
  starting transfers between devices  23.3 us (17%)
  between operations  14.2 us (10%)
  Pallas kernels  12.9 us (9%)
  local copies, waits for them, and re-layouts  4.84 us (4%)
    all_to_all x1, waiting for transfers between devices, swap(): return lax.all_to_all(a, axes, split_axis=0, concat_axis=0, tiled=True)  22.2 us
    all_to_all x1, blocking collectives, shards(): lax.all_to_all(send, ('x', 'y'), split_axis=0, concat_axis=0, tiled=True)  21 us
    all_to_all x1, blocking collectives, shards(): vec = lax.all_to_all(vec_send, mp, split_axis=0, concat_axis=0, tiled=True)  15 us
    all_to_all x1, blocking collectives, swap(): return lax.all_to_all(a, axes, split_axis=0, concat_axis=0, tiled=True)  12.1 us
    ppermute x1, starting transfers between devices, shards(): got_bottom = lax.ppermute(bottom, dp, others)  10.5 us
    all_to_all x1, starting transfers between devices, swap(): return lax.all_to_all(a, axes, split_axis=0, concat_axis=0, tiled=True)  5.07 us
    reduce_scatter x1, waiting for transfers between devices, shards(): sums = lax.psum_scatter(sums, 'zh', scatter_dimension=0, tiled=True)  3.92 us
    ppermute x1, starting transfers between devices, shards(): got_top = lax.ppermute(top, dp, pairs)  3.88 us
  transfers between devices with their start and end apart: 6, of which 5 were waited for; matrix products, arithmetic and copies ran while one was open for 2% of the time, Pallas kernels for 4%

profile of v7, /device:TPU:8, one launch (start us, length us, event | category | flops | bytes accessed | tf_op | source)
XLA Modules:
  0.0 135.5 jit_solution(11374876339274384778)
XLA Ops:
  7.2 0.0 reduce-scatter.2.cloned.1.call-start
  7.2 2.8 %pack.1 = (bf16[16,224,128]{2,1,0:T(8,128)(2,1)S(1)}, bf16[32,2048]{1,0:T(8,128)(2,1)S(1)}, bf16[448,1024]{1,0:T(8,128)(2,1)S(1)}) custom-call(s32[1]{0:T(128)} %bitcast.1.where, s32[1,8]{1,0:T(1,128)} %tenants.5, s32[1,8]{1,0:T(1,128)} %counts_hbm.1, bf16[32,5120]{1,0:T(8,128)(2,1)} %x_hbm.1, bf16[32,1024]{1,0:T(8,128)(2,1)} %k_hbm.1, ...), custom_call_target="tpu_custom_call" | custom-call | tf_op jit(solution)/shard_map/pack/pallas_call | solution.py:337
  10.0 0.0 copy-start
  10.0 21.0 %all_to_all.20.recv_ref = bf16[16,224,128]{2,1,0:T(8,128)(2,1)S(1)} all-to-all(bf16[16,224,128]{2,1,0:T(8,128)(2,1)S(1)} %get-tuple-element.23.send_ref), channel_id=1, replica_groups=mesh['zh'=8,'zl'=2,'y'=4,'x'=4,'core'=2] {'x','y'}, dimensions={0} | all-to-all | bytes 1835008 | tf_op jit(solution)/shard_map/all_to_all | solution.py:369
  31.0 1.9 %collective-permute-start = (bf16[16,224,128]{2,1,0:T(8,128)(2,1)S(1)}, bf16[16,224,128]{2,1,0:T(8,128)(2,1)S(1)}, u32[]{:S(2)}, u32[]{:S(2)}) collective-permute-start(bf16[16,224,128]{2,1,0:T(8,128)(2,1)S(1)} %all_to_all.20.recv_ref), channel_id=1, source_target_pairs={{0,1},{1,0},{2,3},{3,2},{4,5},{5,4},{6,7},{7,6},{8,9},{9,8},{10,11... | collective-permute-start | bytes 2752520 | tf_op jit(solution)/shard_map/ppermute | solution.py:371
  32.9 0.4 half.1.half_ref
  33.3 0.0 copy-start.3
  33.3 2.0 %collective-permute-done.other_ref = bf16[16,224,128]{2,1,0:T(8,128)(2,1)S(1)} collective-permute-done((bf16[16,224,128]{2,1,0:T(8,128)(2,1)S(1)}, bf16[16,224,128]{2,1,0:T(8,128)(2,1)S(1)}, u32[]{:S(2)}, u32[]{:S(2)}) %collective-permute-start) | collective-permute-done | bytes 917536 | tf_op jit(solution)/shard_map/ppermute | solution.py:371
  35.4 0.5 vectors.1
  35.9 15.0 %all_to_all.21.vec_ref = f32[32,32,128]{2,1,0:T(8,128)S(1)} all-to-all(f32[32,32,128]{2,1,0:T(8,128)S(1)} %vectors.1), channel_id=1, replica_groups=mesh['zh'=8,'zl'=2,'y'=4,'x'=4,'core'=2] {'y','x','core'}, dimensions={0} | all-to-all | bytes 1048576 | tf_op jit(solution)/shard_map/all_to_all | solution.py:388
  50.9 0.0 copy-done.3
  50.9 0.9 parts.1
  51.8 3.9 %collective-permute-start.1 = (f32[520,128]{1,0:T(8,128)S(1)}, f32[520,128]{1,0:T(8,128)S(1)}, u32[]{:S(2)}, u32[]{:S(2)}) collective-permute-start(f32[520,128]{1,0:T(8,128)S(1)} %get-tuple-element.24.top_ref), channel_id=1, source_target_pairs={{0,32},{32,0},{64,96},{96,64},{128,160},{160,128},{192,224},{224,1... | collective-permute-start | bytes 798728 | tf_op jit(solution)/shard_map/ppermute | solution.py:403
  55.6 10.5 %collective-permute-start.2 = (f32[264,128]{1,0:T(8,128)S(1)}, f32[264,128]{1,0:T(8,128)S(1)}, u32[]{:S(2)}, u32[]{:S(2)}) collective-permute-start(f32[264,128]{1,0:T(8,128)S(1)} %get-tuple-element.25.bottom_ref), channel_id=1, source_target_pairs={{0,480},{32,64},{64,32},{96,128},{128,96},{160,192},{192,160},{224... | collective-permute-start | bytes 405512 | tf_op jit(solution)/shard_map/ppermute | solution.py:404
  66.1 2.6 %own.1.own_hbm = f32[32,96,128]{2,1,0:T(8,128)} custom-call(s32[1]{0:T(128)} %bitcast.plane, s32[1,8]{1,0:T(1,128)S(1)} %copy-done.3, f32[520,128]{1,0:T(8,128)S(1)} %get-tuple-element.24.top_ref, f32[264,128]{1,0:T(8,128)S(1)} %get-tuple-element.25.bottom_ref), custom_call_target="tpu_custom_call" | custom-call | tf_op jit(solution)/shard_map/own/pallas_call | solution.py:407
  68.7 0.0 collective-permute-done.1.got_top
  68.7 1.7 %collective-permute-done.2.got_bottom = f32[264,128]{1,0:T(8,128)S(1)} collective-permute-done((f32[264,128]{1,0:T(8,128)S(1)}, f32[264,128]{1,0:T(8,128)S(1)}, u32[]{:S(2)}, u32[]{:S(2)}) %collective-permute-start.2) | collective-permute-done | bytes 135200 | tf_op jit(solution)/shard_map/ppermute | solution.py:404
  70.4 1.7 %merge.1 = f32[32,96,128]{2,1,0:T(8,128)} custom-call(s32[1]{0:T(128)} %bitcast.plane, s32[1,8]{1,0:T(1,128)S(1)} %copy-done.3, f32[520,128]{1,0:T(8,128)S(1)} %get-tuple-element.24.top_ref, f32[264,128]{1,0:T(8,128)S(1)} %get-tuple-element.25.bottom_ref, f32[520,128]{1,0:T(8,128)S(1)} %collective-permute-done.1.got_top, ...), custom_call_target="tpu_custom_call", output_to_operand_aliasing={{}: (6, {})} | custom-call | tf_op jit(solution)/shard_map/merge/pallas_call | solution.py:422
  72.1 0.0 reduce-scatter.2.cloned.1.call-update
  72.1 1.6 %broadcast_in_dim.2 = bf16[16,32,2048]{2,1,0:T(8,128)(2,1)} broadcast(bf16[32,2048]{1,0:T(8,128)(2,1)S(1)} %get-tuple-element.30), dimensions={1,2} | broadcast | bytes 2228224 | tf_op jit(solution)/shard_map/broadcast_in_dim | solution.py:442
  73.7 5.1 %all-to-all-start.2 = ((bf16[16,32,2048]{2,1,0:T(8,128)(2,1)}), bf16[16,32,2048]{2,1,0:T(8,128)(2,1)S(1)}, u32[]{:S(2)}, u32[]{:S(2)}) async-start(bf16[16,32,2048]{2,1,0:T(8,128)(2,1)} %broadcast_in_dim.2), calls=%async_computation.3 | async-start | bytes 4194304 | tf_op jit(solution)/shard_map/all_to_all | solution.py:440
  78.8 0.0 copy-done
  78.8 1.9 %collective-permute-start.3 = (bf16[448,1024]{1,0:T(8,128)(2,1)S(1)}, bf16[448,1024]{1,0:T(8,128)(2,1)S(1)}, u32[]{:S(2)}, u32[]{:S(2)}) collective-permute-start(bf16[448,1024]{1,0:T(8,128)(2,1)S(1)} %get-tuple-element.31.near_ref), channel_id=1, source_target_pairs={{0,1},{1,0},{2,3},{3,2},{4,5},{5,4},{6,7},{7,6},{8,9},{9,8},{10,11... | collective-permute-start | bytes 2752520 | tf_op jit(solution)/shard_map/ppermute | solution.py:421
  80.7 2.4 %collective-permute-done.3.far_ref = bf16[448,1024]{1,0:T(8,128)(2,1)S(1)} collective-permute-done((bf16[448,1024]{1,0:T(8,128)(2,1)S(1)}, bf16[448,1024]{1,0:T(8,128)(2,1)S(1)}, u32[]{:S(2)}, u32[]{:S(2)}) %collective-permute-start.3) | collective-permute-done | bytes 917536 | tf_op jit(solution)/shard_map/ppermute | solution.py:421
  83.2 0.0 copy-start.1
  83.2 1.2 copy-done.1
  84.3 0.3 weights.1
  84.7 0.0 copy-start.2
  84.7 0.9 copy-done.2
  85.6 22.2 %all-to-all-done.2.kv_ref = bf16[16,32,2048]{2,1,0:T(8,128)(2,1)S(1)} async-done(((bf16[16,32,2048]{2,1,0:T(8,128)(2,1)}), bf16[16,32,2048]{2,1,0:T(8,128)(2,1)S(1)}, u32[]{:S(2)}, u32[]{:S(2)}) %all-to-all-start.2) | async-done | bytes 2097184 | tf_op jit(solution)/shard_map/all_to_all | solution.py:440
  107.8 2.0 %base.1 = bf16[16,32,320]{2,1,0:T(8,128)(2,1)S(1)} custom-call(bf16[16,32,2048]{2,1,0:T(8,128)(2,1)S(1)} %all-to-all-done.2.kv_ref, bf16[320,2048]{1,0:T(8,128)(2,1)S(1)} %get-tuple-element.32.w_ref, bf16[8,128,320]{2,1,0:T(8,128)(2,1)} %copy-done.2, bf16[16,32,128]{2,1,0:T(8,128)(2,1)S(1)} %get-tuple-element.34.low_ref), custom_call_target="tpu_custom_call" | custom-call | tf_op jit(solution)/shard_map/base/pallas_call | solution.py:454
  109.8 12.1 %all_to_all.22 = bf16[16,32,320]{2,1,0:T(8,128)(2,1)S(1)} all-to-all(bf16[16,32,320]{2,1,0:T(8,128)(2,1)S(1)} %base.1), channel_id=1, replica_groups=mesh['zh'=8,'zl'=2,'y'=4,'x'=4,'core'=2] {'y','x'}, dimensions={0} | all-to-all | bytes 655360 | tf_op jit(solution)/shard_map/all_to_all | solution.py:440
  121.9 0.1 copy.17
  122.0 1.0 reshape.22
  123.0 3.9 %reduce-scatter.2.cloned.1.call-done.sum_hbm = f32[4,96,128]{2,1,0:T(8,128)} async-done(((f32[32,96,128]{2,1,0:T(8,128)}), f32[4,96,128]{2,1,0:T(8,128)}) %reduce-scatter.2.cloned.1.call-update) | async-done | bytes 196624 | tf_op jit(solution)/shard_map/reduce_scatter | solution.py:437
  127.0 1.7 %finish.1 = (f32[4,32,160]{2,1,0:T(8,128)}, f32[4,32,160]{2,1,0:T(8,128)}, f32[4,32,32]{2,1,0:T(8,128)}, f32[4,32,32]{2,1,0:T(8,128)}) custom-call(f32[4,96,128]{2,1,0:T(8,128)} %reduce-scatter.2.cloned.1.call-done.sum_hbm), custom_call_target="tpu_custom_call" | custom-call | tf_op jit(solution)/shard_map/finish/pallas_call | solution.py:468
Async XLA Ops:
  7.2 119.8 %reduce-scatter.2.cloned.1.call-start = ((), (), s32[]{:S(2)}) async-start(), calls=%async_computation.5 | async-start | bytes 1769472 | tf_op jit(solution)/shard_map/reduce_scatter | solution.py:437
  10.0 68.8 %copy-start = (bf16[448,1024]{1,0:T(8,128)(2,1)}, bf16[448,1024]{1,0:T(8,128)(2,1)S(1)}, u32[]{:S(2)}) copy-start(bf16[448,1024]{1,0:T(8,128)(2,1)S(1)} %get-tuple-element.31.near_ref) | copy-start | bytes 2752516
  31.0 4.4 %collective-permute-start = (bf16[16,224,128]{2,1,0:T(8,128)(2,1)S(1)}, bf16[16,224,128]{2,1,0:T(8,128)(2,1)S(1)}, u32[]{:S(2)}, u32[]{:S(2)}) collective-permute-start(bf16[16,224,128]{2,1,0:T(8,128)(2,1)S(1)} %all_to_all.20.recv_ref), channel_id=1, source_target_pairs={{0,1},{1,0},{2,3},{3,2},{4,5},{5,4},{6,7},{7,6},{8,9},{9,8},{10,11... | collective-permute-start | bytes 2752520 | tf_op jit(solution)/shard_map/ppermute | solution.py:371
  33.3 17.5 %copy-start.3 = (s32[1,8]{1,0:T(1,128)S(1)}, s32[1,8]{1,0:T(1,128)}, u32[]{:S(2)}) copy-start(s32[1,8]{1,0:T(1,128)} %tenants.5) | copy-start | bytes 100
  51.8 17.0 %collective-permute-start.1 = (f32[520,128]{1,0:T(8,128)S(1)}, f32[520,128]{1,0:T(8,128)S(1)}, u32[]{:S(2)}, u32[]{:S(2)}) collective-permute-start(f32[520,128]{1,0:T(8,128)S(1)} %get-tuple-element.24.top_ref), channel_id=1, source_target_pairs={{0,32},{32,0},{64,96},{96,64},{128,160},{160,128},{192,224},{224,1... | collective-permute-start | bytes 798728 | tf_op jit(solution)/shard_map/ppermute | solution.py:403
  55.6 14.8 %collective-permute-start.2 = (f32[264,128]{1,0:T(8,128)S(1)}, f32[264,128]{1,0:T(8,128)S(1)}, u32[]{:S(2)}, u32[]{:S(2)}) collective-permute-start(f32[264,128]{1,0:T(8,128)S(1)} %get-tuple-element.25.bottom_ref), channel_id=1, source_target_pairs={{0,480},{32,64},{64,32},{96,128},{128,96},{160,192},{192,160},{224... | collective-permute-start | bytes 405512 | tf_op jit(solution)/shard_map/ppermute | solution.py:404
  73.7 34.1 %all-to-all-start.2 = ((bf16[16,32,2048]{2,1,0:T(8,128)(2,1)}), bf16[16,32,2048]{2,1,0:T(8,128)(2,1)S(1)}, u32[]{:S(2)}, u32[]{:S(2)}) async-start(bf16[16,32,2048]{2,1,0:T(8,128)(2,1)} %broadcast_in_dim.2), calls=%async_computation.3 | async-start | bytes 4194304 | tf_op jit(solution)/shard_map/all_to_all | solution.py:440
  78.8 4.4 %collective-permute-start.3 = (bf16[448,1024]{1,0:T(8,128)(2,1)S(1)}, bf16[448,1024]{1,0:T(8,128)(2,1)S(1)}, u32[]{:S(2)}, u32[]{:S(2)}) collective-permute-start(bf16[448,1024]{1,0:T(8,128)(2,1)S(1)} %get-tuple-element.31.near_ref), channel_id=1, source_target_pairs={{0,1},{1,0},{2,3},{3,2},{4,5},{5,4},{6,7},{7,6},{8,9},{9,8},{10,11... | collective-permute-start | bytes 2752520 | tf_op jit(solution)/shard_map/ppermute | solution.py:421
  83.2 1.2 copy-start.1
  84.7 0.9 copy-start.2
Sparse Core Ops, SparseCore 0:
  72.2 54.6 reduce-scatter.1

commit v8 on v7

--- a/solution.py
+++ b/solution.py
@@ -169,27 +169,37 @@
 PART = sum(PIECES)
 
 
-def parts_kernel(where, tenants, vec_ref, recv_ref, other_ref, top_ref, bottom_ref, low_ref):
+def block_product(vec_ref, recv_ref, core, b):
+    vec, near, far = [], [], []
+    for chip in (2 * b, 2 * b + 1):
+        vec.append(vec_ref[slot(chip)] * SCALE)
+        first_part, last_part = tokens_of(recv_ref, chip, core)
+        near.append(first_part)
+        far.append(last_part)
+    lhs = jnp.concatenate(split(jnp.concatenate(vec, axis=0)), axis=0)
+    rhs = jnp.concatenate([jnp.concatenate(near, axis=0), jnp.concatenate(far, axis=0)], axis=1)
+    rhs = jnp.concatenate([rhs, rhs], axis=0)
+    return lax.dot_general(lhs, rhs, (((0,), (0,)), ((), ())), preferred_element_type=F32)
+
+
+def half_parts_kernel(where, vec_ref, recv_ref, out_ref, low_ref):
     core = where[0] % 2
-    blocks = vec_ref.shape[0] // 4
+    for b in range(out_ref.shape[0]):
+        out_ref[b] = block_product(vec_ref, recv_ref, core, b)
+    for chip in range(low_ref.shape[0]):
+        back = vec_ref[slot(chip)][:, 64:] * SCALE
+        low_ref[chip] = jnp.concatenate(split(back), axis=1)
+
+
+def parts_kernel(where, tenants, vec_ref, recv_ref, half_ref, top_ref, bottom_ref):
+    core = where[0] % 2
+    blocks = half_ref.shape[0]
     m0, m1, m2, m3 = [lane_mask(32, s) for s in range(4)]
     first = first_blocks(tenants, blocks)
     top_ref[...] = jnp.zeros_like(top_ref)
     bottom_ref[...] = jnp.zeros_like(bottom_ref)
     for b in range(blocks):
-        vec, near, far = [], [], []
-        for chip in (2 * b, 2 * b + 1):
-            for ref, c in ((recv_ref, core), (other_ref, 1 - core)):
-                vec.append(vec_ref[2 * chip + c] * SCALE)
-                first_part, last_part = tokens_of(ref, chip, core)
-                near.append(first_part)
-                far.append(last_part)
-        lhs = jnp.concatenate(split(jnp.concatenate(vec, axis=0)), axis=0)
-        near = jnp.concatenate(near, axis=0)
-        far = jnp.concatenate(far, axis=0)
-        rhs = jnp.concatenate([near, far], axis=1)
-        rhs = jnp.concatenate([rhs, rhs], axis=0)
-        p = lax.dot_general(lhs, rhs, (((0,), (0,)), ((), ())), preferred_element_type=F32)
+        p = half_ref[b] + block_product(vec_ref, recv_ref, core, b)
         q = p[:, LANE:]
         tail = jnp.where(m0, q[64:96], jnp.where(m1, q[0:32], jnp.where(m2, q[96:128], q[32:64])))
         top_ref[pl.ds(pl.multiple_of(first[b] * 64, 8), 64), :] += p[64:128, :LANE]
@@ -200,9 +210,6 @@
         ids = jnp.where((row == b) & (first[b] == b), tenants[0, b], ids)
     top_ref[blocks * 64 :, :] = ids.astype(F32)
     bottom_ref[blocks * 32 :, :] = ids.astype(F32)
-    for i in range(low_ref.shape[0]):
-        back = vec_ref[2 * i + core][:, 64:] * SCALE
-        low_ref[i] = jnp.concatenate(split(back), axis=1)
 
 
 def kept(tenant, parity):
@@ -379,22 +386,34 @@
     )(me, send, recv)
     vec_send = pl.pallas_call(
         vector_kernel,
-        out_shape=jax.ShapeDtypeStruct((n_mp, tok, LANE), F32),
+        out_shape=jax.ShapeDtypeStruct((n_mp // 2, tok, LANE), F32),
         in_specs=[SMEM, VMEM, VMEM, VMEM],
         out_specs=VMEM,
         compiler_params=PARAMS,
         name="vectors",
     )(me, send, other, half_vec)
-    vec = lax.all_to_all(vec_send, mp, split_axis=0, concat_axis=0, tiled=True)
+    vec = lax.all_to_all(vec_send, ("x", "y"), split_axis=0, concat_axis=0, tiled=True)
+    other_vec = lax.ppermute(vec, "core", siblings)
+    half_parts, low = pl.pallas_call(
+        half_parts_kernel,
+        out_shape=(
+            jax.ShapeDtypeStruct((blocks, LANE, 2 * LANE), F32),
+            jax.ShapeDtypeStruct((n_mp // 2, tok, LANE), BF16),
+        ),
+        in_specs=[SMEM, VMEM, VMEM],
+        out_specs=(VMEM, VMEM),
+        compiler_params=PARAMS,
+        name="half_parts",
+    )(me, vec, recv)
     groups = [jax.ShapeDtypeStruct((blocks * n + blocks, LANE), F32) for n in PIECES]
-    top, bottom, low = pl.pallas_call(
+    top, bottom = pl.pallas_call(
         parts_kernel,
-        out_shape=(*groups, jax.ShapeDtypeStruct((n_mp // 2, tok, LANE), BF16)),
+        out_shape=tuple(groups),
         in_specs=[SMEM, SMEM, VMEM, VMEM, VMEM],
-        out_specs=(VMEM, VMEM, VMEM),
+        out_specs=(VMEM, VMEM),
         compiler_params=PARAMS,
         name="parts",
-    )(me, tenant_of_block, vec, recv, other)
+    )(me, tenant_of_block, other_vec, other, half_parts)
 
     dp = ("zh", "zl")
     n_dp = lax.axis_size(dp)

time: 137 us -> 137 us (level)
  the two profiles are of different devices: /device:TPU:8 before, /device:TPU:34 now
where the time goes in v8:
time: 137 us
  blocking collectives  48.1 us (35%)
  waiting for transfers between devices  37.4 us (27%)
  starting transfers between devices  18.8 us (14%)
  between operations  14.2 us (10%)
  Pallas kernels  13.3 us (10%)
  local copies, waits for them, and re-layouts  4.81 us (4%)
    all_to_all x1, blocking collectives, shards(): lax.all_to_all(send, ('x', 'y'), split_axis=0, concat_axis=0, tiled=True)  20.9 us
    all_to_all x1, waiting for transfers between devices, swap(): return lax.all_to_all(a, axes, split_axis=0, concat_axis=0, tiled=True)  20.1 us
    all_to_all x1, blocking collectives, swap(): return lax.all_to_all(a, axes, split_axis=0, concat_axis=0, tiled=True)  14.7 us
    all_to_all x1, blocking collectives, shards(): lax.all_to_all(vec_send, ('x', 'y'), split_axis=0, concat_axis=0, tiled=T...  12.5 us
    reduce_scatter x1, waiting for transfers between devices, shards(): sums = lax.psum_scatter(sums, 'zh', scatter_dimension=0, tiled=True)  10.8 us
    ppermute x1, starting transfers between devices, shards(): got_bottom = lax.ppermute(bottom, dp, others)  5.68 us
    all_to_all x1, starting transfers between devices, swap(): return lax.all_to_all(a, axes, split_axis=0, concat_axis=0, tiled=True)  5.35 us
    pallas_call x1, Pallas kernels, shards(): pl.pallas_call(pack_kernel, out_shape=(jax.ShapeDtypeStruct((n_mp // 2, P...  2.75 us
  transfers between devices with their start and end apart: 7, of which 6 were waited for; matrix products, arithmetic and copies ran while one was open for 2% of the time, Pallas kernels for 4%

profile of v8, /device:TPU:34, one launch (start us, length us, event | category | flops | bytes accessed | tf_op | source)
XLA Modules:
  0.0 136.5 jit_solution(9030567882141796878)
XLA Ops:
  7.2 0.0 reduce-scatter.2.cloned.1.call-start
  7.2 2.8 %pack.1 = (bf16[16,224,128]{2,1,0:T(8,128)(2,1)S(1)}, bf16[32,2048]{1,0:T(8,128)(2,1)S(1)}, bf16[448,1024]{1,0:T(8,128)(2,1)S(1)}) custom-call(s32[1]{0:T(128)} %bitcast.1.where, s32[1,8]{1,0:T(1,128)} %tenants.5, s32[1,8]{1,0:T(1,128)} %counts_hbm.1, bf16[32,5120]{1,0:T(8,128)(2,1)} %x_hbm.1, bf16[32,1024]{1,0:T(8,128)(2,1)} %k_hbm.1, ...), custom_call_target="tpu_custom_call" | custom-call | tf_op jit(solution)/shard_map/pack/pallas_call | solution.py:344
  10.0 0.0 copy-start
  10.0 20.9 %all_to_all.20.recv_ref = bf16[16,224,128]{2,1,0:T(8,128)(2,1)S(1)} all-to-all(bf16[16,224,128]{2,1,0:T(8,128)(2,1)S(1)} %get-tuple-element.24.send_ref), channel_id=1, replica_groups=mesh['zh'=8,'zl'=2,'y'=4,'x'=4,'core'=2] {'x','y'}, dimensions={0} | all-to-all | bytes 1835008 | tf_op jit(solution)/shard_map/all_to_all | solution.py:376
  30.9 1.9 %collective-permute-start = (bf16[16,224,128]{2,1,0:T(8,128)(2,1)S(1)}, bf16[16,224,128]{2,1,0:T(8,128)(2,1)S(1)}, u32[]{:S(2)}, u32[]{:S(2)}) collective-permute-start(bf16[16,224,128]{2,1,0:T(8,128)(2,1)S(1)} %all_to_all.20.recv_ref), channel_id=1, source_target_pairs={{0,1},{1,0},{2,3},{3,2},{4,5},{5,4},{6,7},{7,6},{8,9},{9,8},{10,11... | collective-permute-start | bytes 2752520 | tf_op jit(solution)/shard_map/ppermute | solution.py:378
  32.8 0.4 half.1.half_ref
  33.2 0.0 copy-start.3
  33.2 2.0 %collective-permute-done.other_ref.recv_ref = bf16[16,224,128]{2,1,0:T(8,128)(2,1)S(1)} collective-permute-done((bf16[16,224,128]{2,1,0:T(8,128)(2,1)S(1)}, bf16[16,224,128]{2,1,0:T(8,128)(2,1)S(1)}, u32[]{:S(2)}, u32[]{:S(2)}) %collective-permute-start) | collective-permute-done | bytes 917536 | tf_op jit(solution)/shard_map/ppermute | solution.py:378
  35.2 0.5 vectors.1
  35.7 12.5 %all_to_all.21.vec_ref = f32[16,32,128]{2,1,0:T(8,128)S(1)} all-to-all(f32[16,32,128]{2,1,0:T(8,128)S(1)} %vectors.1), channel_id=1, replica_groups=mesh['zh'=8,'zl'=2,'y'=4,'x'=4,'core'=2] {'x','y'}, dimensions={0} | all-to-all | bytes 524288 | tf_op jit(solution)/shard_map/all_to_all | solution.py:395
  48.2 1.9 %collective-permute-start.1 = (f32[16,32,128]{2,1,0:T(8,128)S(1)}, f32[16,32,128]{2,1,0:T(8,128)S(1)}, u32[]{:S(2)}, u32[]{:S(2)}) collective-permute-start(f32[16,32,128]{2,1,0:T(8,128)S(1)} %all_to_all.21.vec_ref), channel_id=1, source_target_pairs={{0,1},{1,0},{2,3},{3,2},{4,5},{5,4},{6,7},{7,6},{8,9},{9,8},{10,11... | collective-permute-start | bytes 786440 | tf_op jit(solution)/shard_map/ppermute | solution.py:396
  50.1 0.3 half_parts.1
  50.5 1.2 collective-permute-done.1.vec_ref
  51.6 0.0 copy-done.3
  51.6 0.9 parts.1
  52.5 2.0 %collective-permute-start.2 = (f32[520,128]{1,0:T(8,128)S(1)}, f32[520,128]{1,0:T(8,128)S(1)}, u32[]{:S(2)}, u32[]{:S(2)}) collective-permute-start(f32[520,128]{1,0:T(8,128)S(1)} %get-tuple-element.26.top_ref), channel_id=1, source_target_pairs={{0,32},{32,0},{64,96},{96,64},{128,160},{160,128},{192,224},{224,1... | collective-permute-start | bytes 798728 | tf_op jit(solution)/shard_map/ppermute | solution.py:422
  54.5 5.7 %collective-permute-start.3 = (f32[264,128]{1,0:T(8,128)S(1)}, f32[264,128]{1,0:T(8,128)S(1)}, u32[]{:S(2)}, u32[]{:S(2)}) collective-permute-start(f32[264,128]{1,0:T(8,128)S(1)} %get-tuple-element.27.bottom_ref), channel_id=1, source_target_pairs={{0,480},{32,64},{64,32},{96,128},{128,96},{160,192},{192,160},{224... | collective-permute-start | bytes 405512 | tf_op jit(solution)/shard_map/ppermute | solution.py:423
  60.2 2.6 %own.1.own_hbm = f32[32,96,128]{2,1,0:T(8,128)} custom-call(s32[1]{0:T(128)} %bitcast.plane, s32[1,8]{1,0:T(1,128)S(1)} %copy-done.3, f32[520,128]{1,0:T(8,128)S(1)} %get-tuple-element.26.top_ref, f32[264,128]{1,0:T(8,128)S(1)} %get-tuple-element.27.bottom_ref), custom_call_target="tpu_custom_call" | custom-call | tf_op jit(solution)/shard_map/own/pallas_call | solution.py:426
  62.9 0.0 collective-permute-done.2.got_top
  62.9 0.9 collective-permute-done.3.got_bottom
  63.8 1.6 %merge.1 = f32[32,96,128]{2,1,0:T(8,128)} custom-call(s32[1]{0:T(128)} %bitcast.plane, s32[1,8]{1,0:T(1,128)S(1)} %copy-done.3, f32[520,128]{1,0:T(8,128)S(1)} %get-tuple-element.26.top_ref, f32[264,128]{1,0:T(8,128)S(1)} %get-tuple-element.27.bottom_ref, f32[520,128]{1,0:T(8,128)S(1)} %collective-permute-done.2.got_top, ...), custom_call_target="tpu_custom_call", output_to_operand_aliasing={{}: (6, {})} | custom-call | tf_op jit(solution)/shard_map/merge/pallas_call | solution.py:441
  65.5 0.0 reduce-scatter.2.cloned.1.call-update
  65.5 1.6 %broadcast_in_dim.2 = bf16[16,32,2048]{2,1,0:T(8,128)(2,1)} broadcast(bf16[32,2048]{1,0:T(8,128)(2,1)S(1)} %get-tuple-element.32), dimensions={1,2} | broadcast | bytes 2228224 | tf_op jit(solution)/shard_map/broadcast_in_dim | solution.py:461
  67.1 5.3 %all-to-all-start.2 = ((bf16[16,32,2048]{2,1,0:T(8,128)(2,1)}), bf16[16,32,2048]{2,1,0:T(8,128)(2,1)S(1)}, u32[]{:S(2)}, u32[]{:S(2)}) async-start(bf16[16,32,2048]{2,1,0:T(8,128)(2,1)} %broadcast_in_dim.2), calls=%async_computation.3 | async-start | bytes 4194304 | tf_op jit(solution)/shard_map/all_to_all | solution.py:459
  72.4 0.0 copy-done
  72.4 1.9 %collective-permute-start.4 = (bf16[448,1024]{1,0:T(8,128)(2,1)S(1)}, bf16[448,1024]{1,0:T(8,128)(2,1)S(1)}, u32[]{:S(2)}, u32[]{:S(2)}) collective-permute-start(bf16[448,1024]{1,0:T(8,128)(2,1)S(1)} %get-tuple-element.33.near_ref), channel_id=1, source_target_pairs={{0,1},{1,0},{2,3},{3,2},{4,5},{5,4},{6,7},{7,6},{8,9},{9,8},{10,11... | collective-permute-start | bytes 2752520 | tf_op jit(solution)/shard_map/ppermute | solution.py:440
  74.3 2.4 %collective-permute-done.4.far_ref = bf16[448,1024]{1,0:T(8,128)(2,1)S(1)} collective-permute-done((bf16[448,1024]{1,0:T(8,128)(2,1)S(1)}, bf16[448,1024]{1,0:T(8,128)(2,1)S(1)}, u32[]{:S(2)}, u32[]{:S(2)}) %collective-permute-start.4) | collective-permute-done | bytes 917536 | tf_op jit(solution)/shard_map/ppermute | solution.py:440
  76.8 0.0 copy-start.1
  76.8 1.2 copy-done.1
  78.0 0.3 weights.1
  78.3 0.0 copy-start.2
  78.3 0.9 copy-done.2
  79.2 20.1 %all-to-all-done.2.kv_ref = bf16[16,32,2048]{2,1,0:T(8,128)(2,1)S(1)} async-done(((bf16[16,32,2048]{2,1,0:T(8,128)(2,1)}), bf16[16,32,2048]{2,1,0:T(8,128)(2,1)S(1)}, u32[]{:S(2)}, u32[]{:S(2)}) %all-to-all-start.2) | async-done | bytes 2097184 | tf_op jit(solution)/shard_map/all_to_all | solution.py:459
  99.3 2.0 %base.1 = bf16[16,32,320]{2,1,0:T(8,128)(2,1)S(1)} custom-call(bf16[16,32,2048]{2,1,0:T(8,128)(2,1)S(1)} %all-to-all-done.2.kv_ref, bf16[320,2048]{1,0:T(8,128)(2,1)S(1)} %get-tuple-element.34.w_ref, bf16[8,128,320]{2,1,0:T(8,128)(2,1)} %copy-done.2, bf16[16,32,128]{2,1,0:T(8,128)(2,1)S(1)} %get-tuple-element.36.low_ref), custom_call_target="tpu_custom_call" | custom-call | tf_op jit(solution)/shard_map/base/pallas_call | solution.py:473
  101.3 14.7 %all_to_all.22 = bf16[16,32,320]{2,1,0:T(8,128)(2,1)S(1)} all-to-all(bf16[16,32,320]{2,1,0:T(8,128)(2,1)S(1)} %base.1), channel_id=1, replica_groups=mesh['zh'=8,'zl'=2,'y'=4,'x'=4,'core'=2] {'y','x'}, dimensions={0} | all-to-all | bytes 655360 | tf_op jit(solution)/shard_map/all_to_all | solution.py:459
  116.0 0.1 copy.17
  116.2 1.0 reshape.22
  117.2 10.8 %reduce-scatter.2.cloned.1.call-done.sum_hbm = f32[4,96,128]{2,1,0:T(8,128)} async-done(((f32[32,96,128]{2,1,0:T(8,128)}), f32[4,96,128]{2,1,0:T(8,128)}) %reduce-scatter.2.cloned.1.call-update) | async-done | bytes 196624 | tf_op jit(solution)/shard_map/reduce_scatter | solution.py:456
  128.0 1.7 %finish.1 = (f32[4,32,160]{2,1,0:T(8,128)}, f32[4,32,160]{2,1,0:T(8,128)}, f32[4,32,32]{2,1,0:T(8,128)}, f32[4,32,32]{2,1,0:T(8,128)}) custom-call(f32[4,96,128]{2,1,0:T(8,128)} %reduce-scatter.2.cloned.1.call-done.sum_hbm), custom_call_target="tpu_custom_call" | custom-call | tf_op jit(solution)/shard_map/finish/pallas_call | solution.py:487
Async XLA Ops:
  7.2 120.8 %reduce-scatter.2.cloned.1.call-start = ((), (), s32[]{:S(2)}) async-start(), calls=%async_computation.5 | async-start | bytes 1769472 | tf_op jit(solution)/shard_map/reduce_scatter | solution.py:456
  10.0 62.4 %copy-start = (bf16[448,1024]{1,0:T(8,128)(2,1)}, bf16[448,1024]{1,0:T(8,128)(2,1)S(1)}, u32[]{:S(2)}) copy-start(bf16[448,1024]{1,0:T(8,128)(2,1)S(1)} %get-tuple-element.33.near_ref) | copy-start | bytes 2752516
  30.9 4.4 %collective-permute-start = (bf16[16,224,128]{2,1,0:T(8,128)(2,1)S(1)}, bf16[16,224,128]{2,1,0:T(8,128)(2,1)S(1)}, u32[]{:S(2)}, u32[]{:S(2)}) collective-permute-start(bf16[16,224,128]{2,1,0:T(8,128)(2,1)S(1)} %all_to_all.20.recv_ref), channel_id=1, source_target_pairs={{0,1},{1,0},{2,3},{3,2},{4,5},{5,4},{6,7},{7,6},{8,9},{9,8},{10,11... | collective-permute-start | bytes 2752520 | tf_op jit(solution)/shard_map/ppermute | solution.py:378
  33.2 18.4 %copy-start.3 = (s32[1,8]{1,0:T(1,128)S(1)}, s32[1,8]{1,0:T(1,128)}, u32[]{:S(2)}) copy-start(s32[1,8]{1,0:T(1,128)} %tenants.5) | copy-start | bytes 100
  48.2 3.4 %collective-permute-start.1 = (f32[16,32,128]{2,1,0:T(8,128)S(1)}, f32[16,32,128]{2,1,0:T(8,128)S(1)}, u32[]{:S(2)}, u32[]{:S(2)}) collective-permute-start(f32[16,32,128]{2,1,0:T(8,128)S(1)} %all_to_all.21.vec_ref), channel_id=1, source_target_pairs={{0,1},{1,0},{2,3},{3,2},{4,5},{5,4},{6,7},{7,6},{8,9},{9,8},{10,11... | collective-permute-start | bytes 786440 | tf_op jit(solution)/shard_map/ppermute | solution.py:396
  52.5 10.3 %collective-permute-start.2 = (f32[520,128]{1,0:T(8,128)S(1)}, f32[520,128]{1,0:T(8,128)S(1)}, u32[]{:S(2)}, u32[]{:S(2)}) collective-permute-start(f32[520,128]{1,0:T(8,128)S(1)} %get-tuple-element.26.top_ref), channel_id=1, source_target_pairs={{0,32},{32,0},{64,96},{96,64},{128,160},{160,128},{192,224},{224,1... | collective-permute-start | bytes 798728 | tf_op jit(solution)/shard_map/ppermute | solution.py:422
  54.5 9.3 %collective-permute-start.3 = (f32[264,128]{1,0:T(8,128)S(1)}, f32[264,128]{1,0:T(8,128)S(1)}, u32[]{:S(2)}, u32[]{:S(2)}) collective-permute-start(f32[264,128]{1,0:T(8,128)S(1)} %get-tuple-element.27.bottom_ref), channel_id=1, source_target_pairs={{0,480},{32,64},{64,32},{96,128},{128,96},{160,192},{192,160},{224... | collective-permute-start | bytes 405512 | tf_op jit(solution)/shard_map/ppermute | solution.py:423
  67.1 32.2 %all-to-all-start.2 = ((bf16[16,32,2048]{2,1,0:T(8,128)(2,1)}), bf16[16,32,2048]{2,1,0:T(8,128)(2,1)S(1)}, u32[]{:S(2)}, u32[]{:S(2)}) async-start(bf16[16,32,2048]{2,1,0:T(8,128)(2,1)} %broadcast_in_dim.2), calls=%async_computation.3 | async-start | bytes 4194304 | tf_op jit(solution)/shard_map/all_to_all | solution.py:459
  72.4 4.4 %collective-permute-start.4 = (bf16[448,1024]{1,0:T(8,128)(2,1)S(1)}, bf16[448,1024]{1,0:T(8,128)(2,1)S(1)}, u32[]{:S(2)}, u32[]{:S(2)}) collective-permute-start(bf16[448,1024]{1,0:T(8,128)(2,1)S(1)} %get-tuple-element.33.near_ref), channel_id=1, source_target_pairs={{0,1},{1,0},{2,3},{3,2},{4,5},{5,4},{6,7},{7,6},{8,9},{9,8},{10,11... | collective-permute-start | bytes 2752520 | tf_op jit(solution)/shard_map/ppermute | solution.py:440
  76.8 1.2 copy-start.1
  78.3 0.9 copy-start.2
Sparse Core Ops, SparseCore 0:
  65.6 62.3 reduce-scatter.1

commit v9 on v8

--- a/solution.py
+++ b/solution.py
@@ -179,13 +179,19 @@
     lhs = jnp.concatenate(split(jnp.concatenate(vec, axis=0)), axis=0)
     rhs = jnp.concatenate([jnp.concatenate(near, axis=0), jnp.concatenate(far, axis=0)], axis=1)
     rhs = jnp.concatenate([rhs, rhs], axis=0)
-    return lax.dot_general(lhs, rhs, (((0,), (0,)), ((), ())), preferred_element_type=F32)
+    p = lax.dot_general(lhs, rhs, (((0,), (0,)), ((), ())), preferred_element_type=F32)
+    m0, m1, m2, _ = [lane_mask(32, s) for s in range(4)]
+    q = p[:, LANE:]
+    tail = jnp.where(m0, q[64:96], jnp.where(m1, q[0:32], jnp.where(m2, q[96:128], q[32:64])))
+    return p[64:128, :LANE], tail
 
 
 def half_parts_kernel(where, vec_ref, recv_ref, out_ref, low_ref):
     core = where[0] % 2
     for b in range(out_ref.shape[0]):
-        out_ref[b] = block_product(vec_ref, recv_ref, core, b)
+        main, tail = block_product(vec_ref, recv_ref, core, b)
+        out_ref[b, 0:64, :] = main
+        out_ref[b, 64:96, :] = tail
     for chip in range(low_ref.shape[0]):
         back = vec_ref[slot(chip)][:, 64:] * SCALE
         low_ref[chip] = jnp.concatenate(split(back), axis=1)
@@ -194,16 +200,13 @@
 def parts_kernel(where, tenants, vec_ref, recv_ref, half_ref, top_ref, bottom_ref):
     core = where[0] % 2
     blocks = half_ref.shape[0]
-    m0, m1, m2, m3 = [lane_mask(32, s) for s in range(4)]
     first = first_blocks(tenants, blocks)
     top_ref[...] = jnp.zeros_like(top_ref)
     bottom_ref[...] = jnp.zeros_like(bottom_ref)
     for b in range(blocks):
-        p = half_ref[b] + block_product(vec_ref, recv_ref, core, b)
-        q = p[:, LANE:]
-        tail = jnp.where(m0, q[64:96], jnp.where(m1, q[0:32], jnp.where(m2, q[96:128], q[32:64])))
-        top_ref[pl.ds(pl.multiple_of(first[b] * 64, 8), 64), :] += p[64:128, :LANE]
-        bottom_ref[pl.ds(pl.multiple_of(first[b] * 32, 8), 32), :] += tail
+        main, tail = block_product(vec_ref, recv_ref, core, b)
+        top_ref[pl.ds(pl.multiple_of(first[b] * 64, 8), 64), :] += half_ref[b, 0:64, :] + main
+        bottom_ref[pl.ds(pl.multiple_of(first[b] * 32, 8), 32), :] += half_ref[b, 64:96, :] + tail
     row = lax.broadcasted_iota(jnp.int32, (blocks, LANE), 0)
     ids = jnp.full((blocks, LANE), -1, jnp.int32)
     for b in range(blocks):
@@ -397,7 +400,7 @@
     half_parts, low = pl.pallas_call(
         half_parts_kernel,
         out_shape=(
-            jax.ShapeDtypeStruct((blocks, LANE, 2 * LANE), F32),
+            jax.ShapeDtypeStruct((blocks, PART, LANE), F32),
             jax.ShapeDtypeStruct((n_mp // 2, tok, LANE), BF16),
         ),
         in_specs=[SMEM, VMEM, VMEM],

time: 137 us -> 137 us (level)
  the two profiles are of different devices: /device:TPU:34 before, /device:TPU:40 now
where the time goes in v9:
time: 137 us
  blocking collectives  45.8 us (33%)
  waiting for transfers between devices  40 us (29%)
  starting transfers between devices  18.5 us (14%)
  between operations  14.2 us (10%)
  Pallas kernels  13.2 us (10%)
  local copies, waits for them, and re-layouts  4.81 us (4%)
    all_to_all x1, waiting for transfers between devices, swap(): return lax.all_to_all(a, axes, split_axis=0, concat_axis=0, tiled=True)  21.8 us
    all_to_all x1, blocking collectives, shards(): lax.all_to_all(send, ('x', 'y'), split_axis=0, concat_axis=0, tiled=True)  21 us
    all_to_all x1, blocking collectives, shards(): lax.all_to_all(vec_send, ('x', 'y'), split_axis=0, concat_axis=0, tiled=T...  12.5 us
    all_to_all x1, blocking collectives, swap(): return lax.all_to_all(a, axes, split_axis=0, concat_axis=0, tiled=True)  12.2 us
    reduce_scatter x1, waiting for transfers between devices, shards(): sums = lax.psum_scatter(sums, 'zh', scatter_dimension=0, tiled=True)  11.6 us
    ppermute x1, starting transfers between devices, shards(): got_bottom = lax.ppermute(bottom, dp, others)  5.68 us
    all_to_all x1, starting transfers between devices, swap(): return lax.all_to_all(a, axes, split_axis=0, concat_axis=0, tiled=True)  5.11 us
    pallas_call x1, Pallas kernels, shards(): pl.pallas_call(pack_kernel, out_shape=(jax.ShapeDtypeStruct((n_mp // 2, P...  2.75 us
  transfers between devices with their start and end apart: 7, of which 7 were waited for; matrix products, arithmetic and copies ran while one was open for 2% of the time, Pallas kernels for 4%

profile of v9, /device:TPU:40, one launch (start us, length us, event | category | flops | bytes accessed | tf_op | source)
XLA Modules:
  0.0 136.5 jit_solution(15008745232538346954)
XLA Ops:
  7.2 0.0 reduce-scatter.2.cloned.1.call-start
  7.2 2.8 %pack.1 = (bf16[16,224,128]{2,1,0:T(8,128)(2,1)S(1)}, bf16[32,2048]{1,0:T(8,128)(2,1)S(1)}, bf16[448,1024]{1,0:T(8,128)(2,1)S(1)}) custom-call(s32[1]{0:T(128)} %bitcast.1.where, s32[1,8]{1,0:T(1,128)} %tenants.5, s32[1,8]{1,0:T(1,128)} %counts_hbm.1, bf16[32,5120]{1,0:T(8,128)(2,1)} %x_hbm.1, bf16[32,1024]{1,0:T(8,128)(2,1)} %k_hbm.1, ...), custom_call_target="tpu_custom_call" | custom-call | tf_op jit(solution)/shard_map/pack/pallas_call | solution.py:347
  10.0 0.0 copy-start
  10.0 21.0 %all_to_all.20.recv_ref = bf16[16,224,128]{2,1,0:T(8,128)(2,1)S(1)} all-to-all(bf16[16,224,128]{2,1,0:T(8,128)(2,1)S(1)} %get-tuple-element.24.send_ref), channel_id=1, replica_groups=mesh['zh'=8,'zl'=2,'y'=4,'x'=4,'core'=2] {'x','y'}, dimensions={0} | all-to-all | bytes 1835008 | tf_op jit(solution)/shard_map/all_to_all | solution.py:379
  31.0 1.9 %collective-permute-start = (bf16[16,224,128]{2,1,0:T(8,128)(2,1)S(1)}, bf16[16,224,128]{2,1,0:T(8,128)(2,1)S(1)}, u32[]{:S(2)}, u32[]{:S(2)}) collective-permute-start(bf16[16,224,128]{2,1,0:T(8,128)(2,1)S(1)} %all_to_all.20.recv_ref), channel_id=1, source_target_pairs={{0,1},{1,0},{2,3},{3,2},{4,5},{5,4},{6,7},{7,6},{8,9},{9,8},{10,11... | collective-permute-start | bytes 2752520 | tf_op jit(solution)/shard_map/ppermute | solution.py:381
  32.9 0.4 half.1.half_ref
  33.3 0.0 copy-start.3
  33.3 2.0 %collective-permute-done.other_ref.recv_ref = bf16[16,224,128]{2,1,0:T(8,128)(2,1)S(1)} collective-permute-done((bf16[16,224,128]{2,1,0:T(8,128)(2,1)S(1)}, bf16[16,224,128]{2,1,0:T(8,128)(2,1)S(1)}, u32[]{:S(2)}, u32[]{:S(2)}) %collective-permute-start) | collective-permute-done | bytes 917536 | tf_op jit(solution)/shard_map/ppermute | solution.py:381
  35.4 0.5 vectors.1
  35.8 12.5 %all_to_all.21.vec_ref = f32[16,32,128]{2,1,0:T(8,128)S(1)} all-to-all(f32[16,32,128]{2,1,0:T(8,128)S(1)} %vectors.1), channel_id=1, replica_groups=mesh['zh'=8,'zl'=2,'y'=4,'x'=4,'core'=2] {'x','y'}, dimensions={0} | all-to-all | bytes 524288 | tf_op jit(solution)/shard_map/all_to_all | solution.py:398
  48.4 1.9 %collective-permute-start.1 = (f32[16,32,128]{2,1,0:T(8,128)S(1)}, f32[16,32,128]{2,1,0:T(8,128)S(1)}, u32[]{:S(2)}, u32[]{:S(2)}) collective-permute-start(f32[16,32,128]{2,1,0:T(8,128)S(1)} %all_to_all.21.vec_ref), channel_id=1, source_target_pairs={{0,1},{1,0},{2,3},{3,2},{4,5},{5,4},{6,7},{7,6},{8,9},{9,8},{10,11... | collective-permute-start | bytes 786440 | tf_op jit(solution)/shard_map/ppermute | solution.py:399
  50.3 0.3 half_parts.1
  50.6 1.2 collective-permute-done.1.vec_ref
  51.8 0.0 copy-done.3
  51.8 0.9 parts.1
  52.7 2.0 %collective-permute-start.2 = (f32[520,128]{1,0:T(8,128)S(1)}, f32[520,128]{1,0:T(8,128)S(1)}, u32[]{:S(2)}, u32[]{:S(2)}) collective-permute-start(f32[520,128]{1,0:T(8,128)S(1)} %get-tuple-element.26.top_ref), channel_id=1, source_target_pairs={{0,32},{32,0},{64,96},{96,64},{128,160},{160,128},{192,224},{224,1... | collective-permute-start | bytes 798728 | tf_op jit(solution)/shard_map/ppermute | solution.py:425
  54.7 5.7 %collective-permute-start.3 = (f32[264,128]{1,0:T(8,128)S(1)}, f32[264,128]{1,0:T(8,128)S(1)}, u32[]{:S(2)}, u32[]{:S(2)}) collective-permute-start(f32[264,128]{1,0:T(8,128)S(1)} %get-tuple-element.27.bottom_ref), channel_id=1, source_target_pairs={{0,480},{32,64},{64,32},{96,128},{128,96},{160,192},{192,160},{224... | collective-permute-start | bytes 405512 | tf_op jit(solution)/shard_map/ppermute | solution.py:426
  60.4 2.6 %own.1.own_hbm = f32[32,96,128]{2,1,0:T(8,128)} custom-call(s32[1]{0:T(128)} %bitcast.plane, s32[1,8]{1,0:T(1,128)S(1)} %copy-done.3, f32[520,128]{1,0:T(8,128)S(1)} %get-tuple-element.26.top_ref, f32[264,128]{1,0:T(8,128)S(1)} %get-tuple-element.27.bottom_ref), custom_call_target="tpu_custom_call" | custom-call | tf_op jit(solution)/shard_map/own/pallas_call | solution.py:429
  62.9 0.1 collective-permute-done.2.got_top
  63.0 0.9 collective-permute-done.3.got_bottom
  63.9 1.7 %merge.1 = f32[32,96,128]{2,1,0:T(8,128)} custom-call(s32[1]{0:T(128)} %bitcast.plane, s32[1,8]{1,0:T(1,128)S(1)} %copy-done.3, f32[520,128]{1,0:T(8,128)S(1)} %get-tuple-element.26.top_ref, f32[264,128]{1,0:T(8,128)S(1)} %get-tuple-element.27.bottom_ref, f32[520,128]{1,0:T(8,128)S(1)} %collective-permute-done.2.got_top, ...), custom_call_target="tpu_custom_call", output_to_operand_aliasing={{}: (6, {})} | custom-call | tf_op jit(solution)/shard_map/merge/pallas_call | solution.py:444
  65.6 0.0 reduce-scatter.2.cloned.1.call-update
  65.7 1.6 %broadcast_in_dim.2 = bf16[16,32,2048]{2,1,0:T(8,128)(2,1)} broadcast(bf16[32,2048]{1,0:T(8,128)(2,1)S(1)} %get-tuple-element.32), dimensions={1,2} | broadcast | bytes 2228224 | tf_op jit(solution)/shard_map/broadcast_in_dim | solution.py:464
  67.3 5.1 %all-to-all-start.2 = ((bf16[16,32,2048]{2,1,0:T(8,128)(2,1)}), bf16[16,32,2048]{2,1,0:T(8,128)(2,1)S(1)}, u32[]{:S(2)}, u32[]{:S(2)}) async-start(bf16[16,32,2048]{2,1,0:T(8,128)(2,1)} %broadcast_in_dim.2), calls=%async_computation.3 | async-start | bytes 4194304 | tf_op jit(solution)/shard_map/all_to_all | solution.py:462
  72.4 0.0 copy-done
  72.4 1.9 %collective-permute-start.4 = (bf16[448,1024]{1,0:T(8,128)(2,1)S(1)}, bf16[448,1024]{1,0:T(8,128)(2,1)S(1)}, u32[]{:S(2)}, u32[]{:S(2)}) collective-permute-start(bf16[448,1024]{1,0:T(8,128)(2,1)S(1)} %get-tuple-element.33.near_ref), channel_id=1, source_target_pairs={{0,1},{1,0},{2,3},{3,2},{4,5},{5,4},{6,7},{7,6},{8,9},{9,8},{10,11... | collective-permute-start | bytes 2752520 | tf_op jit(solution)/shard_map/ppermute | solution.py:443
  74.3 2.4 %collective-permute-done.4.far_ref = bf16[448,1024]{1,0:T(8,128)(2,1)S(1)} collective-permute-done((bf16[448,1024]{1,0:T(8,128)(2,1)S(1)}, bf16[448,1024]{1,0:T(8,128)(2,1)S(1)}, u32[]{:S(2)}, u32[]{:S(2)}) %collective-permute-start.4) | collective-permute-done | bytes 917536 | tf_op jit(solution)/shard_map/ppermute | solution.py:443
  76.7 0.0 copy-start.1
  76.7 1.2 copy-done.1
  77.9 0.3 weights.1
  78.3 0.0 copy-start.2
  78.3 0.9 copy-done.2
  79.2 21.8 %all-to-all-done.2.kv_ref = bf16[16,32,2048]{2,1,0:T(8,128)(2,1)S(1)} async-done(((bf16[16,32,2048]{2,1,0:T(8,128)(2,1)}), bf16[16,32,2048]{2,1,0:T(8,128)(2,1)S(1)}, u32[]{:S(2)}, u32[]{:S(2)}) %all-to-all-start.2) | async-done | bytes 2097184 | tf_op jit(solution)/shard_map/all_to_all | solution.py:462
  100.9 2.0 %base.1 = bf16[16,32,320]{2,1,0:T(8,128)(2,1)S(1)} custom-call(bf16[16,32,2048]{2,1,0:T(8,128)(2,1)S(1)} %all-to-all-done.2.kv_ref, bf16[320,2048]{1,0:T(8,128)(2,1)S(1)} %get-tuple-element.34.w_ref, bf16[8,128,320]{2,1,0:T(8,128)(2,1)} %copy-done.2, bf16[16,32,128]{2,1,0:T(8,128)(2,1)S(1)} %get-tuple-element.36.low_ref), custom_call_target="tpu_custom_call" | custom-call | tf_op jit(solution)/shard_map/base/pallas_call | solution.py:476
  103.0 12.2 %all_to_all.22 = bf16[16,32,320]{2,1,0:T(8,128)(2,1)S(1)} all-to-all(bf16[16,32,320]{2,1,0:T(8,128)(2,1)S(1)} %base.1), channel_id=1, replica_groups=mesh['zh'=8,'zl'=2,'y'=4,'x'=4,'core'=2] {'y','x'}, dimensions={0} | all-to-all | bytes 655360 | tf_op jit(solution)/shard_map/all_to_all | solution.py:462
  115.2 0.1 copy.17
  115.3 1.0 reshape.22
  116.4 11.6 %reduce-scatter.2.cloned.1.call-done.sum_hbm = f32[4,96,128]{2,1,0:T(8,128)} async-done(((f32[32,96,128]{2,1,0:T(8,128)}), f32[4,96,128]{2,1,0:T(8,128)}) %reduce-scatter.2.cloned.1.call-update) | async-done | bytes 196624 | tf_op jit(solution)/shard_map/reduce_scatter | solution.py:459
  127.9 1.7 %finish.1 = (f32[4,32,160]{2,1,0:T(8,128)}, f32[4,32,160]{2,1,0:T(8,128)}, f32[4,32,32]{2,1,0:T(8,128)}, f32[4,32,32]{2,1,0:T(8,128)}) custom-call(f32[4,96,128]{2,1,0:T(8,128)} %reduce-scatter.2.cloned.1.call-done.sum_hbm), custom_call_target="tpu_custom_call" | custom-call | tf_op jit(solution)/shard_map/finish/pallas_call | solution.py:490
Async XLA Ops:
  7.2 120.8 %reduce-scatter.2.cloned.1.call-start = ((), (), s32[]{:S(2)}) async-start(), calls=%async_computation.5 | async-start | bytes 1769472 | tf_op jit(solution)/shard_map/reduce_scatter | solution.py:459
  10.0 62.4 %copy-start = (bf16[448,1024]{1,0:T(8,128)(2,1)}, bf16[448,1024]{1,0:T(8,128)(2,1)S(1)}, u32[]{:S(2)}) copy-start(bf16[448,1024]{1,0:T(8,128)(2,1)S(1)} %get-tuple-element.33.near_ref) | copy-start | bytes 2752516
  31.0 4.4 %collective-permute-start = (bf16[16,224,128]{2,1,0:T(8,128)(2,1)S(1)}, bf16[16,224,128]{2,1,0:T(8,128)(2,1)S(1)}, u32[]{:S(2)}, u32[]{:S(2)}) collective-permute-start(bf16[16,224,128]{2,1,0:T(8,128)(2,1)S(1)} %all_to_all.20.recv_ref), channel_id=1, source_target_pairs={{0,1},{1,0},{2,3},{3,2},{4,5},{5,4},{6,7},{7,6},{8,9},{9,8},{10,11... | collective-permute-start | bytes 2752520 | tf_op jit(solution)/shard_map/ppermute | solution.py:381
  33.3 18.5 %copy-start.3 = (s32[1,8]{1,0:T(1,128)S(1)}, s32[1,8]{1,0:T(1,128)}, u32[]{:S(2)}) copy-start(s32[1,8]{1,0:T(1,128)} %tenants.5) | copy-start | bytes 100
  48.4 3.4 %collective-permute-start.1 = (f32[16,32,128]{2,1,0:T(8,128)S(1)}, f32[16,32,128]{2,1,0:T(8,128)S(1)}, u32[]{:S(2)}, u32[]{:S(2)}) collective-permute-start(f32[16,32,128]{2,1,0:T(8,128)S(1)} %all_to_all.21.vec_ref), channel_id=1, source_target_pairs={{0,1},{1,0},{2,3},{3,2},{4,5},{5,4},{6,7},{7,6},{8,9},{9,8},{10,11... | collective-permute-start | bytes 786440 | tf_op jit(solution)/shard_map/ppermute | solution.py:399
  52.7 10.3 %collective-permute-start.2 = (f32[520,128]{1,0:T(8,128)S(1)}, f32[520,128]{1,0:T(8,128)S(1)}, u32[]{:S(2)}, u32[]{:S(2)}) collective-permute-start(f32[520,128]{1,0:T(8,128)S(1)} %get-tuple-element.26.top_ref), channel_id=1, source_target_pairs={{0,32},{32,0},{64,96},{96,64},{128,160},{160,128},{192,224},{224,1... | collective-permute-start | bytes 798728 | tf_op jit(solution)/shard_map/ppermute | solution.py:425
  54.7 9.3 %collective-permute-start.3 = (f32[264,128]{1,0:T(8,128)S(1)}, f32[264,128]{1,0:T(8,128)S(1)}, u32[]{:S(2)}, u32[]{:S(2)}) collective-permute-start(f32[264,128]{1,0:T(8,128)S(1)} %get-tuple-element.27.bottom_ref), channel_id=1, source_target_pairs={{0,480},{32,64},{64,32},{96,128},{128,96},{160,192},{192,160},{224... | collective-permute-start | bytes 405512 | tf_op jit(solution)/shard_map/ppermute | solution.py:426
  67.3 33.7 %all-to-all-start.2 = ((bf16[16,32,2048]{2,1,0:T(8,128)(2,1)}), bf16[16,32,2048]{2,1,0:T(8,128)(2,1)S(1)}, u32[]{:S(2)}, u32[]{:S(2)}) async-start(bf16[16,32,2048]{2,1,0:T(8,128)(2,1)} %broadcast_in_dim.2), calls=%async_computation.3 | async-start | bytes 4194304 | tf_op jit(solution)/shard_map/all_to_all | solution.py:462
  72.4 4.4 %collective-permute-start.4 = (bf16[448,1024]{1,0:T(8,128)(2,1)S(1)}, bf16[448,1024]{1,0:T(8,128)(2,1)S(1)}, u32[]{:S(2)}, u32[]{:S(2)}) collective-permute-start(bf16[448,1024]{1,0:T(8,128)(2,1)S(1)} %get-tuple-element.33.near_ref), channel_id=1, source_target_pairs={{0,1},{1,0},{2,3},{3,2},{4,5},{5,4},{6,7},{7,6},{8,9},{9,8},{10,11... | collective-permute-start | bytes 2752520 | tf_op jit(solution)/shard_map/ppermute | solution.py:443
  76.7 1.2 copy-start.1
  78.3 0.9 copy-start.2
Sparse Core Ops, SparseCore 0:
  65.8 62.0 reduce-scatter.1
